TPU v7x, 512 devices: a whole 4x4x16 slice. The times are simulated.
512 devices in a mesh: dp: 16 (over z_lo, core), expert: 32 (over y, x, z_hi).
Axes of the slice: x: 4, y: 4, z: 16 (z_hi: 2, z_lo: 8; z = z_hi * 8 + z_lo), core: 2. Of those that a mesh axis runs over, the one named last changes fastest.
Arguments:
- tokens: bfloat16 [4096, 4096], P('expert', 'dp'), may hold values from -6 to 6
- routes: int32 [4096, 2], P('expert'), may hold values from 0 to 31, as said below
- route_weights: float32 [4096, 2], P('expert'), may hold values from 0.05 to 0.5
- cotangent: bfloat16 [4096, 4096], P('expert', 'dp'), may hold values from -6 to 6
- w_gate_up: bfloat16 [32, 4096, 2048], P('expert', 'dp'), may hold values from -0.09375 to 0.09375
- w_down: bfloat16 [32, 1024, 4096], P('expert', None, 'dp'), may hold values from -0.1875 to 0.1875
Outputs:
- mixed: bfloat16 [4096, 4096], P('expert', 'dp')
- token_grad: bfloat16 [4096, 4096], P('expert', 'dp')
- grad_gate_up: bfloat16 [32, 4096, 2048], P('expert', 'dp')
- grad_down: bfloat16 [32, 1024, 4096], P('expert', None, 'dp')
Inputs may be any that keep to these rules, and one draw needn't show every extreme that they name: Each row names 2 different experts. One expert, the same for all rows, is named by exactly 16 routes in each aligned block of 128 rows (the rows of one device); in each such block every other expert is named by at most 8 routes, their counts differ by at most one, and some reach 8.
All inputs are finite; a program needn't handle non-finite values.
Results may differ from a plain program's by a relative error of at most 0.035.
Values may be sent and summed in bfloat16 or wider, within the bound.
No kernel may reach another device: no remote copies, remote signals or barrier semaphores. Data moves between devices by JAX's collectives and lax.ppermute only.
A program may use at most 64 MiB of HBM per device.

v0:
```python
import jax
import jax.numpy as jnp
from jax import lax
from jax.sharding import PartitionSpec as P


def pick_rows(selector, values):
    return jnp.dot(selector, values, preferred_element_type=jnp.float32)


def scaled_rows(selector, matched, flat_weights, values):
    slot_weight = jnp.sum(jnp.where(matched, flat_weights[None, :], 0.0), axis=1)
    return (pick_rows(selector, values) * slot_weight[:, None]).astype(jnp.bfloat16)


def on_device(tokens, routes, route_weights, cotangent, w_gate_up, w_down):
    experts = lax.axis_size("expert")
    tok_rows, feat = tokens.shape
    top = routes.shape[1]
    width = w_down.shape[1]
    busy_slots = 2 * tok_rows * top // experts
    flat_experts = routes.reshape(-1)
    flat_weights = route_weights.reshape(-1)
    expert_ids = jnp.arange(experts, dtype=jnp.int32)
    matches = (flat_experts[:, None] == expert_ids[None, :]).astype(jnp.int32)
    hot = jnp.int32(-1)
    hot_mask = flat_experts == hot
    cold_matches = matches * (1 - hot_mask.astype(jnp.int32))[:, None]
    rank = jnp.cumsum(cold_matches, axis=0) - cold_matches
    slot_of = jnp.sum(rank * cold_matches, axis=1)
    target = jnp.where(hot_mask, -1, flat_experts * busy_slots + slot_of)
    matched = jnp.arange(experts * busy_slots, dtype=jnp.int32)[:, None] == target[None, :]
    selector = matched.astype(jnp.bfloat16)
    tok_routes = jnp.repeat(tokens, top, axis=0)
    cot_routes = jnp.repeat(cotangent, top, axis=0)
    send_x = pick_rows(selector, tok_routes).astype(jnp.bfloat16).reshape(experts, busy_slots, feat)
    send_g = scaled_rows(selector, matched, flat_weights, cot_routes).reshape(
        experts, busy_slots, feat
    )
    recv_x, recv_g = (
        lax.all_to_all(send_x, "expert", split_axis=0, concat_axis=0, tiled=True),
        lax.all_to_all(send_g, "expert", split_axis=0, concat_axis=0, tiled=True),
    )
    own_gu = w_gate_up[0]
    own_down = w_down[0]
    groups = [(recv_x.reshape(-1, feat), recv_g.reshape(-1, feat), own_gu, own_down)]
    start = 0
    group = groups[0]
    bounds = [(start, start + group[0].shape[0])]
    partial_value = jnp.concatenate(
        [jnp.dot(g[0], g[2], preferred_element_type=jnp.float32) for g in groups], axis=0
    )
    sums = lax.psum(partial_value.astype(jnp.bfloat16), "dp").astype(jnp.float32)
    gate = sums[:, :width]
    up = sums[:, width:]
    sig = jax.nn.sigmoid(gate)
    silu_vals = gate * sig
    hidden = (silu_vals * up).astype(jnp.bfloat16)
    outputs = [
        jnp.dot(hidden, g[3], preferred_element_type=jnp.float32).astype(jnp.bfloat16)
        for g, (a, b) in zip(groups, bounds)
    ]
    cold_out = outputs[0].reshape(experts, busy_slots, feat)
    back_out = lax.all_to_all(cold_out, "expert", split_axis=0, concat_axis=0, tiled=True)
    grad_part = jnp.concatenate(
        [jnp.dot(g[1], g[3].T, preferred_element_type=jnp.float32) for g in groups], axis=0
    )
    hidden_grad = lax.psum(grad_part.astype(jnp.bfloat16), "dp").astype(jnp.float32)
    dgate = hidden_grad * up * sig * (1.0 + gate * (1.0 - sig))
    dup = hidden_grad * silu_vals
    gate_up_grad = jnp.concatenate([dgate, dup], axis=1).astype(jnp.bfloat16)
    route_grads = [
        jnp.dot(gate_up_grad, g[2].T, preferred_element_type=jnp.float32).astype(jnp.bfloat16)
        for g, (a, b) in zip(groups, bounds)
    ]
    cold_dx = route_grads[0].reshape(experts, busy_slots, feat)
    back_dx = lax.all_to_all(cold_dx, "expert", split_axis=0, concat_axis=0, tiled=True)
    out_routes = jnp.dot(selector.T, back_out.reshape(-1, feat), preferred_element_type=jnp.float32)
    dx_routes = jnp.dot(selector.T, back_dx.reshape(-1, feat), preferred_element_type=jnp.float32)
    grad_gu = jnp.dot(groups[0][0].T, gate_up_grad, preferred_element_type=jnp.float32)
    grad_dn = jnp.dot(hidden.T, groups[0][1], preferred_element_type=jnp.float32)
    grad_gu = grad_gu.astype(jnp.bfloat16)
    grad_dn = grad_dn.astype(jnp.bfloat16)
    weighted_out = out_routes * flat_weights[:, None]
    mixed = jnp.sum(weighted_out.reshape(tok_rows, top, feat), axis=1).astype(jnp.bfloat16)
    token_grad = jnp.sum(dx_routes.reshape(tok_rows, top, feat), axis=1).astype(jnp.bfloat16)
    return (mixed, token_grad, grad_gu[None], grad_dn[None])


def solution(mesh):
    return jax.shard_map(
        on_device,
        mesh=mesh,
        in_specs=(
            P("expert", "dp"),
            P("expert", None),
            P("expert", None),
            P("expert", "dp"),
            P("expert", "dp", None),
            P("expert", None, "dp"),
        ),
        out_specs=(
            P("expert", "dp"),
            P("expert", "dp"),
            P("expert", "dp", None),
            P("expert", None, "dp"),
        ),
        check_vma=False,
    )
```

profile of v0, /device:TPU:6, one launch (start us, length us, event | category | flops | bytes accessed | tf_op | source)
XLA Modules:
  0.0 356.3 jit_solution(10380677813770472840)
XLA Ops:
  7.2 0.0 copy-start
  7.2 0.0 copy-start.4
  7.2 0.9 copy.15
  8.1 0.1 eq.73
  8.2 0.1 reshape.117
  8.4 0.6 reduce-window.6
  9.0 0.2 slice_reduce_fusion
  9.2 0.1 fusion.18
  9.3 0.8 copy.18
  10.1 0.1 mul.73
  10.3 0.9 broadcast_in_dim.32
  11.2 0.1 reshape.125
  11.2 0.1 select_reduce_fusion
  11.4 1.0 fusion.8
  12.3 20.8 %all-to-all-start.2 = ((bf16[32,16,256]{2,1,0:T(8,128)(2,1)}), bf16[32,16,256]{2,1,0:T(8,128)(2,1)S(1)}, u32[]{:S(2)}, u32[]{:S(2)}) async-start(bf16[32,16,256]{2,1,0:T(8,128)(2,1)} %bitcast.7), calls=%async_computation.2 | async-start | bytes 524288 | tf_op jit(solution)/shard_map/all_to_all | solution.py:42
  33.2 0.9 broadcast_in_dim.31
  34.1 0.1 reshape.119
  34.1 0.9 convolution_convert_fusion.5
  35.1 14.3 %all-to-all-done.2 = bf16[32,16,256]{2,1,0:T(8,128)(2,1)S(1)} async-done(((bf16[32,16,256]{2,1,0:T(8,128)(2,1)}), bf16[32,16,256]{2,1,0:T(8,128)(2,1)S(1)}, u32[]{:S(2)}, u32[]{:S(2)}) %all-to-all-start.2) | async-done | bytes 262176 | tf_op jit(solution)/shard_map/all_to_all | solution.py:42
  49.4 6.3 %all-to-all-start = ((bf16[32,16,256]{2,1,0:T(8,128)(2,1)}), bf16[32,16,256]{2,1,0:T(8,128)(2,1)S(1)}, u32[]{:S(2)}, u32[]{:S(2)}) async-start(bf16[32,16,256]{2,1,0:T(8,128)(2,1)} %bitcast.1), calls=%async_computation | async-start | bytes 524288 | tf_op jit(solution)/shard_map/all_to_all | solution.py:41
  55.6 0.0 all-reduce.3.cloned.1.call-start
  55.7 0.0 copy-done.4
  55.7 1.4 convolution_convert_fusion.2
  57.1 14.3 %all-to-all-done = bf16[32,16,256]{2,1,0:T(8,128)(2,1)S(1)} async-done(((bf16[32,16,256]{2,1,0:T(8,128)(2,1)}), bf16[32,16,256]{2,1,0:T(8,128)(2,1)S(1)}, u32[]{:S(2)}, u32[]{:S(2)}) %all-to-all-start) | async-done | bytes 262176 | tf_op jit(solution)/shard_map/all_to_all | solution.py:41
  71.5 0.0 copy-done
  71.5 2.0 convolution_convert_fusion
  73.5 0.0 all-reduce.3.cloned.1.call-update
  73.5 213.8 %all-reduce.3.cloned.1.call-done = (bf16[512,2048]{1,0:T(8,128)(2,1)}, bf16[512,1024]{1,0:T(8,128)(2,1)}) async-done(((bf16[512,2048]{1,0:T(8,128)(2,1)}, bf16[512,1024]{1,0:T(8,128)(2,1)}), (bf16[512,2048]{1,0:T(8,128)(2,1)}, bf16[512,1024]{1,0:T(8,128)(2,1)})) %all-reduce.3.cloned.1.call-update) | async-done | bytes 3145744 | tf_op jit(solution)/shard_map/psum | solution.py:53
  287.3 2.2 convert_element_type.56
  289.5 0.0 copy-done.3
  289.6 2.4 fusion.3
  292.0 1.0 copy-done.2
  293.0 1.1 convolution_convert_fusion.4
  294.1 15.7 %all-to-all-start.1 = ((bf16[32,16,256]{2,1,0:T(8,128)(2,1)}), bf16[32,16,256]{2,1,0:T(8,128)(2,1)S(1)}, u32[]{:S(2)}, u32[]{:S(2)}) async-start(bf16[32,16,256]{2,1,0:T(8,128)(2,1)} %bitcast.5), calls=%async_computation.1 | async-start | bytes 524288 | tf_op jit(solution)/shard_map/all_to_all | solution.py:64
  309.8 2.7 fusion.9
  312.5 13.1 %all-to-all-done.1 = bf16[32,16,256]{2,1,0:T(8,128)(2,1)S(1)} async-done(((bf16[32,16,256]{2,1,0:T(8,128)(2,1)}), bf16[32,16,256]{2,1,0:T(8,128)(2,1)S(1)}, u32[]{:S(2)}, u32[]{:S(2)}) %all-to-all-start.1) | async-done | bytes 262176 | tf_op jit(solution)/shard_map/all_to_all | solution.py:64
  325.6 6.2 %all-to-all-start.3 = ((bf16[32,16,256]{2,1,0:T(8,128)(2,1)}), bf16[32,16,256]{2,1,0:T(8,128)(2,1)S(1)}, u32[]{:S(2)}, u32[]{:S(2)}) async-start(bf16[32,16,256]{2,1,0:T(8,128)(2,1)} %bitcast.9), calls=%async_computation.3 | async-start | bytes 524288 | tf_op jit(solution)/shard_map/all_to_all | solution.py:77
  331.9 0.1 iota_compare_fusion
  332.0 0.2 eq.87
  332.2 0.0 copy-start.1
  332.2 2.6 fusion.7
  334.8 0.0 copy-done.1
  334.8 1.7 fusion
  336.5 0.3 convolution_multiply_fusion.1
  336.8 0.1 reshape.124
  337.0 10.6 %all-to-all-done.3 = bf16[32,16,256]{2,1,0:T(8,128)(2,1)S(1)} async-done(((bf16[32,16,256]{2,1,0:T(8,128)(2,1)}), bf16[32,16,256]{2,1,0:T(8,128)(2,1)S(1)}, u32[]{:S(2)}, u32[]{:S(2)}) %all-to-all-start.3) | async-done | bytes 262176 | tf_op jit(solution)/shard_map/all_to_all | solution.py:77
  347.6 0.9 convolution_reduce_fusion
  348.5 0.9 reduce_sum.37
  (8 shorter events, 0.1 us)
Async XLA Ops:
  7.2 64.3 %copy-start = (bf16[1,256,2048]{2,1,0:T(8,128)(2,1)S(1)}, bf16[1,256,2048]{2,1,0:T(8,128)(2,1)}, u32[]{:S(2)}) copy-start(bf16[1,256,2048]{2,1,0:T(8,128)(2,1)} %param.10) | copy-start | bytes 3145732
  7.2 48.5 %copy-start.4 = (bf16[1,1024,256]{2,1,0:T(8,128)(2,1)S(1)}, bf16[1,1024,256]{2,1,0:T(8,128)(2,1)}, u32[]{:S(2)}) copy-start(bf16[1,1024,256]{2,1,0:T(8,128)(2,1)} %param.11) | copy-start | bytes 1572868
  12.3 37.0 %all-to-all-start.2 = ((bf16[32,16,256]{2,1,0:T(8,128)(2,1)}), bf16[32,16,256]{2,1,0:T(8,128)(2,1)S(1)}, u32[]{:S(2)}, u32[]{:S(2)}) async-start(bf16[32,16,256]{2,1,0:T(8,128)(2,1)} %bitcast.7), calls=%async_computation.2 | async-start | bytes 524288 | tf_op jit(solution)/shard_map/all_to_all | solution.py:42
  49.4 22.1 %all-to-all-start = ((bf16[32,16,256]{2,1,0:T(8,128)(2,1)}), bf16[32,16,256]{2,1,0:T(8,128)(2,1)S(1)}, u32[]{:S(2)}, u32[]{:S(2)}) async-start(bf16[32,16,256]{2,1,0:T(8,128)(2,1)} %bitcast.1), calls=%async_computation | async-start | bytes 524288 | tf_op jit(solution)/shard_map/all_to_all | solution.py:41
  55.6 231.7 %all-reduce.3.cloned.1.call-start = ((), (), s32[]{:S(2)}) async-start(), calls=%async_computation.4 | async-start | bytes 6291456 | tf_op jit(solution)/shard_map/psum | solution.py:53
  287.3 2.2 copy-start.3
  292.0 1.0 copy-start.2
  294.1 31.5 %all-to-all-start.1 = ((bf16[32,16,256]{2,1,0:T(8,128)(2,1)}), bf16[32,16,256]{2,1,0:T(8,128)(2,1)S(1)}, u32[]{:S(2)}, u32[]{:S(2)}) async-start(bf16[32,16,256]{2,1,0:T(8,128)(2,1)} %bitcast.5), calls=%async_computation.1 | async-start | bytes 524288 | tf_op jit(solution)/shard_map/all_to_all | solution.py:64
  325.6 22.0 %all-to-all-start.3 = ((bf16[32,16,256]{2,1,0:T(8,128)(2,1)}), bf16[32,16,256]{2,1,0:T(8,128)(2,1)S(1)}, u32[]{:S(2)}, u32[]{:S(2)}) async-start(bf16[32,16,256]{2,1,0:T(8,128)(2,1)} %bitcast.9), calls=%async_computation.3 | async-start | bytes 524288 | tf_op jit(solution)/shard_map/all_to_all | solution.py:77
  332.2 2.6 copy-start.1
Sparse Core Ops, SparseCore 0:
  73.6 213.6 all-reduce.2
where the time goes:
time: 358 us; the launch traced here: 356 us
  waiting for transfers between devices  266 us (74%)
  starting transfers between devices  49 us (14%)
  matrix products  14.7 us (4%)
  between operations  14.2 us (4%)
  other arithmetic  6.6 us (2%)
  local copies, waits for them, and re-layouts  5.55 us (2%)
    psum x1, waiting for transfers between devices, on_device(): lax.psum(partial_value.astype(jnp.bfloat16), 'dp').astype(jnp.float32)  214 us
    all_to_all x1, starting transfers between devices, on_device(): lax.all_to_all(send_g, 'expert', split_axis=0, concat_axis=0, tiled=True)  20.8 us
    all_to_all x1, starting transfers between devices, on_device(): lax.all_to_all(cold_out, 'expert', split_axis=0, concat_axis=0, tiled=True)  15.7 us
    all_to_all x1, waiting for transfers between devices, on_device(): lax.all_to_all(send_x, 'expert', split_axis=0, concat_axis=0, tiled=True)  14.3 us
    all_to_all x1, waiting for transfers between devices, on_device(): lax.all_to_all(send_g, 'expert', split_axis=0, concat_axis=0, tiled=True)  14.3 us
    all_to_all x1, waiting for transfers between devices, on_device(): lax.all_to_all(cold_out, 'expert', split_axis=0, concat_axis=0, tiled=True)  13.1 us
    all_to_all x1, waiting for transfers between devices, on_device(): lax.all_to_all(cold_dx, 'expert', split_axis=0, concat_axis=0, tiled=True)  10.6 us
  transfers between devices with their start and end apart: 5, of which 5 were waited for; matrix products, arithmetic and copies ran while one was open for 3% of the time, Pallas kernels for 0%

commit v1 on v0

v1 whole, which is shorter than its diff:
```python
import jax
import jax.numpy as jnp
from jax import lax
from jax.sharding import PartitionSpec as P

BF = jnp.bfloat16
F32 = jnp.float32


def mm(a, b):
    return jnp.dot(a, b, preferred_element_type=F32)


def mm_nt(a, b):
    return lax.dot_general(a, b, (((1,), (1,)), ((), ())), preferred_element_type=F32)


def mm_tn(a, b):
    return lax.dot_general(a, b, (((0,), (0,)), ((), ())), preferred_element_type=F32)


def roll_rows(rows, shift):
    twice = jnp.concatenate([rows, rows], axis=0)
    return lax.dynamic_slice_in_dim(twice, shift, rows.shape[0], axis=0)


def route_slots(routes_t, experts, slots):
    top, count = routes_t.shape
    ids = lax.broadcasted_iota(jnp.int32, (experts, count), 0)
    earlier = lax.broadcasted_iota(jnp.int32, (count, count), 0) < lax.broadcasted_iota(
        jnp.int32, (count, count), 1
    )
    earlier = earlier.astype(BF)
    before = jnp.zeros((experts, 1), F32)
    targets = []
    for k in range(top):
        named = ids == routes_t[k : k + 1]
        hot = named.astype(BF)
        rank = mm(hot, earlier) + before
        slot = jnp.sum(jnp.where(named, rank, 0.0), axis=0, keepdims=True)
        targets.append(routes_t[k : k + 1] * slots + slot.astype(jnp.int32))
        before = before + jnp.sum(hot.astype(F32), axis=1, keepdims=True)
    return targets


def on_device(tokens, routes, route_weights, cotangent, w_gate_up, w_down):
    experts = lax.axis_size("expert")
    n_dp = lax.axis_size("dp")
    chips = n_dp // 2
    tok_rows, feat = tokens.shape
    top = routes.shape[1]
    width = w_down.shape[1]
    slots = 2 * tok_rows * top // experts
    rows = experts * slots
    half = rows // 2
    step = half // chips
    me = lax.axis_index("dp")
    chip = me // 2
    core = me % 2
    gu = w_gate_up[0]
    down = w_down[0]

    targets = route_slots(routes.T, experts, slots)
    weights = route_weights.T
    slot_ids = lax.broadcasted_iota(jnp.int32, (rows, tok_rows), 0)
    picked = [slot_ids == target for target in targets]
    selector = sum(p.astype(BF) for p in picked)
    slot_weight = sum(
        jnp.sum(jnp.where(p, weights[k : k + 1], 0.0), axis=1, keepdims=True)
        for k, p in enumerate(picked)
    )
    send_x = mm(selector, tokens).astype(BF)
    send_g = (mm(selector, cotangent) * slot_weight).astype(BF)
    send = jnp.concatenate([send_x, send_g], axis=1).reshape(experts, slots, 2 * feat)
    recv = lax.all_to_all(send, "expert", split_axis=0, concat_axis=0, tiled=True)

    both = recv.reshape(2, half, 2 * feat)
    mine = roll_rows(lax.dynamic_index_in_dim(both, core, 0, keepdims=False), chip * step)
    theirs = roll_rows(lax.dynamic_index_in_dim(both, 1 - core, 0, keepdims=False), chip * step)

    def terms(xg):
        return jnp.concatenate(
            [mm(xg[:, :feat], gu).astype(BF), mm_nt(xg[:, feat:], down).astype(BF)], axis=1
        )

    pair = [(i, i ^ 1) for i in range(n_dp)]
    right = [(i, i + 2) for i in range(n_dp - 2)]
    left = [(i + 2, i) for i in range(n_dp - 2)]
    from_pair = lax.ppermute(terms(theirs), "dp", pair)
    part = (terms(mine).astype(F32) + from_pair.astype(F32)).astype(BF).reshape(chips, step, -1)

    go_right, go_left = part[chips - 1], part[1]
    for s in range(chips - 1):
        got_r = lax.ppermute(go_right, "dp", right)
        got_l = lax.ppermute(go_left, "dp", left)
        if s < chips - 2:
            go_right = (got_r.astype(F32) + part[chips - 2 - s].astype(F32)).astype(BF)
            go_left = (got_l.astype(F32) + part[2 + s].astype(F32)).astype(BF)
    sums = got_r.astype(F32) + got_l.astype(F32) + part[0].astype(F32)

    gate = sums[:, :width]
    up = sums[:, width : 2 * width]
    hidden_grad = sums[:, 2 * width :]
    sig = jax.nn.sigmoid(gate)
    silu_vals = gate * sig
    own = jnp.concatenate(
        [
            (silu_vals * up).astype(BF),
            (hidden_grad * up * sig * (1.0 + gate * (1.0 - sig))).astype(BF),
            (hidden_grad * silu_vals).astype(BF),
        ],
        axis=1,
    )

    rights, lefts = [], []
    go_right = go_left = own
    for s in range(chips - 1):
        go_right = lax.ppermute(go_right, "dp", right)
        go_left = lax.ppermute(go_left, "dp", left)
        rights.append(go_right)
        lefts.append(go_left)
    pieces = [own]
    for m in range(1, chips):
        pieces.append(jnp.where(chip + m < chips, lefts[m - 1], rights[chips - 1 - m]))
    act_mine = jnp.concatenate(pieces, axis=0)
    act_theirs = lax.ppermute(act_mine, "dp", pair)

    def outputs(act):
        return jnp.concatenate(
            [
                mm(act[:, :width], down).astype(BF),
                mm_nt(act[:, width:], gu).astype(BF),
            ],
            axis=1,
        )

    back = [roll_rows(outputs(a), half - chip * step) for a in (act_mine, act_theirs)]
    first = jnp.where(core == 0, back[0], back[1])
    second = jnp.where(core == 0, back[1], back[0])
    back = jnp.concatenate([first, second], axis=0).reshape(experts, slots, 2 * feat)
    ret = lax.all_to_all(back, "expert", split_axis=0, concat_axis=0, tiled=True)
    ret = ret.reshape(rows, 2 * feat)

    act = jnp.concatenate([act_mine, act_theirs], axis=0)
    xg = jnp.concatenate([mine, theirs], axis=0)
    grad_gu = mm_tn(xg[:, :feat], act[:, width:]).astype(BF)
    grad_dn = mm_tn(act[:, :width], xg[:, feat:]).astype(BF)

    mixed = sum(
        mm_tn(p.astype(BF), ret[:, :feat]) * route_weights[:, k : k + 1]
        for k, p in enumerate(picked)
    ).astype(BF)
    token_grad = mm_tn(selector, ret[:, feat:]).astype(BF)
    return (mixed, token_grad, grad_gu[None], grad_dn[None])


def solution(mesh):
    return jax.shard_map(
        on_device,
        mesh=mesh,
        in_specs=(
            P("expert", "dp"),
            P("expert", None),
            P("expert", None),
            P("expert", "dp"),
            P("expert", "dp", None),
            P("expert", None, "dp"),
        ),
        out_specs=(
            P("expert", "dp"),
            P("expert", "dp"),
            P("expert", "dp", None),
            P("expert", None, "dp"),
        ),
        check_vma=False,
    )
```

time: 358 us -> 271 us (0.76)
  the two profiles are of different devices: /device:TPU:6 before, /device:TPU:97 now
where the time goes in v1:
time: 271 us; the launch traced here: 269 us
  starting transfers between devices  140 us (52%)
  waiting for transfers between devices  93 us (34%)
  matrix products  18.6 us (7%)
  other arithmetic  11.2 us (4%)
  local copies, waits for them, and re-layouts  5.15 us (2%)
    ppermute x7, starting transfers between devices, on_device(): go_right = lax.ppermute(go_right, 'dp', right)  35.5 us
    ppermute x7, starting transfers between devices, on_device(): got_r = lax.ppermute(go_right, 'dp', right)  32.7 us
    all_to_all x1, waiting for transfers between devices, on_device(): lax.all_to_all(send, 'expert', split_axis=0, concat_axis=0, tiled=True)  32.5 us
    all_to_all x1, waiting for transfers between devices, on_device(): lax.all_to_all(back, 'expert', split_axis=0, concat_axis=0, tiled=True)  25.8 us
    ppermute x1, starting transfers between devices, on_device(): act_theirs = lax.ppermute(act_mine, 'dp', pair)  18.4 us
    all_to_all x1, starting transfers between devices, on_device(): lax.all_to_all(send, 'expert', split_axis=0, concat_axis=0, tiled=True)  17.6 us
    ppermute x7, starting transfers between devices, on_device(): got_l = lax.ppermute(go_left, 'dp', left)  14.2 us
    ppermute x7, waiting for transfers between devices, on_device(): got_l = lax.ppermute(go_left, 'dp', left)  14.1 us
  transfers between devices with their start and end apart: 32, of which 28 were waited for; matrix products, arithmetic and copies ran while one was open for 6% of the time, Pallas kernels for 0%

profile of v1, /device:TPU:97, one launch (start us, length us, event | category | flops | bytes accessed | tf_op | source)
XLA Modules:
  0.0 269.4 jit_solution(10313134160779214634)
XLA Ops:
  6.9 17.6 %all-to-all-start = ((bf16[32,16,512]{2,1,0:T(8,128)(2,1)}), bf16[32,16,512]{2,1,0:T(8,128)(2,1)S(1)}, u32[]{:S(2)}, u32[]{:S(2)}) async-start(bf16[32,16,512]{2,1,0:T(8,128)(2,1)} %bitcast.10), calls=%async_computation | async-start | bytes 1048576 | tf_op jit(solution)/shard_map/all_to_all | solution.py:75
  24.5 32.5 %all-to-all-done = bf16[32,16,512]{2,1,0:T(8,128)(2,1)S(1)} async-done(((bf16[32,16,512]{2,1,0:T(8,128)(2,1)}), bf16[32,16,512]{2,1,0:T(8,128)(2,1)S(1)}, u32[]{:S(2)}, u32[]{:S(2)}) %all-to-all-start) | async-done | bytes 524320 | tf_op jit(solution)/shard_map/all_to_all | solution.py:75
  58.6 3.8 %collective-permute-start = (bf16[256,3072]{1,0:T(8,128)(2,1)S(1)}, bf16[256,3072]{1,0:T(8,128)(2,1)S(1)}, u32[]{:S(2)}, u32[]{:S(2)}) collective-permute-start(bf16[256,3072]{1,0:T(8,128)(2,1)S(1)} %pad_maximum_fusion), channel_id=1, source_target_pairs={{0,32},{32,0},{64,96},{96,64},{128,160},{160,128},{192,224},{224,1... | collective-permute-start | bytes 4718600 | tf_op jit(solution)/shard_map/ppermute | solution.py:89
  63.5 1.9 collective-permute-done
  66.0 2.6 collective-permute-start.1
  68.6 2.7 collective-permute-start.8
  71.3 2.7 %collective-permute-done.1 = bf16[32,3072]{1,0:T(8,128)(2,1)S(1)} collective-permute-done((bf16[32,3072]{1,0:T(8,128)(2,1)S(1)}, bf16[32,3072]{1,0:T(8,128)(2,1)S(1)}, u32[]{:S(2)}, u32[]{:S(2)}) %collective-permute-start.1) | collective-permute-done | bytes 196640 | tf_op jit(solution)/shard_map/ppermute | solution.py:94
  74.0 3.5 %collective-permute-done.8 = bf16[32,3072]{1,0:T(8,128)(2,1)S(1)} collective-permute-done((bf16[32,3072]{1,0:T(8,128)(2,1)S(1)}, bf16[32,3072]{1,0:T(8,128)(2,1)S(1)}, u32[]{:S(2)}, u32[]{:S(2)}) %collective-permute-start.8) | collective-permute-done | bytes 196640 | tf_op jit(solution)/shard_map/ppermute | solution.py:95
  77.6 5.4 %collective-permute-start.2 = (bf16[32,3072]{1,0:T(8,128)(2,1)S(1)}, bf16[32,3072]{1,0:T(8,128)(2,1)S(1)}, u32[]{:S(2)}, u32[]{:S(2)}) collective-permute-start(bf16[32,3072]{1,0:T(8,128)(2,1)S(1)} %get-tuple-element.17), channel_id=1, source_target_pairs={{0,64},{32,96},{64,128},{96,160},{128,192},{160,224},{192,256},{22... | collective-permute-start | bytes 589832 | tf_op jit(solution)/shard_map/ppermute | solution.py:94
  83.0 1.9 collective-permute-start.9
  86.0 5.0 %collective-permute-done.9 = bf16[32,3072]{1,0:T(8,128)(2,1)S(1)} collective-permute-done((bf16[32,3072]{1,0:T(8,128)(2,1)S(1)}, bf16[32,3072]{1,0:T(8,128)(2,1)S(1)}, u32[]{:S(2)}, u32[]{:S(2)}) %collective-permute-start.9) | collective-permute-done | bytes 196640 | tf_op jit(solution)/shard_map/ppermute | solution.py:95
  91.2 1.9 collective-permute-start.10
  93.1 4.6 %collective-permute-start.3 = (bf16[32,3072]{1,0:T(8,128)(2,1)S(1)}, bf16[32,3072]{1,0:T(8,128)(2,1)S(1)}, u32[]{:S(2)}, u32[]{:S(2)}) collective-permute-start(bf16[32,3072]{1,0:T(8,128)(2,1)S(1)} %get-tuple-element.15), channel_id=1, source_target_pairs={{0,64},{32,96},{64,128},{96,160},{128,192},{160,224},{192,256},{22... | collective-permute-start | bytes 589832 | tf_op jit(solution)/shard_map/ppermute | solution.py:94
  98.8 1.5 collective-permute-done.3
  100.3 1.9 collective-permute-start.11
  102.3 5.0 %collective-permute-start.4 = (bf16[32,3072]{1,0:T(8,128)(2,1)S(1)}, bf16[32,3072]{1,0:T(8,128)(2,1)S(1)}, u32[]{:S(2)}, u32[]{:S(2)}) collective-permute-start(bf16[32,3072]{1,0:T(8,128)(2,1)S(1)} %get-tuple-element.13), channel_id=1, source_target_pairs={{0,64},{32,96},{64,128},{96,160},{128,192},{160,224},{192,256},{22... | collective-permute-start | bytes 589832 | tf_op jit(solution)/shard_map/ppermute | solution.py:94
  108.4 1.5 collective-permute-done.4
  110.0 1.9 collective-permute-start.12
  111.9 5.0 %collective-permute-start.5 = (bf16[32,3072]{1,0:T(8,128)(2,1)S(1)}, bf16[32,3072]{1,0:T(8,128)(2,1)S(1)}, u32[]{:S(2)}, u32[]{:S(2)}) collective-permute-start(bf16[32,3072]{1,0:T(8,128)(2,1)S(1)} %get-tuple-element.11), channel_id=1, source_target_pairs={{0,64},{32,96},{64,128},{96,160},{128,192},{160,224},{192,256},{22... | collective-permute-start | bytes 589832 | tf_op jit(solution)/shard_map/ppermute | solution.py:94
  118.1 1.5 collective-permute-done.5
  119.7 1.9 collective-permute-start.13
  121.6 5.0 %collective-permute-start.6 = (bf16[32,3072]{1,0:T(8,128)(2,1)S(1)}, bf16[32,3072]{1,0:T(8,128)(2,1)S(1)}, u32[]{:S(2)}, u32[]{:S(2)}) collective-permute-start(bf16[32,3072]{1,0:T(8,128)(2,1)S(1)} %get-tuple-element.9), channel_id=1, source_target_pairs={{0,64},{32,96},{64,128},{96,160},{128,192},{160,224},{192,256},{22... | collective-permute-start | bytes 589832 | tf_op jit(solution)/shard_map/ppermute | solution.py:94
  127.7 1.5 collective-permute-done.6
  129.3 1.9 collective-permute-start.14
  131.2 5.0 %collective-permute-start.7 = (bf16[32,3072]{1,0:T(8,128)(2,1)S(1)}, bf16[32,3072]{1,0:T(8,128)(2,1)S(1)}, u32[]{:S(2)}, u32[]{:S(2)}) collective-permute-start(bf16[32,3072]{1,0:T(8,128)(2,1)S(1)} %get-tuple-element.7), channel_id=1, source_target_pairs={{0,64},{32,96},{64,128},{96,160},{128,192},{160,224},{192,256},{22... | collective-permute-start | bytes 589832 | tf_op jit(solution)/shard_map/ppermute | solution.py:94
  139.8 5.0 %collective-permute-start.16 = (bf16[32,3072]{1,0:T(8,128)(2,1)S(1)}, bf16[32,3072]{1,0:T(8,128)(2,1)S(1)}, u32[]{:S(2)}, u32[]{:S(2)}) collective-permute-start(bf16[32,3072]{1,0:T(8,128)(2,1)S(1)} %get-tuple-element.42), channel_id=1, source_target_pairs={{0,64},{32,96},{64,128},{96,160},{128,192},{160,224},{192,256},{22... | collective-permute-start | bytes 589832 | tf_op jit(solution)/shard_map/ppermute | solution.py:118
  144.9 1.9 collective-permute-start.15
  146.8 1.9 collective-permute-done.16
  148.7 5.0 %collective-permute-start.17 = (bf16[32,3072]{1,0:T(8,128)(2,1)S(1)}, bf16[32,3072]{1,0:T(8,128)(2,1)S(1)}, u32[]{:S(2)}, u32[]{:S(2)}) collective-permute-start(bf16[32,3072]{1,0:T(8,128)(2,1)S(1)} %collective-permute-done.16), channel_id=1, source_target_pairs={{0,64},{32,96},{64,128},{96,160},{128,192},{160,224},{192,256},{22... | collective-permute-start | bytes 589832 | tf_op jit(solution)/shard_map/ppermute | solution.py:118
  153.8 1.9 collective-permute-start.23
  157.1 5.3 %collective-permute-start.18 = (bf16[32,3072]{1,0:T(8,128)(2,1)S(1)}, bf16[32,3072]{1,0:T(8,128)(2,1)S(1)}, u32[]{:S(2)}, u32[]{:S(2)}) collective-permute-start(bf16[32,3072]{1,0:T(8,128)(2,1)S(1)} %collective-permute-done.17), channel_id=1, source_target_pairs={{0,64},{32,96},{64,128},{96,160},{128,192},{160,224},{192,256},{22... | collective-permute-start | bytes 589832 | tf_op jit(solution)/shard_map/ppermute | solution.py:118
  162.4 1.9 collective-permute-start.24
  165.0 5.0 %collective-permute-start.19 = (bf16[32,3072]{1,0:T(8,128)(2,1)S(1)}, bf16[32,3072]{1,0:T(8,128)(2,1)S(1)}, u32[]{:S(2)}, u32[]{:S(2)}) collective-permute-start(bf16[32,3072]{1,0:T(8,128)(2,1)S(1)} %collective-permute-done.18), channel_id=1, source_target_pairs={{0,64},{32,96},{64,128},{96,160},{128,192},{160,224},{192,256},{22... | collective-permute-start | bytes 589832 | tf_op jit(solution)/shard_map/ppermute | solution.py:118
  170.1 1.9 collective-permute-start.25
  172.6 5.0 %collective-permute-start.20 = (bf16[32,3072]{1,0:T(8,128)(2,1)S(1)}, bf16[32,3072]{1,0:T(8,128)(2,1)S(1)}, u32[]{:S(2)}, u32[]{:S(2)}) collective-permute-start(bf16[32,3072]{1,0:T(8,128)(2,1)S(1)} %collective-permute-done.19), channel_id=1, source_target_pairs={{0,64},{32,96},{64,128},{96,160},{128,192},{160,224},{192,256},{22... | collective-permute-start | bytes 589832 | tf_op jit(solution)/shard_map/ppermute | solution.py:118
  177.7 1.9 collective-permute-start.26
  180.2 5.0 %collective-permute-start.21 = (bf16[32,3072]{1,0:T(8,128)(2,1)S(1)}, bf16[32,3072]{1,0:T(8,128)(2,1)}, u32[]{:S(2)}, u32[]{:S(2)}) collective-permute-start(bf16[32,3072]{1,0:T(8,128)(2,1)S(1)} %collective-permute-done.20), channel_id=1, source_target_pairs={{0,64},{32,96},{64,128},{96,160},{128,192},{160,224},{192,256},{22... | collective-permute-start | bytes 589832 | tf_op jit(solution)/shard_map/ppermute | solution.py:118
  185.4 1.9 collective-permute-start.27
  187.9 5.1 %collective-permute-start.22 = (bf16[32,3072]{1,0:T(8,128)(2,1)}, bf16[32,3072]{1,0:T(8,128)(2,1)}, u32[]{:S(2)}, u32[]{:S(2)}) collective-permute-start(bf16[32,3072]{1,0:T(8,128)(2,1)} %collective-permute-done.21), channel_id=1, source_target_pairs={{0,64},{32,96},{64,128},{96,160},{128,192},{160,224},{192,256},{22... | collective-permute-start | bytes 589832 | tf_op jit(solution)/shard_map/ppermute | solution.py:118
  193.3 1.9 collective-permute-start.28
  202.0 18.4 %collective-permute-start.29 = (bf16[256,3072]{1,0:T(8,128)(2,1)}, bf16[256,3072]{1,0:T(8,128)(2,1)S(1)}, u32[]{:S(2)}, u32[]{:S(2)}) collective-permute-start(bf16[256,3072]{1,0:T(8,128)(2,1)} %get-tuple-element.24), channel_id=1, source_target_pairs={{0,32},{32,0},{64,96},{96,64},{128,160},{160,128},{192,224},{224,1... | collective-permute-start | bytes 4718600 | tf_op jit(solution)/shard_map/ppermute | solution.py:126
  221.8 1.7 convolution_convert_fusion.10
  226.9 4.6 %all-to-all-start.1 = ((bf16[32,16,512]{2,1,0:T(8,128)(2,1)}), bf16[32,16,512]{2,1,0:T(8,128)(2,1)}, u32[]{:S(2)}, u32[]{:S(2)}) async-start(bf16[32,16,512]{2,1,0:T(8,128)(2,1)} %bitcast.16), calls=%async_computation.1 | async-start | bytes 1048576 | tf_op jit(solution)/shard_map/all_to_all | solution.py:141
  232.9 2.5 fusion.2
  235.4 3.3 %fusion = bf16[1,256,2048]{2,1,0:T(8,128)(2,1)} fusion(bf16[512,3072]{1,0:T(8,128)(2,1)} %constant_dynamic-update-slice_fusion.1, bf16[256,512]{1,0:T(8,128)(2,1)S(1)} %copy-done.3, bf16[256,512]{1,0:T(8,128)(2,1)S(1)} %fusion.40), kind=kOutput, calls=%fused_computation.4 | convolution fusion | flops 537919488 | bytes 3670016 | tf_op jit(solution)/shard_map/dot_general | solution.py:19
  238.7 25.8 %all-to-all-done.1 = bf16[32,16,512]{2,1,0:T(8,128)(2,1)} async-done(((bf16[32,16,512]{2,1,0:T(8,128)(2,1)}), bf16[32,16,512]{2,1,0:T(8,128)(2,1)}, u32[]{:S(2)}, u32[]{:S(2)}) %all-to-all-start.1) | async-done | bytes 524320 | tf_op jit(solution)/shard_map/all_to_all | solution.py:141
  264.5 1.8 convolution_convert_fusion.11
  267.5 1.9 fusion.5
  (83 shorter events, 37.5 us)
Async XLA Ops:
  0.6 56.8 %copy-start = (bf16[1,256,2048]{2,1,0:T(8,128)(2,1)S(1)}, bf16[1,256,2048]{2,1,0:T(8,128)(2,1)}, u32[]{:S(2)}) copy-start(bf16[1,256,2048]{2,1,0:T(8,128)(2,1)} %param.10) | copy-start | bytes 3145732
  6.9 50.1 %all-to-all-start = ((bf16[32,16,512]{2,1,0:T(8,128)(2,1)}), bf16[32,16,512]{2,1,0:T(8,128)(2,1)S(1)}, u32[]{:S(2)}, u32[]{:S(2)}) async-start(bf16[32,16,512]{2,1,0:T(8,128)(2,1)} %bitcast.10), calls=%async_computation | async-start | bytes 1048576 | tf_op jit(solution)/shard_map/all_to_all | solution.py:75
  57.1 1.0 copy-start.1
  58.6 6.8 %collective-permute-start = (bf16[256,3072]{1,0:T(8,128)(2,1)S(1)}, bf16[256,3072]{1,0:T(8,128)(2,1)S(1)}, u32[]{:S(2)}, u32[]{:S(2)}) collective-permute-start(bf16[256,3072]{1,0:T(8,128)(2,1)S(1)} %pad_maximum_fusion), channel_id=1, source_target_pairs={{0,32},{32,0},{64,96},{96,64},{128,160},{160,128},{192,224},{224,1... | collective-permute-start | bytes 4718600 | tf_op jit(solution)/shard_map/ppermute | solution.py:89
  62.7 0.8 copy-start.2
  66.0 8.0 %collective-permute-start.1 = (bf16[32,3072]{1,0:T(8,128)(2,1)S(1)}, bf16[32,3072]{1,0:T(8,128)(2,1)S(1)}, u32[]{:S(2)}, u32[]{:S(2)}) collective-permute-start(bf16[32,3072]{1,0:T(8,128)(2,1)S(1)} %get-tuple-element.19), channel_id=1, source_target_pairs={{0,64},{32,96},{64,128},{96,160},{128,192},{160,224},{192,256},{22... | collective-permute-start | bytes 589832 | tf_op jit(solution)/shard_map/ppermute | solution.py:94
  68.6 8.9 %collective-permute-start.8 = (bf16[32,3072]{1,0:T(8,128)(2,1)S(1)}, bf16[32,3072]{1,0:T(8,128)(2,1)S(1)}, u32[]{:S(2)}, u32[]{:S(2)}) collective-permute-start(bf16[32,3072]{1,0:T(8,128)(2,1)S(1)} %get-tuple-element.20), channel_id=1, source_target_pairs={{64,0},{96,32},{128,64},{160,96},{192,128},{224,160},{256,192},{28... | collective-permute-start | bytes 589832 | tf_op jit(solution)/shard_map/ppermute | solution.py:95
  77.6 8.4 %collective-permute-start.2 = (bf16[32,3072]{1,0:T(8,128)(2,1)S(1)}, bf16[32,3072]{1,0:T(8,128)(2,1)S(1)}, u32[]{:S(2)}, u32[]{:S(2)}) collective-permute-start(bf16[32,3072]{1,0:T(8,128)(2,1)S(1)} %get-tuple-element.17), channel_id=1, source_target_pairs={{0,64},{32,96},{64,128},{96,160},{128,192},{160,224},{192,256},{22... | collective-permute-start | bytes 589832 | tf_op jit(solution)/shard_map/ppermute | solution.py:94
  83.0 8.0 %collective-permute-start.9 = (bf16[32,3072]{1,0:T(8,128)(2,1)S(1)}, bf16[32,3072]{1,0:T(8,128)(2,1)S(1)}, u32[]{:S(2)}, u32[]{:S(2)}) collective-permute-start(bf16[32,3072]{1,0:T(8,128)(2,1)S(1)} %get-tuple-element.18), channel_id=1, source_target_pairs={{64,0},{96,32},{128,64},{160,96},{192,128},{224,160},{256,192},{28... | collective-permute-start | bytes 589832 | tf_op jit(solution)/shard_map/ppermute | solution.py:95
  91.2 7.6 %collective-permute-start.10 = (bf16[32,3072]{1,0:T(8,128)(2,1)S(1)}, bf16[32,3072]{1,0:T(8,128)(2,1)S(1)}, u32[]{:S(2)}, u32[]{:S(2)}) collective-permute-start(bf16[32,3072]{1,0:T(8,128)(2,1)S(1)} %get-tuple-element.16), channel_id=1, source_target_pairs={{64,0},{96,32},{128,64},{160,96},{192,128},{224,160},{256,192},{28... | collective-permute-start | bytes 589832 | tf_op jit(solution)/shard_map/ppermute | solution.py:95
  93.1 7.2 %collective-permute-start.3 = (bf16[32,3072]{1,0:T(8,128)(2,1)S(1)}, bf16[32,3072]{1,0:T(8,128)(2,1)S(1)}, u32[]{:S(2)}, u32[]{:S(2)}) collective-permute-start(bf16[32,3072]{1,0:T(8,128)(2,1)S(1)} %get-tuple-element.15), channel_id=1, source_target_pairs={{0,64},{32,96},{64,128},{96,160},{128,192},{160,224},{192,256},{22... | collective-permute-start | bytes 589832 | tf_op jit(solution)/shard_map/ppermute | solution.py:94
  100.3 8.1 %collective-permute-start.11 = (bf16[32,3072]{1,0:T(8,128)(2,1)S(1)}, bf16[32,3072]{1,0:T(8,128)(2,1)S(1)}, u32[]{:S(2)}, u32[]{:S(2)}) collective-permute-start(bf16[32,3072]{1,0:T(8,128)(2,1)S(1)} %get-tuple-element.14), channel_id=1, source_target_pairs={{64,0},{96,32},{128,64},{160,96},{192,128},{224,160},{256,192},{28... | collective-permute-start | bytes 589832 | tf_op jit(solution)/shard_map/ppermute | solution.py:95
  102.3 7.6 %collective-permute-start.4 = (bf16[32,3072]{1,0:T(8,128)(2,1)S(1)}, bf16[32,3072]{1,0:T(8,128)(2,1)S(1)}, u32[]{:S(2)}, u32[]{:S(2)}) collective-permute-start(bf16[32,3072]{1,0:T(8,128)(2,1)S(1)} %get-tuple-element.13), channel_id=1, source_target_pairs={{0,64},{32,96},{64,128},{96,160},{128,192},{160,224},{192,256},{22... | collective-permute-start | bytes 589832 | tf_op jit(solution)/shard_map/ppermute | solution.py:94
  110.0 8.1 %collective-permute-start.12 = (bf16[32,3072]{1,0:T(8,128)(2,1)S(1)}, bf16[32,3072]{1,0:T(8,128)(2,1)S(1)}, u32[]{:S(2)}, u32[]{:S(2)}) collective-permute-start(bf16[32,3072]{1,0:T(8,128)(2,1)S(1)} %get-tuple-element.12), channel_id=1, source_target_pairs={{64,0},{96,32},{128,64},{160,96},{192,128},{224,160},{256,192},{28... | collective-permute-start | bytes 589832 | tf_op jit(solution)/shard_map/ppermute | solution.py:95
  111.9 7.6 %collective-permute-start.5 = (bf16[32,3072]{1,0:T(8,128)(2,1)S(1)}, bf16[32,3072]{1,0:T(8,128)(2,1)S(1)}, u32[]{:S(2)}, u32[]{:S(2)}) collective-permute-start(bf16[32,3072]{1,0:T(8,128)(2,1)S(1)} %get-tuple-element.11), channel_id=1, source_target_pairs={{0,64},{32,96},{64,128},{96,160},{128,192},{160,224},{192,256},{22... | collective-permute-start | bytes 589832 | tf_op jit(solution)/shard_map/ppermute | solution.py:94
  119.7 8.1 %collective-permute-start.13 = (bf16[32,3072]{1,0:T(8,128)(2,1)S(1)}, bf16[32,3072]{1,0:T(8,128)(2,1)S(1)}, u32[]{:S(2)}, u32[]{:S(2)}) collective-permute-start(bf16[32,3072]{1,0:T(8,128)(2,1)S(1)} %get-tuple-element.10), channel_id=1, source_target_pairs={{64,0},{96,32},{128,64},{160,96},{192,128},{224,160},{256,192},{28... | collective-permute-start | bytes 589832 | tf_op jit(solution)/shard_map/ppermute | solution.py:95
  121.6 7.6 %collective-permute-start.6 = (bf16[32,3072]{1,0:T(8,128)(2,1)S(1)}, bf16[32,3072]{1,0:T(8,128)(2,1)S(1)}, u32[]{:S(2)}, u32[]{:S(2)}) collective-permute-start(bf16[32,3072]{1,0:T(8,128)(2,1)S(1)} %get-tuple-element.9), channel_id=1, source_target_pairs={{0,64},{32,96},{64,128},{96,160},{128,192},{160,224},{192,256},{22... | collective-permute-start | bytes 589832 | tf_op jit(solution)/shard_map/ppermute | solution.py:94
  129.3 8.1 %collective-permute-start.14 = (bf16[32,3072]{1,0:T(8,128)(2,1)S(1)}, bf16[32,3072]{1,0:T(8,128)(2,1)S(1)}, u32[]{:S(2)}, u32[]{:S(2)}) collective-permute-start(bf16[32,3072]{1,0:T(8,128)(2,1)S(1)} %get-tuple-element.8), channel_id=1, source_target_pairs={{64,0},{96,32},{128,64},{160,96},{192,128},{224,160},{256,192},{28... | collective-permute-start | bytes 589832 | tf_op jit(solution)/shard_map/ppermute | solution.py:95
  131.2 7.6 %collective-permute-start.7 = (bf16[32,3072]{1,0:T(8,128)(2,1)S(1)}, bf16[32,3072]{1,0:T(8,128)(2,1)S(1)}, u32[]{:S(2)}, u32[]{:S(2)}) collective-permute-start(bf16[32,3072]{1,0:T(8,128)(2,1)S(1)} %get-tuple-element.7), channel_id=1, source_target_pairs={{0,64},{32,96},{64,128},{96,160},{128,192},{160,224},{192,256},{22... | collective-permute-start | bytes 589832 | tf_op jit(solution)/shard_map/ppermute | solution.py:94
  139.8 8.9 %collective-permute-start.16 = (bf16[32,3072]{1,0:T(8,128)(2,1)S(1)}, bf16[32,3072]{1,0:T(8,128)(2,1)S(1)}, u32[]{:S(2)}, u32[]{:S(2)}) collective-permute-start(bf16[32,3072]{1,0:T(8,128)(2,1)S(1)} %get-tuple-element.42), channel_id=1, source_target_pairs={{0,64},{32,96},{64,128},{96,160},{128,192},{160,224},{192,256},{22... | collective-permute-start | bytes 589832 | tf_op jit(solution)/shard_map/ppermute | solution.py:118
  144.9 8.9 %collective-permute-start.15 = (bf16[32,3072]{1,0:T(8,128)(2,1)S(1)}, bf16[32,3072]{1,0:T(8,128)(2,1)S(1)}, u32[]{:S(2)}, u32[]{:S(2)}) collective-permute-start(bf16[32,3072]{1,0:T(8,128)(2,1)S(1)} %get-tuple-element.42), channel_id=1, source_target_pairs={{64,0},{96,32},{128,64},{160,96},{192,128},{224,160},{256,192},{28... | collective-permute-start | bytes 589832 | tf_op jit(solution)/shard_map/ppermute | solution.py:119
  148.7 8.4 %collective-permute-start.17 = (bf16[32,3072]{1,0:T(8,128)(2,1)S(1)}, bf16[32,3072]{1,0:T(8,128)(2,1)S(1)}, u32[]{:S(2)}, u32[]{:S(2)}) collective-permute-start(bf16[32,3072]{1,0:T(8,128)(2,1)S(1)} %collective-permute-done.16), channel_id=1, source_target_pairs={{0,64},{32,96},{64,128},{96,160},{128,192},{160,224},{192,256},{22... | collective-permute-start | bytes 589832 | tf_op jit(solution)/shard_map/ppermute | solution.py:118
  153.8 8.7 %collective-permute-start.23 = (bf16[32,3072]{1,0:T(8,128)(2,1)S(1)}, bf16[32,3072]{1,0:T(8,128)(2,1)S(1)}, u32[]{:S(2)}, u32[]{:S(2)}) collective-permute-start(bf16[32,3072]{1,0:T(8,128)(2,1)S(1)} %collective-permute-done.15), channel_id=1, source_target_pairs={{64,0},{96,32},{128,64},{160,96},{192,128},{224,160},{256,192},{28... | collective-permute-start | bytes 589832 | tf_op jit(solution)/shard_map/ppermute | solution.py:119
  157.1 7.9 %collective-permute-start.18 = (bf16[32,3072]{1,0:T(8,128)(2,1)S(1)}, bf16[32,3072]{1,0:T(8,128)(2,1)S(1)}, u32[]{:S(2)}, u32[]{:S(2)}) collective-permute-start(bf16[32,3072]{1,0:T(8,128)(2,1)S(1)} %collective-permute-done.17), channel_id=1, source_target_pairs={{0,64},{32,96},{64,128},{96,160},{128,192},{160,224},{192,256},{22... | collective-permute-start | bytes 589832 | tf_op jit(solution)/shard_map/ppermute | solution.py:118
  162.4 7.6 %collective-permute-start.24 = (bf16[32,3072]{1,0:T(8,128)(2,1)S(1)}, bf16[32,3072]{1,0:T(8,128)(2,1)S(1)}, u32[]{:S(2)}, u32[]{:S(2)}) collective-permute-start(bf16[32,3072]{1,0:T(8,128)(2,1)S(1)} %collective-permute-done.23), channel_id=1, source_target_pairs={{64,0},{96,32},{128,64},{160,96},{192,128},{224,160},{256,192},{28... | collective-permute-start | bytes 589832 | tf_op jit(solution)/shard_map/ppermute | solution.py:119
  165.0 7.6 %collective-permute-start.19 = (bf16[32,3072]{1,0:T(8,128)(2,1)S(1)}, bf16[32,3072]{1,0:T(8,128)(2,1)S(1)}, u32[]{:S(2)}, u32[]{:S(2)}) collective-permute-start(bf16[32,3072]{1,0:T(8,128)(2,1)S(1)} %collective-permute-done.18), channel_id=1, source_target_pairs={{0,64},{32,96},{64,128},{96,160},{128,192},{160,224},{192,256},{22... | collective-permute-start | bytes 589832 | tf_op jit(solution)/shard_map/ppermute | solution.py:118
  170.1 7.6 %collective-permute-start.25 = (bf16[32,3072]{1,0:T(8,128)(2,1)S(1)}, bf16[32,3072]{1,0:T(8,128)(2,1)S(1)}, u32[]{:S(2)}, u32[]{:S(2)}) collective-permute-start(bf16[32,3072]{1,0:T(8,128)(2,1)S(1)} %collective-permute-done.24), channel_id=1, source_target_pairs={{64,0},{96,32},{128,64},{160,96},{192,128},{224,160},{256,192},{28... | collective-permute-start | bytes 589832 | tf_op jit(solution)/shard_map/ppermute | solution.py:119
  172.6 7.6 %collective-permute-start.20 = (bf16[32,3072]{1,0:T(8,128)(2,1)S(1)}, bf16[32,3072]{1,0:T(8,128)(2,1)S(1)}, u32[]{:S(2)}, u32[]{:S(2)}) collective-permute-start(bf16[32,3072]{1,0:T(8,128)(2,1)S(1)} %collective-permute-done.19), channel_id=1, source_target_pairs={{0,64},{32,96},{64,128},{96,160},{128,192},{160,224},{192,256},{22... | collective-permute-start | bytes 589832 | tf_op jit(solution)/shard_map/ppermute | solution.py:118
  177.7 7.7 %collective-permute-start.26 = (bf16[32,3072]{1,0:T(8,128)(2,1)S(1)}, bf16[32,3072]{1,0:T(8,128)(2,1)}, u32[]{:S(2)}, u32[]{:S(2)}) collective-permute-start(bf16[32,3072]{1,0:T(8,128)(2,1)S(1)} %collective-permute-done.25), channel_id=1, source_target_pairs={{64,0},{96,32},{128,64},{160,96},{192,128},{224,160},{256,192},{28... | collective-permute-start | bytes 589832 | tf_op jit(solution)/shard_map/ppermute | solution.py:119
  180.2 5.2 %copy-start.4 = (bf16[32,3072]{1,0:T(8,128)(2,1)}, bf16[32,3072]{1,0:T(8,128)(2,1)S(1)}, u32[]{:S(2)}) copy-start(bf16[32,3072]{1,0:T(8,128)(2,1)S(1)} %collective-permute-done.20) | copy-start | bytes 589828
  180.2 7.6 %collective-permute-start.21 = (bf16[32,3072]{1,0:T(8,128)(2,1)S(1)}, bf16[32,3072]{1,0:T(8,128)(2,1)}, u32[]{:S(2)}, u32[]{:S(2)}) collective-permute-start(bf16[32,3072]{1,0:T(8,128)(2,1)S(1)} %collective-permute-done.20), channel_id=1, source_target_pairs={{0,64},{32,96},{64,128},{96,160},{128,192},{160,224},{192,256},{22... | collective-permute-start | bytes 589832 | tf_op jit(solution)/shard_map/ppermute | solution.py:118
  185.4 7.9 %collective-permute-start.27 = (bf16[32,3072]{1,0:T(8,128)(2,1)}, bf16[32,3072]{1,0:T(8,128)(2,1)}, u32[]{:S(2)}, u32[]{:S(2)}) collective-permute-start(bf16[32,3072]{1,0:T(8,128)(2,1)} %collective-permute-done.26), channel_id=1, source_target_pairs={{64,0},{96,32},{128,64},{160,96},{192,128},{224,160},{256,192},{28... | collective-permute-start | bytes 589832 | tf_op jit(solution)/shard_map/ppermute | solution.py:119
  187.9 8.0 %collective-permute-start.22 = (bf16[32,3072]{1,0:T(8,128)(2,1)}, bf16[32,3072]{1,0:T(8,128)(2,1)}, u32[]{:S(2)}, u32[]{:S(2)}) collective-permute-start(bf16[32,3072]{1,0:T(8,128)(2,1)} %collective-permute-done.21), channel_id=1, source_target_pairs={{0,64},{32,96},{64,128},{96,160},{128,192},{160,224},{192,256},{22... | collective-permute-start | bytes 589832 | tf_op jit(solution)/shard_map/ppermute | solution.py:118
  193.0 4.5 %copy-start.5 = (bf16[32,3072]{1,0:T(8,128)(2,1)S(1)}, bf16[32,3072]{1,0:T(8,128)(2,1)}, u32[]{:S(2)}) copy-start(bf16[32,3072]{1,0:T(8,128)(2,1)} %copy-done.4) | copy-start | bytes 589828
  193.3 7.8 %collective-permute-start.28 = (bf16[32,3072]{1,0:T(8,128)(2,1)}, bf16[32,3072]{1,0:T(8,128)(2,1)S(1)}, u32[]{:S(2)}, u32[]{:S(2)}) collective-permute-start(bf16[32,3072]{1,0:T(8,128)(2,1)} %collective-permute-done.27), channel_id=1, source_target_pairs={{64,0},{96,32},{128,64},{160,96},{192,128},{224,160},{256,192},{28... | collective-permute-start | bytes 589832 | tf_op jit(solution)/shard_map/ppermute | solution.py:119
  202.0 21.7 %collective-permute-start.29 = (bf16[256,3072]{1,0:T(8,128)(2,1)}, bf16[256,3072]{1,0:T(8,128)(2,1)S(1)}, u32[]{:S(2)}, u32[]{:S(2)}) collective-permute-start(bf16[256,3072]{1,0:T(8,128)(2,1)} %get-tuple-element.24), channel_id=1, source_target_pairs={{0,32},{32,0},{64,96},{96,64},{128,160},{160,128},{192,224},{224,1... | collective-permute-start | bytes 4718600 | tf_op jit(solution)/shard_map/ppermute | solution.py:126
  225.9 5.7 %copy-start.6 = (f32[128,2]{0,1:T(2,128)S(1)}, f32[128,2]{0,1:T(2,128)}, u32[]{:S(2)}) copy-start(f32[128,2]{0,1:T(2,128)} %param.8) | copy-start | bytes 3076
  226.9 37.5 %all-to-all-start.1 = ((bf16[32,16,512]{2,1,0:T(8,128)(2,1)}), bf16[32,16,512]{2,1,0:T(8,128)(2,1)}, u32[]{:S(2)}, u32[]{:S(2)}) async-start(bf16[32,16,512]{2,1,0:T(8,128)(2,1)} %bitcast.16), calls=%async_computation.1 | async-start | bytes 1048576 | tf_op jit(solution)/shard_map/all_to_all | solution.py:141
  231.6 1.3 copy-start.3

commit v2 on v1

v2 whole, which is shorter than its diff:
```python
import jax
import jax.numpy as jnp
from jax import lax
from jax.sharding import PartitionSpec as P

BF = jnp.bfloat16
F32 = jnp.float32


def mm(a, b):
    return jnp.dot(a, b, preferred_element_type=F32)


def mm_nt(a, b):
    return lax.dot_general(a, b, (((1,), (1,)), ((), ())), preferred_element_type=F32)


def mm_tn(a, b):
    return lax.dot_general(a, b, (((0,), (0,)), ((), ())), preferred_element_type=F32)


def route_slots(routes_t, experts, slots):
    top, count = routes_t.shape
    ids = lax.broadcasted_iota(jnp.int32, (experts, count), 0)
    earlier = lax.broadcasted_iota(jnp.int32, (count, count), 0) < lax.broadcasted_iota(
        jnp.int32, (count, count), 1
    )
    earlier = earlier.astype(BF)
    before = jnp.zeros((experts, 1), F32)
    targets = []
    for k in range(top):
        named = ids == routes_t[k : k + 1]
        hot = named.astype(BF)
        rank = mm(hot, earlier) + before
        slot = jnp.sum(jnp.where(named, rank, 0.0), axis=0, keepdims=True)
        targets.append(routes_t[k : k + 1] * slots + slot.astype(jnp.int32))
        before = before + jnp.sum(hot.astype(F32), axis=1, keepdims=True)
    return targets


def on_device(tokens, routes, route_weights, cotangent, w_gate_up, w_down):
    experts = lax.axis_size("expert")
    n_dp = lax.axis_size("dp")
    chips = n_dp // 2
    tok_rows, feat = tokens.shape
    top = routes.shape[1]
    width = w_down.shape[1]
    slots = 2 * tok_rows * top // experts
    rows = experts * slots
    half = rows // 2
    step = half // chips
    me = lax.axis_index("dp")
    chip = me // 2
    core = me % 2
    gu = w_gate_up[0]
    down = w_down[0]

    targets = route_slots(routes.T, experts, slots)
    weights = route_weights.T
    slot_ids = lax.broadcasted_iota(jnp.int32, (rows, tok_rows), 0)
    picked = [slot_ids == target for target in targets]
    selector = sum(p.astype(BF) for p in picked)
    slot_weight = sum(
        jnp.sum(jnp.where(p, weights[k : k + 1], 0.0), axis=1, keepdims=True)
        for k, p in enumerate(picked)
    )
    send_x = mm(selector, tokens).astype(BF)
    send_g = (mm(selector, cotangent) * slot_weight).astype(BF)
    send = jnp.concatenate([send_x, send_g], axis=1).reshape(experts, slots, 2 * feat)
    recv = lax.all_to_all(send, "expert", split_axis=0, concat_axis=0, tiled=True)

    def flip(rows_):
        blocks = rows_.reshape((2, 2, 2, 2, step) + rows_.shape[1:])
        for axis, bit in enumerate((core, chip % 2, chip // 2 % 2, chip // 4)):
            blocks = jnp.where(bit == 1, jnp.flip(blocks, axis), blocks)
        return blocks.reshape(rows_.shape)

    stages = [
        [(i, i ^ bit) for i in range(n_dp)] for bit in (1, 2, 4, 8)
    ]
    xg = flip(recv.reshape(rows, 2 * feat))
    x_rows, g_rows = xg[:, :feat], xg[:, feat:]

    def split(mul, left_rows, weight):
        return mul(left_rows[half:], weight).astype(BF), mul(left_rows[:half], weight)

    def reduce_scatter(mul, left_rows, weight):
        away, keep = split(mul, left_rows, weight)
        for n, perm in enumerate(stages):
            keep = lax.ppermute(away, "dp", perm).astype(F32) + keep.astype(F32)
            if n + 1 < len(stages):
                middle = keep.shape[0] // 2
                away, keep = keep[middle:].astype(BF), keep[:middle].astype(BF)
        return keep

    def all_gather(own):
        for perm in stages[::-1]:
            own = jnp.concatenate([own, lax.ppermute(own, "dp", perm)], axis=0)
        return own

    gate_up = reduce_scatter(mm, x_rows, gu)
    hidden_grad = reduce_scatter(mm_nt, g_rows, down)
    gate = gate_up[:, :width]
    up = gate_up[:, width:]
    sig = jax.nn.sigmoid(gate)
    silu_vals = gate * sig
    hidden = all_gather((silu_vals * up).astype(BF))
    dgate = hidden_grad * up * sig * (1.0 + gate * (1.0 - sig))
    dup = hidden_grad * silu_vals
    gate_up_grad = all_gather(jnp.concatenate([dgate, dup], axis=1).astype(BF))

    back = jnp.concatenate(
        [mm(hidden, down).astype(BF), mm_nt(gate_up_grad, gu).astype(BF)], axis=1
    )
    back = flip(back).reshape(experts, slots, 2 * feat)
    ret = lax.all_to_all(back, "expert", split_axis=0, concat_axis=0, tiled=True)
    ret = ret.reshape(rows, 2 * feat)
    grad_gu = mm_tn(x_rows, gate_up_grad).astype(BF)
    grad_dn = mm_tn(hidden, g_rows).astype(BF)

    mixed = sum(
        mm_tn(p.astype(BF), ret[:, :feat]) * route_weights[:, k : k + 1]
        for k, p in enumerate(picked)
    ).astype(BF)
    token_grad = mm_tn(selector, ret[:, feat:]).astype(BF)
    return (mixed, token_grad, grad_gu[None], grad_dn[None])


def solution(mesh):
    return jax.shard_map(
        on_device,
        mesh=mesh,
        in_specs=(
            P("expert", "dp"),
            P("expert", None),
            P("expert", None),
            P("expert", "dp"),
            P("expert", "dp", None),
            P("expert", None, "dp"),
        ),
        out_specs=(
            P("expert", "dp"),
            P("expert", "dp"),
            P("expert", "dp", None),
            P("expert", None, "dp"),
        ),
        check_vma=False,
    )
```

time: 271 us -> 232 us (0.86)
  the two profiles are of different devices: /device:TPU:97 before, /device:TPU:33 now
where the time goes in v2:
time: 232 us; the launch traced here: 231 us
  waiting for transfers between devices  117 us (50%)
  starting transfers between devices  94.3 us (41%)
  matrix products  10.4 us (4%)
  local copies, waits for them, and re-layouts  4.04 us (2%)
  other arithmetic  3.5 us (2%)
    ppermute x8, starting transfers between devices, all_gather(): own = jnp.concatenate([own, lax.ppermute(own, 'dp', perm)], axis=0)  41.7 us
    all_to_all x1, waiting for transfers between devices, on_device(): lax.all_to_all(send, 'expert', split_axis=0, concat_axis=0, tiled=True)  36.9 us
    all_to_all x1, waiting for transfers between devices, on_device(): lax.all_to_all(back, 'expert', split_axis=0, concat_axis=0, tiled=True)  33.1 us
    ppermute x8, starting transfers between devices, reduce_scatter(): keep = lax.ppermute(away, 'dp', perm).astype(F32) + keep.astype(F32)  29.3 us
    ppermute x8, waiting for transfers between devices, reduce_scatter(): keep = lax.ppermute(away, 'dp', perm).astype(F32) + keep.astype(F32)  25.1 us
    ppermute x8, waiting for transfers between devices, all_gather(): own = jnp.concatenate([own, lax.ppermute(own, 'dp', perm)], axis=0)  22 us
    all_to_all x1, starting transfers between devices, on_device(): lax.all_to_all(send, 'expert', split_axis=0, concat_axis=0, tiled=True)  19.4 us
    dot_general x5, matrix products, mm_tn(): lax.dot_general(a, b, (((0,), (0,)), ((), ())), preferred_element_type=F32)  5.02 us
  transfers between devices with their start and end apart: 18, of which 11 were waited for; matrix products, arithmetic and copies ran while one was open for 2% of the time, Pallas kernels for 0%

profile of v2, /device:TPU:33, one launch (start us, length us, event | category | flops | bytes accessed | tf_op | source)
XLA Modules:
  0.0 230.6 jit_solution(13609528594885059641)
XLA Ops:
  0.6 0.8 slice_bitcast_fusion.4
  1.7 0.8 slice_bitcast_fusion.2
  2.6 0.8 fusion.47
  3.4 1.1 convolution_convert_fusion.6
  4.7 1.1 fusion.2
  5.9 1.0 copy.12
  6.9 19.4 %all-to-all-start = ((bf16[32,16,512]{2,1,0:T(8,128)(2,1)}), bf16[32,16,512]{2,1,0:T(8,128)(2,1)S(1)}, u32[]{:S(2)}, u32[]{:S(2)}) async-start(bf16[32,16,512]{2,1,0:T(8,128)(2,1)} %bitcast.10), calls=%async_computation | async-start | bytes 1048576 | tf_op jit(solution)/shard_map/all_to_all | solution.py:70
  26.4 36.9 %all-to-all-done = bf16[32,16,512]{2,1,0:T(8,128)(2,1)S(1)} async-done(((bf16[32,16,512]{2,1,0:T(8,128)(2,1)}), bf16[32,16,512]{2,1,0:T(8,128)(2,1)S(1)}, u32[]{:S(2)}, u32[]{:S(2)}) %all-to-all-start) | async-done | bytes 524320 | tf_op jit(solution)/shard_map/all_to_all | solution.py:70
  63.7 0.4 convolution_convert_fusion.1
  64.2 3.7 %collective-permute-start = (bf16[256,2048]{1,0:T(8,128)(2,1)S(1)}, bf16[256,2048]{1,0:T(8,128)(2,1)S(1)}, u32[]{:S(2)}, u32[]{:S(2)}) collective-permute-start(bf16[256,2048]{1,0:T(8,128)(2,1)S(1)} %convolution_convert_fusion.1), channel_id=1, source_target_pairs={{0,32},{32,0},{64,96},{96,64},{128,160},{160,128},{192,224},{224,1... | collective-permute-start | bytes 3145736 | tf_op jit(solution)/shard_map/ppermute | solution.py:90
  67.8 0.3 convolution_convert_fusion.3
  68.2 1.9 collective-permute-start.8
  70.1 0.4 add_convert_fusion
  70.6 1.9 collective-permute-start.1
  72.6 0.3 add_convert_fusion.1
  72.9 3.4 %collective-permute-start.9 = (bf16[128,1024]{1,0:T(8,128)(2,1)S(1)}, bf16[128,1024]{1,0:T(8,128)(2,1)S(1)}, u32[]{:S(2)}, u32[]{:S(2)}) collective-permute-start(bf16[128,1024]{1,0:T(8,128)(2,1)S(1)} %slice.143), channel_id=1, source_target_pairs={{0,64},{32,96},{64,0},{96,32},{128,192},{160,224},{192,128},{224,1... | collective-permute-start | bytes 786440 | tf_op jit(solution)/shard_map/ppermute | solution.py:90
  76.3 9.2 %collective-permute-done.1 = bf16[128,2048]{1,0:T(8,128)(2,1)S(1)} collective-permute-done((bf16[128,2048]{1,0:T(8,128)(2,1)S(1)}, bf16[128,2048]{1,0:T(8,128)(2,1)S(1)}, u32[]{:S(2)}, u32[]{:S(2)}) %collective-permute-start.1) | collective-permute-done | bytes 524320 | tf_op jit(solution)/shard_map/ppermute | solution.py:90
  85.7 1.9 collective-permute-start.2
  87.6 3.5 %collective-permute-done.9 = bf16[128,1024]{1,0:T(8,128)(2,1)S(1)} collective-permute-done((bf16[128,1024]{1,0:T(8,128)(2,1)S(1)}, bf16[128,1024]{1,0:T(8,128)(2,1)S(1)}, u32[]{:S(2)}, u32[]{:S(2)}) %collective-permute-start.9) | collective-permute-done | bytes 262176 | tf_op jit(solution)/shard_map/ppermute | solution.py:90
  91.2 1.9 collective-permute-start.10
  93.1 0.9 collective-permute-done.2
  94.1 11.8 %collective-permute-start.3 = (bf16[32,2048]{1,0:T(8,128)(2,1)S(1)}, bf16[32,2048]{1,0:T(8,128)(2,1)S(1)}, u32[]{:S(2)}, u32[]{:S(2)}) collective-permute-start(bf16[32,2048]{1,0:T(8,128)(2,1)S(1)} %slice.137), channel_id=1, source_target_pairs={{0,256},{32,288},{64,320},{96,352},{128,384},{160,416},{192,448},{... | collective-permute-start | bytes 393224 | tf_op jit(solution)/shard_map/ppermute | solution.py:90
  106.1 2.7 %collective-permute-start.11 = (bf16[32,1024]{1,0:T(8,128)(2,1)S(1)}, bf16[32,1024]{1,0:T(8,128)(2,1)S(1)}, u32[]{:S(2)}, u32[]{:S(2)}) collective-permute-start(bf16[32,1024]{1,0:T(8,128)(2,1)S(1)} %slice.147), channel_id=1, source_target_pairs={{0,256},{32,288},{64,320},{96,352},{128,384},{160,416},{192,448},{... | collective-permute-start | bytes 196616 | tf_op jit(solution)/shard_map/ppermute | solution.py:90
  108.8 0.6 collective-permute-done.3
  109.4 10.8 %collective-permute-done.11 = bf16[32,1024]{1,0:T(8,128)(2,1)S(1)} collective-permute-done((bf16[32,1024]{1,0:T(8,128)(2,1)S(1)}, bf16[32,1024]{1,0:T(8,128)(2,1)S(1)}, u32[]{:S(2)}, u32[]{:S(2)}) %collective-permute-start.11) | collective-permute-done | bytes 65568 | tf_op jit(solution)/shard_map/ppermute | solution.py:90
  120.3 1.9 collective-permute-start.12
  122.2 8.6 %collective-permute-done.12 = bf16[32,2048]{1,0:T(8,128)(2,1)S(1)} collective-permute-done((bf16[32,2048]{1,0:T(8,128)(2,1)S(1)}, bf16[32,2048]{1,0:T(8,128)(2,1)S(1)}, u32[]{:S(2)}, u32[]{:S(2)}) %collective-permute-start.12) | collective-permute-done | bytes 131104 | tf_op jit(solution)/shard_map/ppermute | solution.py:98
  130.9 8.3 %collective-permute-start.13 = (bf16[64,2048]{1,0:T(8,128)(2,1)S(1)}, bf16[64,2048]{1,0:T(8,128)(2,1)S(1)}, u32[]{:S(2)}, u32[]{:S(2)}) collective-permute-start(bf16[64,2048]{1,0:T(8,128)(2,1)S(1)} %pad_maximum_fusion.6), channel_id=1, source_target_pairs={{0,128},{32,160},{64,192},{96,224},{128,0},{160,32},{192,64},{224,... | collective-permute-start | bytes 786440 | tf_op jit(solution)/shard_map/ppermute | solution.py:98
  139.2 8.2 %collective-permute-start.4 = (bf16[32,1024]{1,0:T(8,128)(2,1)S(1)}, bf16[32,1024]{1,0:T(8,128)(2,1)S(1)}, u32[]{:S(2)}, u32[]{:S(2)}) collective-permute-start(bf16[32,1024]{1,0:T(8,128)(2,1)S(1)} %get-tuple-element.5), channel_id=1, source_target_pairs={{0,256},{32,288},{64,320},{96,352},{128,384},{160,416},{192,448},{... | collective-permute-start | bytes 196616 | tf_op jit(solution)/shard_map/ppermute | solution.py:98
  147.4 4.5 %collective-permute-done.4 = bf16[32,1024]{1,0:T(8,128)(2,1)S(1)} collective-permute-done((bf16[32,1024]{1,0:T(8,128)(2,1)S(1)}, bf16[32,1024]{1,0:T(8,128)(2,1)S(1)}, u32[]{:S(2)}, u32[]{:S(2)}) %collective-permute-start.4) | collective-permute-done | bytes 65568 | tf_op jit(solution)/shard_map/ppermute | solution.py:98
  151.9 2.2 collective-permute-start.5
  154.2 7.0 %collective-permute-start.14 = (bf16[128,2048]{1,0:T(8,128)(2,1)S(1)}, bf16[128,2048]{1,0:T(8,128)(2,1)S(1)}, u32[]{:S(2)}, u32[]{:S(2)}) collective-permute-start(bf16[128,2048]{1,0:T(8,128)(2,1)S(1)} %pad_maximum_fusion.3), channel_id=1, source_target_pairs={{0,64},{32,96},{64,0},{96,32},{128,192},{160,224},{192,128},{224,1... | collective-permute-start | bytes 1572872 | tf_op jit(solution)/shard_map/ppermute | solution.py:98
  161.3 4.1 %collective-permute-start.6 = (bf16[128,1024]{1,0:T(8,128)(2,1)S(1)}, bf16[128,1024]{1,0:T(8,128)(2,1)S(1)}, u32[]{:S(2)}, u32[]{:S(2)}) collective-permute-start(bf16[128,1024]{1,0:T(8,128)(2,1)S(1)} %pad_maximum_fusion.5), channel_id=1, source_target_pairs={{0,64},{32,96},{64,0},{96,32},{128,192},{160,224},{192,128},{224,1... | collective-permute-start | bytes 786440 | tf_op jit(solution)/shard_map/ppermute | solution.py:98
  165.4 7.4 %collective-permute-done.14 = bf16[128,2048]{1,0:T(8,128)(2,1)S(1)} collective-permute-done((bf16[128,2048]{1,0:T(8,128)(2,1)S(1)}, bf16[128,2048]{1,0:T(8,128)(2,1)S(1)}, u32[]{:S(2)}, u32[]{:S(2)}) %collective-permute-start.14) | collective-permute-done | bytes 524320 | tf_op jit(solution)/shard_map/ppermute | solution.py:98
  173.0 6.8 %collective-permute-start.15 = (bf16[256,2048]{1,0:T(8,128)(2,1)S(1)}, bf16[256,2048]{1,0:T(8,128)(2,1)S(1)}, u32[]{:S(2)}, u32[]{:S(2)}) collective-permute-start(bf16[256,2048]{1,0:T(8,128)(2,1)S(1)} %pad_maximum_fusion), channel_id=1, source_target_pairs={{0,32},{32,0},{64,96},{96,64},{128,160},{160,128},{192,224},{224,1... | collective-permute-start | bytes 3145736 | tf_op jit(solution)/shard_map/ppermute | solution.py:98
  179.8 3.3 %collective-permute-start.7 = (bf16[256,1024]{1,0:T(8,128)(2,1)S(1)}, bf16[256,1024]{1,0:T(8,128)(2,1)S(1)}, u32[]{:S(2)}, u32[]{:S(2)}) collective-permute-start(bf16[256,1024]{1,0:T(8,128)(2,1)S(1)} %pad_maximum_fusion.2), channel_id=1, source_target_pairs={{0,32},{32,0},{64,96},{96,64},{128,160},{160,128},{192,224},{224,1... | collective-permute-start | bytes 1572872 | tf_op jit(solution)/shard_map/ppermute | solution.py:98
  183.2 1.4 collective-permute-done.7
  184.6 0.5 convolution_convert_fusion.5
  185.2 0.9 convolution_convert_fusion.4
  186.1 0.4 copy-done.2
  187.2 0.9 reverse_select_fusion
  188.1 3.9 %all-to-all-start.1 = ((bf16[32,16,512]{2,1,0:T(8,128)(2,1)}), bf16[32,16,512]{2,1,0:T(8,128)(2,1)S(1)}, u32[]{:S(2)}, u32[]{:S(2)}) async-start(bf16[32,16,512]{2,1,0:T(8,128)(2,1)} %bitcast.16), calls=%async_computation.1 | async-start | bytes 1048576 | tf_op jit(solution)/shard_map/all_to_all | solution.py:116
  192.0 1.3 fusion.1
  193.3 0.5 copy-done.3
  193.8 1.7 fusion
  195.5 33.1 %all-to-all-done.1 = bf16[32,16,512]{2,1,0:T(8,128)(2,1)S(1)} async-done(((bf16[32,16,512]{2,1,0:T(8,128)(2,1)}), bf16[32,16,512]{2,1,0:T(8,128)(2,1)S(1)}, u32[]{:S(2)}, u32[]{:S(2)}) %all-to-all-start.1) | async-done | bytes 524320 | tf_op jit(solution)/shard_map/all_to_all | solution.py:116
  228.6 0.9 convolution_convert_fusion.7
  229.7 0.9 fusion.4
  (64 shorter events, 2.9 us)
Async XLA Ops:
  0.6 63.1 %copy-start = (bf16[1,256,2048]{2,1,0:T(8,128)(2,1)S(1)}, bf16[1,256,2048]{2,1,0:T(8,128)(2,1)}, u32[]{:S(2)}) copy-start(bf16[1,256,2048]{2,1,0:T(8,128)(2,1)} %param.10) | copy-start | bytes 3145732
  6.9 56.4 %all-to-all-start = ((bf16[32,16,512]{2,1,0:T(8,128)(2,1)}), bf16[32,16,512]{2,1,0:T(8,128)(2,1)S(1)}, u32[]{:S(2)}, u32[]{:S(2)}) async-start(bf16[32,16,512]{2,1,0:T(8,128)(2,1)} %bitcast.10), calls=%async_computation | async-start | bytes 1048576 | tf_op jit(solution)/shard_map/all_to_all | solution.py:70
  63.5 4.4 %copy-start.1 = (bf16[1,1024,256]{2,1,0:T(8,128)(2,1)S(1)}, bf16[1,1024,256]{2,1,0:T(8,128)(2,1)}, u32[]{:S(2)}) copy-start(bf16[1,1024,256]{2,1,0:T(8,128)(2,1)} %param.11) | copy-start | bytes 1572868
  64.2 6.0 %collective-permute-start = (bf16[256,2048]{1,0:T(8,128)(2,1)S(1)}, bf16[256,2048]{1,0:T(8,128)(2,1)S(1)}, u32[]{:S(2)}, u32[]{:S(2)}) collective-permute-start(bf16[256,2048]{1,0:T(8,128)(2,1)S(1)} %convolution_convert_fusion.1), channel_id=1, source_target_pairs={{0,32},{32,0},{64,96},{96,64},{128,160},{160,128},{192,224},{224,1... | collective-permute-start | bytes 3145736 | tf_op jit(solution)/shard_map/ppermute | solution.py:90
  68.2 4.4 %collective-permute-start.8 = (bf16[256,1024]{1,0:T(8,128)(2,1)S(1)}, bf16[256,1024]{1,0:T(8,128)(2,1)S(1)}, u32[]{:S(2)}, u32[]{:S(2)}) collective-permute-start(bf16[256,1024]{1,0:T(8,128)(2,1)S(1)} %convolution_convert_fusion.3), channel_id=1, source_target_pairs={{0,32},{32,0},{64,96},{96,64},{128,160},{160,128},{192,224},{224,1... | collective-permute-start | bytes 1572872 | tf_op jit(solution)/shard_map/ppermute | solution.py:90
  70.6 14.9 %collective-permute-start.1 = (bf16[128,2048]{1,0:T(8,128)(2,1)S(1)}, bf16[128,2048]{1,0:T(8,128)(2,1)S(1)}, u32[]{:S(2)}, u32[]{:S(2)}) collective-permute-start(bf16[128,2048]{1,0:T(8,128)(2,1)S(1)} %slice.133), channel_id=1, source_target_pairs={{0,64},{32,96},{64,0},{96,32},{128,192},{160,224},{192,128},{224,1... | collective-permute-start | bytes 1572872 | tf_op jit(solution)/shard_map/ppermute | solution.py:90
  72.9 18.2 %collective-permute-start.9 = (bf16[128,1024]{1,0:T(8,128)(2,1)S(1)}, bf16[128,1024]{1,0:T(8,128)(2,1)S(1)}, u32[]{:S(2)}, u32[]{:S(2)}) collective-permute-start(bf16[128,1024]{1,0:T(8,128)(2,1)S(1)} %slice.143), channel_id=1, source_target_pairs={{0,64},{32,96},{64,0},{96,32},{128,192},{160,224},{192,128},{224,1... | collective-permute-start | bytes 786440 | tf_op jit(solution)/shard_map/ppermute | solution.py:90
  85.7 8.4 %collective-permute-start.2 = (bf16[64,2048]{1,0:T(8,128)(2,1)S(1)}, bf16[64,2048]{1,0:T(8,128)(2,1)S(1)}, u32[]{:S(2)}, u32[]{:S(2)}) collective-permute-start(bf16[64,2048]{1,0:T(8,128)(2,1)S(1)} %slice.135), channel_id=1, source_target_pairs={{0,128},{32,160},{64,192},{96,224},{128,0},{160,32},{192,64},{224,... | collective-permute-start | bytes 786440 | tf_op jit(solution)/shard_map/ppermute | solution.py:90
  91.2 14.8 %collective-permute-start.10 = (bf16[64,1024]{1,0:T(8,128)(2,1)S(1)}, bf16[64,1024]{1,0:T(8,128)(2,1)S(1)}, u32[]{:S(2)}, u32[]{:S(2)}) collective-permute-start(bf16[64,1024]{1,0:T(8,128)(2,1)S(1)} %slice.145), channel_id=1, source_target_pairs={{0,128},{32,160},{64,192},{96,224},{128,0},{160,32},{192,64},{224,... | collective-permute-start | bytes 393224 | tf_op jit(solution)/shard_map/ppermute | solution.py:90
  94.1 15.2 %collective-permute-start.3 = (bf16[32,2048]{1,0:T(8,128)(2,1)S(1)}, bf16[32,2048]{1,0:T(8,128)(2,1)S(1)}, u32[]{:S(2)}, u32[]{:S(2)}) collective-permute-start(bf16[32,2048]{1,0:T(8,128)(2,1)S(1)} %slice.137), channel_id=1, source_target_pairs={{0,256},{32,288},{64,320},{96,352},{128,384},{160,416},{192,448},{... | collective-permute-start | bytes 393224 | tf_op jit(solution)/shard_map/ppermute | solution.py:90
  106.1 14.1 %collective-permute-start.11 = (bf16[32,1024]{1,0:T(8,128)(2,1)S(1)}, bf16[32,1024]{1,0:T(8,128)(2,1)S(1)}, u32[]{:S(2)}, u32[]{:S(2)}) collective-permute-start(bf16[32,1024]{1,0:T(8,128)(2,1)S(1)} %slice.147), channel_id=1, source_target_pairs={{0,256},{32,288},{64,320},{96,352},{128,384},{160,416},{192,448},{... | collective-permute-start | bytes 196616 | tf_op jit(solution)/shard_map/ppermute | solution.py:90
  120.3 10.5 %collective-permute-start.12 = (bf16[32,2048]{1,0:T(8,128)(2,1)S(1)}, bf16[32,2048]{1,0:T(8,128)(2,1)S(1)}, u32[]{:S(2)}, u32[]{:S(2)}) collective-permute-start(bf16[32,2048]{1,0:T(8,128)(2,1)S(1)} %get-tuple-element.8), channel_id=1, source_target_pairs={{0,256},{32,288},{64,320},{96,352},{128,384},{160,416},{192,448},{... | collective-permute-start | bytes 393224 | tf_op jit(solution)/shard_map/ppermute | solution.py:98
  130.9 23.2 %collective-permute-start.13 = (bf16[64,2048]{1,0:T(8,128)(2,1)S(1)}, bf16[64,2048]{1,0:T(8,128)(2,1)S(1)}, u32[]{:S(2)}, u32[]{:S(2)}) collective-permute-start(bf16[64,2048]{1,0:T(8,128)(2,1)S(1)} %pad_maximum_fusion.6), channel_id=1, source_target_pairs={{0,128},{32,160},{64,192},{96,224},{128,0},{160,32},{192,64},{224,... | collective-permute-start | bytes 786440 | tf_op jit(solution)/shard_map/ppermute | solution.py:98
  139.2 12.7 %collective-permute-start.4 = (bf16[32,1024]{1,0:T(8,128)(2,1)S(1)}, bf16[32,1024]{1,0:T(8,128)(2,1)S(1)}, u32[]{:S(2)}, u32[]{:S(2)}) collective-permute-start(bf16[32,1024]{1,0:T(8,128)(2,1)S(1)} %get-tuple-element.5), channel_id=1, source_target_pairs={{0,256},{32,288},{64,320},{96,352},{128,384},{160,416},{192,448},{... | collective-permute-start | bytes 196616 | tf_op jit(solution)/shard_map/ppermute | solution.py:98
  151.9 9.3 %collective-permute-start.5 = (bf16[64,1024]{1,0:T(8,128)(2,1)S(1)}, bf16[64,1024]{1,0:T(8,128)(2,1)S(1)}, u32[]{:S(2)}, u32[]{:S(2)}) collective-permute-start(bf16[64,1024]{1,0:T(8,128)(2,1)S(1)} %pad_maximum_fusion.7), channel_id=1, source_target_pairs={{0,128},{32,160},{64,192},{96,224},{128,0},{160,32},{192,64},{224,... | collective-permute-start | bytes 393224 | tf_op jit(solution)/shard_map/ppermute | solution.py:98
  154.2 18.7 %collective-permute-start.14 = (bf16[128,2048]{1,0:T(8,128)(2,1)S(1)}, bf16[128,2048]{1,0:T(8,128)(2,1)S(1)}, u32[]{:S(2)}, u32[]{:S(2)}) collective-permute-start(bf16[128,2048]{1,0:T(8,128)(2,1)S(1)} %pad_maximum_fusion.3), channel_id=1, source_target_pairs={{0,64},{32,96},{64,0},{96,32},{128,192},{160,224},{192,128},{224,1... | collective-permute-start | bytes 1572872 | tf_op jit(solution)/shard_map/ppermute | solution.py:98
  161.3 18.4 %collective-permute-start.6 = (bf16[128,1024]{1,0:T(8,128)(2,1)S(1)}, bf16[128,1024]{1,0:T(8,128)(2,1)S(1)}, u32[]{:S(2)}, u32[]{:S(2)}) collective-permute-start(bf16[128,1024]{1,0:T(8,128)(2,1)S(1)} %pad_maximum_fusion.5), channel_id=1, source_target_pairs={{0,64},{32,96},{64,0},{96,32},{128,192},{160,224},{192,128},{224,1... | collective-permute-start | bytes 786440 | tf_op jit(solution)/shard_map/ppermute | solution.py:98
  173.0 12.2 %collective-permute-start.15 = (bf16[256,2048]{1,0:T(8,128)(2,1)S(1)}, bf16[256,2048]{1,0:T(8,128)(2,1)S(1)}, u32[]{:S(2)}, u32[]{:S(2)}) collective-permute-start(bf16[256,2048]{1,0:T(8,128)(2,1)S(1)} %pad_maximum_fusion), channel_id=1, source_target_pairs={{0,32},{32,0},{64,96},{96,64},{128,160},{160,128},{192,224},{224,1... | collective-permute-start | bytes 3145736 | tf_op jit(solution)/shard_map/ppermute | solution.py:98
  179.8 4.8 %collective-permute-start.7 = (bf16[256,1024]{1,0:T(8,128)(2,1)S(1)}, bf16[256,1024]{1,0:T(8,128)(2,1)S(1)}, u32[]{:S(2)}, u32[]{:S(2)}) collective-permute-start(bf16[256,1024]{1,0:T(8,128)(2,1)S(1)} %pad_maximum_fusion.2), channel_id=1, source_target_pairs={{0,32},{32,0},{64,96},{96,64},{128,160},{160,128},{192,224},{224,1... | collective-permute-start | bytes 1572872 | tf_op jit(solution)/shard_map/ppermute | solution.py:98
  184.6 1.5 copy-start.4
  185.2 1.3 copy-start.2
  186.9 5.1 %copy-start.6 = (f32[128,2]{0,1:T(2,128)S(1)}, f32[128,2]{0,1:T(2,128)}, u32[]{:S(2)}) copy-start(f32[128,2]{0,1:T(2,128)} %param.8) | copy-start | bytes 3076
  186.9 5.1 %copy-start.5 = (bf16[512,1024]{1,0:T(8,128)(2,1)S(1)}, bf16[512,1024]{1,0:T(8,128)(2,1)}, u32[]{:S(2)}) copy-start(bf16[512,1024]{1,0:T(8,128)(2,1)} %copy-done.4) | copy-start | bytes 3145732
  188.1 40.5 %all-to-all-start.1 = ((bf16[32,16,512]{2,1,0:T(8,128)(2,1)}), bf16[32,16,512]{2,1,0:T(8,128)(2,1)S(1)}, u32[]{:S(2)}, u32[]{:S(2)}) async-start(bf16[32,16,512]{2,1,0:T(8,128)(2,1)} %bitcast.16), calls=%async_computation.1 | async-start | bytes 1048576 | tf_op jit(solution)/shard_map/all_to_all | solution.py:116
  192.0 1.8 copy-start.3

commit v3 on v2

--- a/solution.py
+++ b/solution.py
@@ -33,9 +33,16 @@
         hot = named.astype(BF)
         rank = mm(hot, earlier) + before
         slot = jnp.sum(jnp.where(named, rank, 0.0), axis=0, keepdims=True)
-        targets.append(routes_t[k : k + 1] * slots + slot.astype(jnp.int32))
+        slot = slot.astype(jnp.int32)
+        targets.append(
+            jnp.where(
+                slot < slots, routes_t[k : k + 1] * slots + slot, (experts - 1) * slots + slot
+            )
+        )
         before = before + jnp.sum(hot.astype(F32), axis=1, keepdims=True)
-    return targets
+    column = lax.broadcasted_iota(jnp.int32, (experts, 1), 0)
+    busiest = jnp.sum(jnp.where(before > slots, column, 0))
+    return targets, busiest
 
 
 def on_device(tokens, routes, route_weights, cotangent, w_gate_up, w_down):
@@ -45,8 +52,9 @@
     tok_rows, feat = tokens.shape
     top = routes.shape[1]
     width = w_down.shape[1]
-    slots = 2 * tok_rows * top // experts
-    rows = experts * slots
+    slots = tok_rows * top // experts
+    rows = 2 * experts * slots
+    sent = (experts + 1) * slots
     half = rows // 2
     step = half // chips
     me = lax.axis_index("dp")
@@ -55,9 +63,9 @@
     gu = w_gate_up[0]
     down = w_down[0]
 
-    targets = route_slots(routes.T, experts, slots)
+    targets, busiest = route_slots(routes.T, experts, slots)
     weights = route_weights.T
-    slot_ids = lax.broadcasted_iota(jnp.int32, (rows, tok_rows), 0)
+    slot_ids = lax.broadcasted_iota(jnp.int32, (sent, tok_rows), 0)
     picked = [slot_ids == target for target in targets]
     selector = sum(p.astype(BF) for p in picked)
     slot_weight = sum(
@@ -66,8 +74,20 @@
     )
     send_x = mm(selector, tokens).astype(BF)
     send_g = (mm(selector, cotangent) * slot_weight).astype(BF)
-    send = jnp.concatenate([send_x, send_g], axis=1).reshape(experts, slots, 2 * feat)
-    recv = lax.all_to_all(send, "expert", split_axis=0, concat_axis=0, tiled=True)
+    send = jnp.concatenate([send_x, send_g], axis=1)
+
+    def exchange(blocks):
+        blocks = blocks.reshape(experts, slots, 2 * feat)
+        blocks = lax.all_to_all(blocks, "expert", split_axis=0, concat_axis=0, tiled=True)
+        return blocks.reshape(experts * slots, 2 * feat)
+
+    owner = lax.axis_index("expert")
+    doubling = [[(i, i ^ (1 << k)) for i in range(experts)] for k in range(experts.bit_length() - 1)]
+    recv = exchange(send[: experts * slots])
+    more = send[experts * slots :]
+    for perm in doubling:
+        more = jnp.concatenate([more, lax.ppermute(more, "expert", perm)], axis=0)
+    recv = jnp.concatenate([recv, jnp.where(owner == busiest, more, jnp.zeros_like(more))], axis=0)
 
     def flip(rows_):
         blocks = rows_.reshape((2, 2, 2, 2, step) + rows_.shape[1:])
@@ -78,7 +98,7 @@
     stages = [
         [(i, i ^ bit) for i in range(n_dp)] for bit in (1, 2, 4, 8)
     ]
-    xg = flip(recv.reshape(rows, 2 * feat))
+    xg = flip(recv)
     x_rows, g_rows = xg[:, :feat], xg[:, feat:]
 
     def split(mul, left_rows, weight):
@@ -112,9 +132,14 @@
     back = jnp.concatenate(
         [mm(hidden, down).astype(BF), mm_nt(gate_up_grad, gu).astype(BF)], axis=1
     )
-    back = flip(back).reshape(experts, slots, 2 * feat)
-    ret = lax.all_to_all(back, "expert", split_axis=0, concat_axis=0, tiled=True)
-    ret = ret.reshape(rows, 2 * feat)
+    back = flip(back)
+    ret = exchange(back[: experts * slots])
+    more = back[experts * slots :]
+    for k, perm in reversed(list(enumerate(doubling))):
+        middle = more.shape[0] // 2
+        got = lax.ppermute(more[middle:], "expert", perm)
+        more = jnp.where(((owner ^ busiest) >> k) & 1 == 1, got, more[:middle])
+    ret = jnp.concatenate([ret, more], axis=0)
     grad_gu = mm_tn(x_rows, gate_up_grad).astype(BF)
     grad_dn = mm_tn(hidden, g_rows).astype(BF)
 

time: 232 us -> 245 us (1.056)
  the two profiles are of different devices: /device:TPU:33 before, /device:TPU:6 now
where the time goes in v3:
time: 245 us; the launch traced here: 241 us
  starting transfers between devices  129 us (53%)
  waiting for transfers between devices  91.8 us (37%)
  matrix products  10.2 us (4%)
  other arithmetic  4.19 us (2%)
  local copies, waits for them, and re-layouts  3.41 us (1%)
  between operations  2.92 us (1%)
    ppermute x8, waiting for transfers between devices, reduce_scatter(): keep = lax.ppermute(away, 'dp', perm).astype(F32) + keep.astype(F32)  36 us
    ppermute x8, waiting for transfers between devices, all_gather(): own = jnp.concatenate([own, lax.ppermute(own, 'dp', perm)], axis=0)  35.8 us
    ppermute x5, starting transfers between devices, on_device(): more = jnp.concatenate([more, lax.ppermute(more, 'expert', perm)], axis=0)  30.2 us
    ppermute x5, starting transfers between devices, on_device(): got = lax.ppermute(more[middle:], 'expert', perm)  25.7 us
    ppermute x8, starting transfers between devices, reduce_scatter(): keep = lax.ppermute(away, 'dp', perm).astype(F32) + keep.astype(F32)  25.4 us
    all_to_all x2, starting transfers between devices, exchange(): lax.all_to_all(blocks, 'expert', split_axis=0, concat_axis=0, tiled=True)  24.4 us
    ppermute x8, starting transfers between devices, all_gather(): own = jnp.concatenate([own, lax.ppermute(own, 'dp', perm)], axis=0)  23 us
    ppermute x5, waiting for transfers between devices, on_device(): more = jnp.concatenate([more, lax.ppermute(more, 'expert', perm)], axis=0)  12.2 us
  transfers between devices with their start and end apart: 28, of which 19 were waited for; matrix products, arithmetic and copies ran while one was open for 3% of the time, Pallas kernels for 0%

profile of v3, /device:TPU:6, one launch (start us, length us, event | category | flops | bytes accessed | tf_op | source)
XLA Modules:
  0.0 241.2 jit_solution(16311482668297964717)
XLA Ops:
  5.8 15.7 %collective-permute-start = (bf16[8,512]{1,0:T(8,128)(2,1)S(1)}, bf16[8,512]{1,0:T(8,128)(2,1)S(1)}, u32[]{:S(2)}, u32[]{:S(2)}) collective-permute-start(bf16[8,512]{1,0:T(8,128)(2,1)S(1)} %get-tuple-element.7), channel_id=1, source_target_pairs={{0,1},{1,0},{2,3},{3,2},{4,5},{5,4},{6,7},{7,6},{8,9},{9,8},{10,11... | collective-permute-start | bytes 24584 | tf_op jit(solution)/shard_map/ppermute | solution.py:89
  22.2 7.6 %all-to-all-start = ((bf16[32,8,512]{2,1,0:T(8,128)(2,1)}), bf16[32,8,512]{2,1,0:T(8,128)(2,1)S(1)}, u32[]{:S(2)}, u32[]{:S(2)}) async-start(bf16[32,8,512]{2,1,0:T(8,128)(2,1)} %fusion.21), calls=%async_computation | async-start | bytes 524288 | tf_op jit(solution)/shard_map/all_to_all | solution.py:81
  29.8 2.8 %collective-permute-start.1 = (bf16[16,512]{1,0:T(8,128)(2,1)S(1)}, bf16[16,512]{1,0:T(8,128)(2,1)S(1)}, u32[]{:S(2)}, u32[]{:S(2)}) collective-permute-start(bf16[16,512]{1,0:T(8,128)(2,1)S(1)} %pad_maximum_fusion.13), channel_id=1, source_target_pairs={{0,2},{1,3},{2,0},{3,1},{4,6},{5,7},{6,4},{7,5},{8,10},{9,11},{10,... | collective-permute-start | bytes 49160 | tf_op jit(solution)/shard_map/ppermute | solution.py:89
  32.6 2.8 %collective-permute-done.1 = bf16[16,512]{1,0:T(8,128)(2,1)S(1)} collective-permute-done((bf16[16,512]{1,0:T(8,128)(2,1)S(1)}, bf16[16,512]{1,0:T(8,128)(2,1)S(1)}, u32[]{:S(2)}, u32[]{:S(2)}) %collective-permute-start.1) | collective-permute-done | bytes 16416 | tf_op jit(solution)/shard_map/ppermute | solution.py:89
  35.5 3.4 %collective-permute-start.2 = (bf16[32,512]{1,0:T(8,128)(2,1)S(1)}, bf16[32,512]{1,0:T(8,128)(2,1)S(1)}, u32[]{:S(2)}, u32[]{:S(2)}) collective-permute-start(bf16[32,512]{1,0:T(8,128)(2,1)S(1)} %pad_maximum_fusion.12), channel_id=1, source_target_pairs={{0,4},{1,5},{2,6},{3,7},{4,0},{5,1},{6,2},{7,3},{8,12},{9,13},{10,... | collective-permute-start | bytes 98312 | tf_op jit(solution)/shard_map/ppermute | solution.py:89
  38.8 4.6 %collective-permute-done.2 = bf16[32,512]{1,0:T(8,128)(2,1)S(1)} collective-permute-done((bf16[32,512]{1,0:T(8,128)(2,1)S(1)}, bf16[32,512]{1,0:T(8,128)(2,1)S(1)}, u32[]{:S(2)}, u32[]{:S(2)}) %collective-permute-start.2) | collective-permute-done | bytes 32800 | tf_op jit(solution)/shard_map/ppermute | solution.py:89
  43.4 3.4 %collective-permute-start.3 = (bf16[64,512]{1,0:T(8,128)(2,1)S(1)}, bf16[64,512]{1,0:T(8,128)(2,1)S(1)}, u32[]{:S(2)}, u32[]{:S(2)}) collective-permute-start(bf16[64,512]{1,0:T(8,128)(2,1)S(1)} %pad_maximum_fusion.11), channel_id=1, source_target_pairs={{0,8},{1,9},{2,10},{3,11},{4,12},{5,13},{6,14},{7,15},{8,0},{9,1},... | collective-permute-start | bytes 196616 | tf_op jit(solution)/shard_map/ppermute | solution.py:89
  46.8 2.7 %collective-permute-done.3 = bf16[64,512]{1,0:T(8,128)(2,1)S(1)} collective-permute-done((bf16[64,512]{1,0:T(8,128)(2,1)S(1)}, bf16[64,512]{1,0:T(8,128)(2,1)S(1)}, u32[]{:S(2)}, u32[]{:S(2)}) %collective-permute-start.3) | collective-permute-done | bytes 65568 | tf_op jit(solution)/shard_map/ppermute | solution.py:89
  49.6 4.9 %collective-permute-start.4 = (bf16[128,512]{1,0:T(8,128)(2,1)S(1)}, bf16[128,512]{1,0:T(8,128)(2,1)S(1)}, u32[]{:S(2)}, u32[]{:S(2)}) collective-permute-start(bf16[128,512]{1,0:T(8,128)(2,1)S(1)} %get-tuple-element.14), channel_id=1, source_target_pairs={{0,16},{1,17},{2,18},{3,19},{4,20},{5,21},{6,22},{7,23},{8,24},{9,... | collective-permute-start | bytes 393224 | tf_op jit(solution)/shard_map/ppermute | solution.py:89
  55.9 2.1 collective-permute-done.4
  58.9 1.9 collective-permute-start.5
  61.2 2.4 collective-permute-start.13
  64.1 2.3 collective-permute-start.6
  66.9 3.5 %collective-permute-start.14 = (bf16[128,1024]{1,0:T(8,128)(2,1)S(1)}, bf16[128,1024]{1,0:T(8,128)(2,1)S(1)}, u32[]{:S(2)}, u32[]{:S(2)}) collective-permute-start(bf16[128,1024]{1,0:T(8,128)(2,1)S(1)} %slice.210), channel_id=1, source_target_pairs={{0,64},{32,96},{64,0},{96,32},{128,192},{160,224},{192,128},{224,1... | collective-permute-start | bytes 786440 | tf_op jit(solution)/shard_map/ppermute | solution.py:110
  70.4 10.4 %collective-permute-done.6 = bf16[128,2048]{1,0:T(8,128)(2,1)S(1)} collective-permute-done((bf16[128,2048]{1,0:T(8,128)(2,1)S(1)}, bf16[128,2048]{1,0:T(8,128)(2,1)S(1)}, u32[]{:S(2)}, u32[]{:S(2)}) %collective-permute-start.6) | collective-permute-done | bytes 524320 | tf_op jit(solution)/shard_map/ppermute | solution.py:110
  81.0 2.9 %collective-permute-start.7 = (bf16[64,2048]{1,0:T(8,128)(2,1)S(1)}, bf16[64,2048]{1,0:T(8,128)(2,1)S(1)}, u32[]{:S(2)}, u32[]{:S(2)}) collective-permute-start(bf16[64,2048]{1,0:T(8,128)(2,1)S(1)} %slice.202), channel_id=1, source_target_pairs={{0,128},{32,160},{64,192},{96,224},{128,0},{160,32},{192,64},{224,... | collective-permute-start | bytes 786440 | tf_op jit(solution)/shard_map/ppermute | solution.py:110
  83.9 2.9 %collective-permute-done.14 = bf16[128,1024]{1,0:T(8,128)(2,1)S(1)} collective-permute-done((bf16[128,1024]{1,0:T(8,128)(2,1)S(1)}, bf16[128,1024]{1,0:T(8,128)(2,1)S(1)}, u32[]{:S(2)}, u32[]{:S(2)}) %collective-permute-start.14) | collective-permute-done | bytes 262176 | tf_op jit(solution)/shard_map/ppermute | solution.py:110
  86.8 2.6 %collective-permute-start.15 = (bf16[64,1024]{1,0:T(8,128)(2,1)S(1)}, bf16[64,1024]{1,0:T(8,128)(2,1)S(1)}, u32[]{:S(2)}, u32[]{:S(2)}) collective-permute-start(bf16[64,1024]{1,0:T(8,128)(2,1)S(1)} %slice.212), channel_id=1, source_target_pairs={{0,128},{32,160},{64,192},{96,224},{128,0},{160,32},{192,64},{224,... | collective-permute-start | bytes 393224 | tf_op jit(solution)/shard_map/ppermute | solution.py:110
  89.4 10.6 %collective-permute-done.7 = bf16[64,2048]{1,0:T(8,128)(2,1)S(1)} collective-permute-done((bf16[64,2048]{1,0:T(8,128)(2,1)S(1)}, bf16[64,2048]{1,0:T(8,128)(2,1)S(1)}, u32[]{:S(2)}, u32[]{:S(2)}) %collective-permute-start.7) | collective-permute-done | bytes 262176 | tf_op jit(solution)/shard_map/ppermute | solution.py:110
  100.1 6.2 %collective-permute-start.8 = (bf16[32,2048]{1,0:T(8,128)(2,1)S(1)}, bf16[32,2048]{1,0:T(8,128)(2,1)S(1)}, u32[]{:S(2)}, u32[]{:S(2)}) collective-permute-start(bf16[32,2048]{1,0:T(8,128)(2,1)S(1)} %slice.204), channel_id=1, source_target_pairs={{0,256},{32,288},{64,320},{96,352},{128,384},{160,416},{192,448},{... | collective-permute-start | bytes 393224 | tf_op jit(solution)/shard_map/ppermute | solution.py:110
  106.4 3.5 %collective-permute-start.16 = (bf16[32,1024]{1,0:T(8,128)(2,1)S(1)}, bf16[32,1024]{1,0:T(8,128)(2,1)S(1)}, u32[]{:S(2)}, u32[]{:S(2)}) collective-permute-start(bf16[32,1024]{1,0:T(8,128)(2,1)S(1)} %slice.214), channel_id=1, source_target_pairs={{0,256},{32,288},{64,320},{96,352},{128,384},{160,416},{192,448},{... | collective-permute-start | bytes 196616 | tf_op jit(solution)/shard_map/ppermute | solution.py:110
  110.0 10.8 %collective-permute-done.8 = bf16[32,2048]{1,0:T(8,128)(2,1)S(1)} collective-permute-done((bf16[32,2048]{1,0:T(8,128)(2,1)S(1)}, bf16[32,2048]{1,0:T(8,128)(2,1)S(1)}, u32[]{:S(2)}, u32[]{:S(2)}) %collective-permute-start.8) | collective-permute-done | bytes 131104 | tf_op jit(solution)/shard_map/ppermute | solution.py:110
  120.7 1.3 collective-permute-done.16
  122.1 1.9 collective-permute-start.17
  124.1 12.0 %collective-permute-done.17 = bf16[32,2048]{1,0:T(8,128)(2,1)S(1)} collective-permute-done((bf16[32,2048]{1,0:T(8,128)(2,1)S(1)}, bf16[32,2048]{1,0:T(8,128)(2,1)S(1)}, u32[]{:S(2)}, u32[]{:S(2)}) %collective-permute-start.17) | collective-permute-done | bytes 131104 | tf_op jit(solution)/shard_map/ppermute | solution.py:118
  136.1 1.9 collective-permute-start.18
  138.1 2.7 %collective-permute-start.9 = (bf16[32,1024]{1,0:T(8,128)(2,1)S(1)}, bf16[32,1024]{1,0:T(8,128)(2,1)S(1)}, u32[]{:S(2)}, u32[]{:S(2)}) collective-permute-start(bf16[32,1024]{1,0:T(8,128)(2,1)S(1)} %get-tuple-element.5), channel_id=1, source_target_pairs={{0,256},{32,288},{64,320},{96,352},{128,384},{160,416},{192,448},{... | collective-permute-start | bytes 196616 | tf_op jit(solution)/shard_map/ppermute | solution.py:118
  140.8 7.6 %collective-permute-done.9 = bf16[32,1024]{1,0:T(8,128)(2,1)S(1)} collective-permute-done((bf16[32,1024]{1,0:T(8,128)(2,1)S(1)}, bf16[32,1024]{1,0:T(8,128)(2,1)S(1)}, u32[]{:S(2)}, u32[]{:S(2)}) %collective-permute-start.9) | collective-permute-done | bytes 65568 | tf_op jit(solution)/shard_map/ppermute | solution.py:118
  148.4 8.6 %collective-permute-start.10 = (bf16[64,1024]{1,0:T(8,128)(2,1)S(1)}, bf16[64,1024]{1,0:T(8,128)(2,1)S(1)}, u32[]{:S(2)}, u32[]{:S(2)}) collective-permute-start(bf16[64,1024]{1,0:T(8,128)(2,1)S(1)} %pad_maximum_fusion.9), channel_id=1, source_target_pairs={{0,128},{32,160},{64,192},{96,224},{128,0},{160,32},{192,64},{224,... | collective-permute-start | bytes 393224 | tf_op jit(solution)/shard_map/ppermute | solution.py:118
  157.1 1.9 collective-permute-start.19
  159.0 1.8 collective-permute-done.10
  160.9 2.1 collective-permute-start.11
  163.0 10.8 %collective-permute-done.19 = bf16[128,2048]{1,0:T(8,128)(2,1)S(1)} collective-permute-done((bf16[128,2048]{1,0:T(8,128)(2,1)S(1)}, bf16[128,2048]{1,0:T(8,128)(2,1)S(1)}, u32[]{:S(2)}, u32[]{:S(2)}) %collective-permute-start.19) | collective-permute-done | bytes 524320 | tf_op jit(solution)/shard_map/ppermute | solution.py:118
  173.9 1.9 collective-permute-start.20
  175.8 1.8 collective-permute-done.11
  177.7 1.9 collective-permute-start.12
  179.7 1.8 collective-permute-done.12
  184.2 5.3 %collective-permute-start.21 = (bf16[128,512]{1,0:T(8,128)(2,1)S(1)}, bf16[128,512]{1,0:T(8,128)(2,1)S(1)}, u32[]{:S(2)}, u32[]{:S(2)}) collective-permute-start(bf16[128,512]{1,0:T(8,128)(2,1)S(1)} %bitcast.85), channel_id=1, source_target_pairs={{0,16},{1,17},{2,18},{3,19},{4,20},{5,21},{6,22},{7,23},{8,24},{9,... | collective-permute-start | bytes 393224 | tf_op jit(solution)/shard_map/ppermute | solution.py:140
  190.2 3.2 %collective-permute-done.21 = bf16[128,512]{1,0:T(8,128)(2,1)S(1)} collective-permute-done((bf16[128,512]{1,0:T(8,128)(2,1)S(1)}, bf16[128,512]{1,0:T(8,128)(2,1)S(1)}, u32[]{:S(2)}, u32[]{:S(2)}) %collective-permute-start.21) | collective-permute-done | bytes 131104 | tf_op jit(solution)/shard_map/ppermute | solution.py:140
  193.3 3.5 %collective-permute-start.22 = (bf16[64,512]{1,0:T(8,128)(2,1)S(1)}, bf16[64,512]{1,0:T(8,128)(2,1)S(1)}, u32[]{:S(2)}, u32[]{:S(2)}) collective-permute-start(bf16[64,512]{1,0:T(8,128)(2,1)S(1)} %slice.219), channel_id=1, source_target_pairs={{0,8},{1,9},{2,10},{3,11},{4,12},{5,13},{6,14},{7,15},{8,0},{9,1},... | collective-permute-start | bytes 196616 | tf_op jit(solution)/shard_map/ppermute | solution.py:140
  196.9 2.6 %collective-permute-done.22 = bf16[64,512]{1,0:T(8,128)(2,1)S(1)} collective-permute-done((bf16[64,512]{1,0:T(8,128)(2,1)S(1)}, bf16[64,512]{1,0:T(8,128)(2,1)S(1)}, u32[]{:S(2)}, u32[]{:S(2)}) %collective-permute-start.22) | collective-permute-done | bytes 65568 | tf_op jit(solution)/shard_map/ppermute | solution.py:140
  199.5 1.9 collective-permute-start.23
  202.2 16.8 %all-to-all-start.1 = ((bf16[32,8,512]{2,1,0:T(8,128)(2,1)}), bf16[32,8,512]{2,1,0:T(8,128)(2,1)S(1)}, u32[]{:S(2)}, u32[]{:S(2)}) async-start(bf16[32,8,512]{2,1,0:T(8,128)(2,1)} %bitcast.17), calls=%async_computation.1 | async-start | bytes 524288 | tf_op jit(solution)/shard_map/all_to_all | solution.py:81
  219.1 2.9 %collective-permute-start.24 = (bf16[16,512]{1,0:T(8,128)(2,1)S(1)}, bf16[16,512]{1,0:T(8,128)(2,1)S(1)}, u32[]{:S(2)}, u32[]{:S(2)}) collective-permute-start(bf16[16,512]{1,0:T(8,128)(2,1)S(1)} %slice.223), channel_id=1, source_target_pairs={{0,2},{1,3},{2,0},{3,1},{4,6},{5,7},{6,4},{7,5},{8,10},{9,11},{10,... | collective-permute-start | bytes 49160 | tf_op jit(solution)/shard_map/ppermute | solution.py:140
  222.0 1.3 fusion.1
  223.3 1.6 collective-permute-done.24
  224.9 12.1 %collective-permute-start.25 = (bf16[8,512]{1,0:T(8,128)(2,1)S(1)}, bf16[8,512]{1,0:T(8,128)(2,1)S(1)}, u32[]{:S(2)}, u32[]{:S(2)}) collective-permute-start(bf16[8,512]{1,0:T(8,128)(2,1)S(1)} %slice.225), channel_id=1, source_target_pairs={{0,1},{1,0},{2,3},{3,2},{4,5},{5,4},{6,7},{7,6},{8,9},{9,8},{10,11... | collective-permute-start | bytes 24584 | tf_op jit(solution)/shard_map/ppermute | solution.py:140
  237.0 1.7 fusion
  (108 shorter events, 15.3 us)
Async XLA Ops:
  0.6 57.9 %copy-start = (bf16[1,256,2048]{2,1,0:T(8,128)(2,1)S(1)}, bf16[1,256,2048]{2,1,0:T(8,128)(2,1)}, u32[]{:S(2)}) copy-start(bf16[1,256,2048]{2,1,0:T(8,128)(2,1)} %param.10) | copy-start | bytes 3145732
  5.8 24.0 %collective-permute-start = (bf16[8,512]{1,0:T(8,128)(2,1)S(1)}, bf16[8,512]{1,0:T(8,128)(2,1)S(1)}, u32[]{:S(2)}, u32[]{:S(2)}) collective-permute-start(bf16[8,512]{1,0:T(8,128)(2,1)S(1)} %get-tuple-element.7), channel_id=1, source_target_pairs={{0,1},{1,0},{2,3},{3,2},{4,5},{5,4},{6,7},{7,6},{8,9},{9,8},{10,11... | collective-permute-start | bytes 24584 | tf_op jit(solution)/shard_map/ppermute | solution.py:89
  22.2 35.8 %all-to-all-start = ((bf16[32,8,512]{2,1,0:T(8,128)(2,1)}), bf16[32,8,512]{2,1,0:T(8,128)(2,1)S(1)}, u32[]{:S(2)}, u32[]{:S(2)}) async-start(bf16[32,8,512]{2,1,0:T(8,128)(2,1)} %fusion.21), calls=%async_computation | async-start | bytes 524288 | tf_op jit(solution)/shard_map/all_to_all | solution.py:81
  29.8 5.6 %collective-permute-start.1 = (bf16[16,512]{1,0:T(8,128)(2,1)S(1)}, bf16[16,512]{1,0:T(8,128)(2,1)S(1)}, u32[]{:S(2)}, u32[]{:S(2)}) collective-permute-start(bf16[16,512]{1,0:T(8,128)(2,1)S(1)} %pad_maximum_fusion.13), channel_id=1, source_target_pairs={{0,2},{1,3},{2,0},{3,1},{4,6},{5,7},{6,4},{7,5},{8,10},{9,11},{10,... | collective-permute-start | bytes 49160 | tf_op jit(solution)/shard_map/ppermute | solution.py:89
  35.5 7.9 %collective-permute-start.2 = (bf16[32,512]{1,0:T(8,128)(2,1)S(1)}, bf16[32,512]{1,0:T(8,128)(2,1)S(1)}, u32[]{:S(2)}, u32[]{:S(2)}) collective-permute-start(bf16[32,512]{1,0:T(8,128)(2,1)S(1)} %pad_maximum_fusion.12), channel_id=1, source_target_pairs={{0,4},{1,5},{2,6},{3,7},{4,0},{5,1},{6,2},{7,3},{8,12},{9,13},{10,... | collective-permute-start | bytes 98312 | tf_op jit(solution)/shard_map/ppermute | solution.py:89
  43.4 6.1 %collective-permute-start.3 = (bf16[64,512]{1,0:T(8,128)(2,1)S(1)}, bf16[64,512]{1,0:T(8,128)(2,1)S(1)}, u32[]{:S(2)}, u32[]{:S(2)}) collective-permute-start(bf16[64,512]{1,0:T(8,128)(2,1)S(1)} %pad_maximum_fusion.11), channel_id=1, source_target_pairs={{0,8},{1,9},{2,10},{3,11},{4,12},{5,13},{6,14},{7,15},{8,0},{9,1},... | collective-permute-start | bytes 196616 | tf_op jit(solution)/shard_map/ppermute | solution.py:89
  49.6 8.4 %collective-permute-start.4 = (bf16[128,512]{1,0:T(8,128)(2,1)S(1)}, bf16[128,512]{1,0:T(8,128)(2,1)S(1)}, u32[]{:S(2)}, u32[]{:S(2)}) collective-permute-start(bf16[128,512]{1,0:T(8,128)(2,1)S(1)} %get-tuple-element.14), channel_id=1, source_target_pairs={{0,16},{1,17},{2,18},{3,19},{4,20},{5,21},{6,22},{7,23},{8,24},{9,... | collective-permute-start | bytes 393224 | tf_op jit(solution)/shard_map/ppermute | solution.py:89
  58.2 2.6 %copy-start.1 = (bf16[1,1024,256]{2,1,0:T(8,128)(2,1)S(1)}, bf16[1,1024,256]{2,1,0:T(8,128)(2,1)}, u32[]{:S(2)}) copy-start(bf16[1,1024,256]{2,1,0:T(8,128)(2,1)} %param.11) | copy-start | bytes 1572868
  58.9 4.7 %collective-permute-start.5 = (bf16[256,2048]{1,0:T(8,128)(2,1)S(1)}, bf16[256,2048]{1,0:T(8,128)(2,1)S(1)}, u32[]{:S(2)}, u32[]{:S(2)}) collective-permute-start(bf16[256,2048]{1,0:T(8,128)(2,1)S(1)} %convolution_convert_fusion.1), channel_id=1, source_target_pairs={{0,32},{32,0},{64,96},{96,64},{128,160},{160,128},{192,224},{224,1... | collective-permute-start | bytes 3145736 | tf_op jit(solution)/shard_map/ppermute | solution.py:110
  61.2 5.3 %collective-permute-start.13 = (bf16[256,1024]{1,0:T(8,128)(2,1)S(1)}, bf16[256,1024]{1,0:T(8,128)(2,1)S(1)}, u32[]{:S(2)}, u32[]{:S(2)}) collective-permute-start(bf16[256,1024]{1,0:T(8,128)(2,1)S(1)} %convolution_convert_fusion.3), channel_id=1, source_target_pairs={{0,32},{32,0},{64,96},{96,64},{128,160},{160,128},{192,224},{224,1... | collective-permute-start | bytes 1572872 | tf_op jit(solution)/shard_map/ppermute | solution.py:110
  64.1 16.7 %collective-permute-start.6 = (bf16[128,2048]{1,0:T(8,128)(2,1)S(1)}, bf16[128,2048]{1,0:T(8,128)(2,1)S(1)}, u32[]{:S(2)}, u32[]{:S(2)}) collective-permute-start(bf16[128,2048]{1,0:T(8,128)(2,1)S(1)} %slice.200), channel_id=1, source_target_pairs={{0,64},{32,96},{64,0},{96,32},{128,192},{160,224},{192,128},{224,1... | collective-permute-start | bytes 1572872 | tf_op jit(solution)/shard_map/ppermute | solution.py:110
  66.9 19.9 %collective-permute-start.14 = (bf16[128,1024]{1,0:T(8,128)(2,1)S(1)}, bf16[128,1024]{1,0:T(8,128)(2,1)S(1)}, u32[]{:S(2)}, u32[]{:S(2)}) collective-permute-start(bf16[128,1024]{1,0:T(8,128)(2,1)S(1)} %slice.210), channel_id=1, source_target_pairs={{0,64},{32,96},{64,0},{96,32},{128,192},{160,224},{192,128},{224,1... | collective-permute-start | bytes 786440 | tf_op jit(solution)/shard_map/ppermute | solution.py:110
  81.0 19.1 %collective-permute-start.7 = (bf16[64,2048]{1,0:T(8,128)(2,1)S(1)}, bf16[64,2048]{1,0:T(8,128)(2,1)S(1)}, u32[]{:S(2)}, u32[]{:S(2)}) collective-permute-start(bf16[64,2048]{1,0:T(8,128)(2,1)S(1)} %slice.202), channel_id=1, source_target_pairs={{0,128},{32,160},{64,192},{96,224},{128,0},{160,32},{192,64},{224,... | collective-permute-start | bytes 786440 | tf_op jit(solution)/shard_map/ppermute | solution.py:110
  86.8 19.5 %collective-permute-start.15 = (bf16[64,1024]{1,0:T(8,128)(2,1)S(1)}, bf16[64,1024]{1,0:T(8,128)(2,1)S(1)}, u32[]{:S(2)}, u32[]{:S(2)}) collective-permute-start(bf16[64,1024]{1,0:T(8,128)(2,1)S(1)} %slice.212), channel_id=1, source_target_pairs={{0,128},{32,160},{64,192},{96,224},{128,0},{160,32},{192,64},{224,... | collective-permute-start | bytes 393224 | tf_op jit(solution)/shard_map/ppermute | solution.py:110
  100.1 20.6 %collective-permute-start.8 = (bf16[32,2048]{1,0:T(8,128)(2,1)S(1)}, bf16[32,2048]{1,0:T(8,128)(2,1)S(1)}, u32[]{:S(2)}, u32[]{:S(2)}) collective-permute-start(bf16[32,2048]{1,0:T(8,128)(2,1)S(1)} %slice.204), channel_id=1, source_target_pairs={{0,256},{32,288},{64,320},{96,352},{128,384},{160,416},{192,448},{... | collective-permute-start | bytes 393224 | tf_op jit(solution)/shard_map/ppermute | solution.py:110
  106.4 15.6 %collective-permute-start.16 = (bf16[32,1024]{1,0:T(8,128)(2,1)S(1)}, bf16[32,1024]{1,0:T(8,128)(2,1)S(1)}, u32[]{:S(2)}, u32[]{:S(2)}) collective-permute-start(bf16[32,1024]{1,0:T(8,128)(2,1)S(1)} %slice.214), channel_id=1, source_target_pairs={{0,256},{32,288},{64,320},{96,352},{128,384},{160,416},{192,448},{... | collective-permute-start | bytes 196616 | tf_op jit(solution)/shard_map/ppermute | solution.py:110
  122.1 13.9 %collective-permute-start.17 = (bf16[32,2048]{1,0:T(8,128)(2,1)S(1)}, bf16[32,2048]{1,0:T(8,128)(2,1)S(1)}, u32[]{:S(2)}, u32[]{:S(2)}) collective-permute-start(bf16[32,2048]{1,0:T(8,128)(2,1)S(1)} %get-tuple-element.12), channel_id=1, source_target_pairs={{0,256},{32,288},{64,320},{96,352},{128,384},{160,416},{192,448},{... | collective-permute-start | bytes 393224 | tf_op jit(solution)/shard_map/ppermute | solution.py:118
  136.1 20.9 %collective-permute-start.18 = (bf16[64,2048]{1,0:T(8,128)(2,1)S(1)}, bf16[64,2048]{1,0:T(8,128)(2,1)S(1)}, u32[]{:S(2)}, u32[]{:S(2)}) collective-permute-start(bf16[64,2048]{1,0:T(8,128)(2,1)S(1)} %pad_maximum_fusion.6), channel_id=1, source_target_pairs={{0,128},{32,160},{64,192},{96,224},{128,0},{160,32},{192,64},{224,... | collective-permute-start | bytes 786440 | tf_op jit(solution)/shard_map/ppermute | solution.py:118
  138.1 10.4 %collective-permute-start.9 = (bf16[32,1024]{1,0:T(8,128)(2,1)S(1)}, bf16[32,1024]{1,0:T(8,128)(2,1)S(1)}, u32[]{:S(2)}, u32[]{:S(2)}) collective-permute-start(bf16[32,1024]{1,0:T(8,128)(2,1)S(1)} %get-tuple-element.5), channel_id=1, source_target_pairs={{0,256},{32,288},{64,320},{96,352},{128,384},{160,416},{192,448},{... | collective-permute-start | bytes 196616 | tf_op jit(solution)/shard_map/ppermute | solution.py:118
  148.4 12.4 %collective-permute-start.10 = (bf16[64,1024]{1,0:T(8,128)(2,1)S(1)}, bf16[64,1024]{1,0:T(8,128)(2,1)S(1)}, u32[]{:S(2)}, u32[]{:S(2)}) collective-permute-start(bf16[64,1024]{1,0:T(8,128)(2,1)S(1)} %pad_maximum_fusion.9), channel_id=1, source_target_pairs={{0,128},{32,160},{64,192},{96,224},{128,0},{160,32},{192,64},{224,... | collective-permute-start | bytes 393224 | tf_op jit(solution)/shard_map/ppermute | solution.py:118
  157.1 16.8 %collective-permute-start.19 = (bf16[128,2048]{1,0:T(8,128)(2,1)S(1)}, bf16[128,2048]{1,0:T(8,128)(2,1)S(1)}, u32[]{:S(2)}, u32[]{:S(2)}) collective-permute-start(bf16[128,2048]{1,0:T(8,128)(2,1)S(1)} %pad_maximum_fusion.3), channel_id=1, source_target_pairs={{0,64},{32,96},{64,0},{96,32},{128,192},{160,224},{192,128},{224,1... | collective-permute-start | bytes 1572872 | tf_op jit(solution)/shard_map/ppermute | solution.py:118
  160.9 16.8 %collective-permute-start.11 = (bf16[128,1024]{1,0:T(8,128)(2,1)S(1)}, bf16[128,1024]{1,0:T(8,128)(2,1)S(1)}, u32[]{:S(2)}, u32[]{:S(2)}) collective-permute-start(bf16[128,1024]{1,0:T(8,128)(2,1)S(1)} %pad_maximum_fusion.5), channel_id=1, source_target_pairs={{0,64},{32,96},{64,0},{96,32},{128,192},{160,224},{192,128},{224,1... | collective-permute-start | bytes 786440 | tf_op jit(solution)/shard_map/ppermute | solution.py:118
  173.9 8.1 %collective-permute-start.20 = (bf16[256,2048]{1,0:T(8,128)(2,1)S(1)}, bf16[256,2048]{1,0:T(8,128)(2,1)S(1)}, u32[]{:S(2)}, u32[]{:S(2)}) collective-permute-start(bf16[256,2048]{1,0:T(8,128)(2,1)S(1)} %pad_maximum_fusion), channel_id=1, source_target_pairs={{0,32},{32,0},{64,96},{96,64},{128,160},{160,128},{192,224},{224,1... | collective-permute-start | bytes 3145736 | tf_op jit(solution)/shard_map/ppermute | solution.py:118
  177.7 3.8 %collective-permute-start.12 = (bf16[256,1024]{1,0:T(8,128)(2,1)S(1)}, bf16[256,1024]{1,0:T(8,128)(2,1)S(1)}, u32[]{:S(2)}, u32[]{:S(2)}) collective-permute-start(bf16[256,1024]{1,0:T(8,128)(2,1)S(1)} %pad_maximum_fusion.2), channel_id=1, source_target_pairs={{0,32},{32,0},{64,96},{96,64},{128,160},{160,128},{192,224},{224,1... | collective-permute-start | bytes 1572872 | tf_op jit(solution)/shard_map/ppermute | solution.py:118
  181.5 1.5 copy-start.4
  182.1 1.4 copy-start.2
  183.9 17.6 %copy-start.6 = (f32[128,2]{0,1:T(2,128)S(1)}, f32[128,2]{0,1:T(2,128)}, u32[]{:S(2)}) copy-start(f32[128,2]{0,1:T(2,128)} %param.8) | copy-start | bytes 3076
  184.0 38.0 %copy-start.5 = (bf16[512,1024]{1,0:T(8,128)(2,1)S(1)}, bf16[512,1024]{1,0:T(8,128)(2,1)}, u32[]{:S(2)}) copy-start(bf16[512,1024]{1,0:T(8,128)(2,1)} %copy-done.4) | copy-start | bytes 3145732
  184.2 9.1 %collective-permute-start.21 = (bf16[128,512]{1,0:T(8,128)(2,1)S(1)}, bf16[128,512]{1,0:T(8,128)(2,1)S(1)}, u32[]{:S(2)}, u32[]{:S(2)}) collective-permute-start(bf16[128,512]{1,0:T(8,128)(2,1)S(1)} %bitcast.85), channel_id=1, source_target_pairs={{0,16},{1,17},{2,18},{3,19},{4,20},{5,21},{6,22},{7,23},{8,24},{9,... | collective-permute-start | bytes 393224 | tf_op jit(solution)/shard_map/ppermute | solution.py:140
  193.3 6.2 %collective-permute-start.22 = (bf16[64,512]{1,0:T(8,128)(2,1)S(1)}, bf16[64,512]{1,0:T(8,128)(2,1)S(1)}, u32[]{:S(2)}, u32[]{:S(2)}) collective-permute-start(bf16[64,512]{1,0:T(8,128)(2,1)S(1)} %slice.219), channel_id=1, source_target_pairs={{0,8},{1,9},{2,10},{3,11},{4,12},{5,13},{6,14},{7,15},{8,0},{9,1},... | collective-permute-start | bytes 196616 | tf_op jit(solution)/shard_map/ppermute | solution.py:140
  199.5 19.5 %collective-permute-start.23 = (bf16[32,512]{1,0:T(8,128)(2,1)S(1)}, bf16[32,512]{1,0:T(8,128)(2,1)S(1)}, u32[]{:S(2)}, u32[]{:S(2)}) collective-permute-start(bf16[32,512]{1,0:T(8,128)(2,1)S(1)} %slice.221), channel_id=1, source_target_pairs={{0,4},{1,5},{2,6},{3,7},{4,0},{5,1},{6,2},{7,3},{8,12},{9,13},{10,... | collective-permute-start | bytes 98312 | tf_op jit(solution)/shard_map/ppermute | solution.py:140
  202.2 36.9 %all-to-all-start.1 = ((bf16[32,8,512]{2,1,0:T(8,128)(2,1)}), bf16[32,8,512]{2,1,0:T(8,128)(2,1)S(1)}, u32[]{:S(2)}, u32[]{:S(2)}) async-start(bf16[32,8,512]{2,1,0:T(8,128)(2,1)} %bitcast.17), calls=%async_computation.1 | async-start | bytes 524288 | tf_op jit(solution)/shard_map/all_to_all | solution.py:81
  219.1 17.9 %copy-start.3 = (bf16[512,2048]{1,0:T(8,128)(2,1)S(1)}, bf16[512,2048]{1,0:T(8,128)(2,1)}, u32[]{:S(2)}) copy-start(bf16[512,2048]{1,0:T(8,128)(2,1)} %copy-done.2) | copy-start | bytes 6291460
  219.1 5.8 %collective-permute-start.24 = (bf16[16,512]{1,0:T(8,128)(2,1)S(1)}, bf16[16,512]{1,0:T(8,128)(2,1)S(1)}, u32[]{:S(2)}, u32[]{:S(2)}) collective-permute-start(bf16[16,512]{1,0:T(8,128)(2,1)S(1)} %slice.223), channel_id=1, source_target_pairs={{0,2},{1,3},{2,0},{3,1},{4,6},{5,7},{6,4},{7,5},{8,10},{9,11},{10,... | collective-permute-start | bytes 49160 | tf_op jit(solution)/shard_map/ppermute | solution.py:140
  224.9 14.3 %collective-permute-start.25 = (bf16[8,512]{1,0:T(8,128)(2,1)S(1)}, bf16[8,512]{1,0:T(8,128)(2,1)S(1)}, u32[]{:S(2)}, u32[]{:S(2)}) collective-permute-start(bf16[8,512]{1,0:T(8,128)(2,1)S(1)} %slice.225), channel_id=1, source_target_pairs={{0,1},{1,0},{2,3},{3,2},{4,5},{5,4},{6,7},{7,6},{8,9},{9,8},{10,11... | collective-permute-start | bytes 24584 | tf_op jit(solution)/shard_map/ppermute | solution.py:140

commit v4 on v3

--- a/solution.py
+++ b/solution.py
@@ -82,11 +82,22 @@
         return blocks.reshape(experts * slots, 2 * feat)
 
     owner = lax.axis_index("expert")
-    doubling = [[(i, i ^ (1 << k)) for i in range(experts)] for k in range(experts.bit_length() - 1)]
+    digits = [(1, 2), (2, 4), (8, experts // 8)]
+
+    def digit(number, place, base):
+        return number // place % base
+
+    shifts = [
+        [
+            [(i, i + place * ((digit(i, place, base) + d) % base - digit(i, place, base))) for i in range(experts)]
+            for d in range(1, base)
+        ]
+        for place, base in digits
+    ]
     recv = exchange(send[: experts * slots])
     more = send[experts * slots :]
-    for perm in doubling:
-        more = jnp.concatenate([more, lax.ppermute(more, "expert", perm)], axis=0)
+    for perms in shifts:
+        more = jnp.concatenate([more] + [lax.ppermute(more, "expert", p) for p in perms], axis=0)
     recv = jnp.concatenate([recv, jnp.where(owner == busiest, more, jnp.zeros_like(more))], axis=0)
 
     def flip(rows_):
@@ -135,10 +146,13 @@
     back = flip(back)
     ret = exchange(back[: experts * slots])
     more = back[experts * slots :]
-    for k, perm in reversed(list(enumerate(doubling))):
-        middle = more.shape[0] // 2
-        got = lax.ppermute(more[middle:], "expert", perm)
-        more = jnp.where(((owner ^ busiest) >> k) & 1 == 1, got, more[:middle])
+    for (place, base), perms in zip(digits[::-1], shifts[::-1]):
+        parts = more.reshape(base, -1, 2 * feat)
+        behind = (digit(busiest, place, base) - digit(owner, place, base)) % base
+        more = parts[0]
+        for d in range(1, base):
+            got = lax.ppermute(parts[d], "expert", perms[base - d - 1])
+            more = jnp.where(behind == d, got, more)
     ret = jnp.concatenate([ret, more], axis=0)
     grad_gu = mm_tn(x_rows, gate_up_grad).astype(BF)
     grad_dn = mm_tn(hidden, g_rows).astype(BF)

time: 245 us -> 245 us (level); the launches traced: 241 us -> 244 us
  starting transfers between devices: 129 us -> 138 us
  waiting for transfers between devices: 91.8 us -> 82.8 us
    ppermute x10 -> x14, starting transfers between devices: 55.9 us -> 66.4 us  [the longest x7 35.7 us: on_device(): lax.ppermute(more, 'expert', p)]
    ppermute x10 -> x14, waiting for transfers between devices: 20 us -> 11.7 us  [the longest x7 7.67 us: on_device(): lax.ppermute(more, 'expert', p)]
  transfers between devices with their start and end apart: 28 -> 32, of which waited for: 19 -> 16; matrix products, arithmetic and copies ran while one was open for 3% -> 3% of each run, Pallas kernels for 0% -> 0%
where the time goes in v4:
time: 245 us; the launch traced here: 244 us
  starting transfers between devices  138 us (56%)
  waiting for transfers between devices  82.8 us (34%)
  matrix products  10.2 us (4%)
  between operations  5.08 us (2%)
  other arithmetic  4.16 us (2%)
  local copies, waits for them, and re-layouts  3.38 us (1%)
    ppermute x8, waiting for transfers between devices, all_gather(): own = jnp.concatenate([own, lax.ppermute(own, 'dp', perm)], axis=0)  35.8 us
    ppermute x7, starting transfers between devices, on_device(): lax.ppermute(more, 'expert', p)  35.7 us
    ppermute x8, waiting for transfers between devices, reduce_scatter(): keep = lax.ppermute(away, 'dp', perm).astype(F32) + keep.astype(F32)  35.2 us
    ppermute x7, starting transfers between devices, on_device(): got = lax.ppermute(parts[d], 'expert', perms[base - d - 1])  30.7 us
    ppermute x8, starting transfers between devices, reduce_scatter(): keep = lax.ppermute(away, 'dp', perm).astype(F32) + keep.astype(F32)  25.9 us
    all_to_all x2, starting transfers between devices, exchange(): lax.all_to_all(blocks, 'expert', split_axis=0, concat_axis=0, tiled=True)  23.4 us
    ppermute x8, starting transfers between devices, all_gather(): own = jnp.concatenate([own, lax.ppermute(own, 'dp', perm)], axis=0)  22.8 us
    ppermute x7, waiting for transfers between devices, on_device(): lax.ppermute(more, 'expert', p)  7.67 us
  transfers between devices with their start and end apart: 32, of which 16 were waited for; matrix products, arithmetic and copies ran while one was open for 3% of the time, Pallas kernels for 0%

profile of v4, /device:TPU:6, one launch (start us, length us, event | category | flops | bytes accessed | tf_op | source)
XLA Modules:
  0.0 244.0 jit_solution(15338223249011991525)
XLA Ops:
  3.7 1.0 convolution_convert_fusion.6
  5.8 15.7 %collective-permute-start = (bf16[8,512]{1,0:T(8,128)(2,1)S(1)}, bf16[8,512]{1,0:T(8,128)(2,1)S(1)}, u32[]{:S(2)}, u32[]{:S(2)}) collective-permute-start(bf16[8,512]{1,0:T(8,128)(2,1)S(1)} %get-tuple-element.7), channel_id=1, source_target_pairs={{0,1},{1,0},{2,3},{3,2},{4,5},{5,4},{6,7},{7,6},{8,9},{9,8},{10,11... | collective-permute-start | bytes 24584 | tf_op jit(solution)/shard_map/ppermute | solution.py:100
  22.2 7.6 %all-to-all-start = ((bf16[32,8,512]{2,1,0:T(8,128)(2,1)}), bf16[32,8,512]{2,1,0:T(8,128)(2,1)S(1)}, u32[]{:S(2)}, u32[]{:S(2)}) async-start(bf16[32,8,512]{2,1,0:T(8,128)(2,1)} %fusion.21), calls=%async_computation | async-start | bytes 524288 | tf_op jit(solution)/shard_map/all_to_all | solution.py:81
  29.9 2.1 collective-permute-start.1
  32.0 4.6 %collective-permute-start.2 = (bf16[16,512]{1,0:T(8,128)(2,1)S(1)}, bf16[16,512]{1,0:T(8,128)(2,1)S(1)}, u32[]{:S(2)}, u32[]{:S(2)}) collective-permute-start(bf16[16,512]{1,0:T(8,128)(2,1)S(1)} %pad_maximum_fusion.11), channel_id=1, source_target_pairs={{0,4},{1,5},{2,6},{3,7},{4,0},{5,1},{6,2},{7,3},{8,12},{9,13},{10,... | collective-permute-start | bytes 49160 | tf_op jit(solution)/shard_map/ppermute | solution.py:100
  36.7 1.9 collective-permute-start.3
  39.2 4.3 %collective-permute-done.3 = bf16[16,512]{1,0:T(8,128)(2,1)S(1)} collective-permute-done((bf16[16,512]{1,0:T(8,128)(2,1)S(1)}, bf16[16,512]{1,0:T(8,128)(2,1)S(1)}, u32[]{:S(2)}, u32[]{:S(2)}) %collective-permute-start.3) | collective-permute-done | bytes 16416 | tf_op jit(solution)/shard_map/ppermute | solution.py:100
  43.5 3.4 %collective-permute-start.4 = (bf16[64,512]{1,0:T(8,128)(2,1)S(1)}, bf16[64,512]{1,0:T(8,128)(2,1)S(1)}, u32[]{:S(2)}, u32[]{:S(2)}) collective-permute-start(bf16[64,512]{1,0:T(8,128)(2,1)S(1)} %get-tuple-element.20), channel_id=1, source_target_pairs={{0,8},{1,9},{2,10},{3,11},{4,12},{5,13},{6,14},{7,15},{8,16},{9,17... | collective-permute-start | bytes 196616 | tf_op jit(solution)/shard_map/ppermute | solution.py:100
  48.2 4.6 %collective-permute-start.5 = (bf16[64,512]{1,0:T(8,128)(2,1)S(1)}, bf16[64,512]{1,0:T(8,128)(2,1)S(1)}, u32[]{:S(2)}, u32[]{:S(2)}) collective-permute-start(bf16[64,512]{1,0:T(8,128)(2,1)S(1)} %get-tuple-element.20), channel_id=1, source_target_pairs={{0,16},{1,17},{2,18},{3,19},{4,20},{5,21},{6,22},{7,23},{8,24},{9,... | collective-permute-start | bytes 196616 | tf_op jit(solution)/shard_map/ppermute | solution.py:100
  52.8 3.3 %collective-permute-start.6 = (bf16[64,512]{1,0:T(8,128)(2,1)S(1)}, bf16[64,512]{1,0:T(8,128)(2,1)S(1)}, u32[]{:S(2)}, u32[]{:S(2)}) collective-permute-start(bf16[64,512]{1,0:T(8,128)(2,1)S(1)} %get-tuple-element.20), channel_id=1, source_target_pairs={{0,24},{1,25},{2,26},{3,27},{4,28},{5,29},{6,30},{7,31},{8,0},{9,1... | collective-permute-start | bytes 196616 | tf_op jit(solution)/shard_map/ppermute | solution.py:100
  56.2 2.8 %collective-permute-done.6 = bf16[64,512]{1,0:T(8,128)(2,1)S(1)} collective-permute-done((bf16[64,512]{1,0:T(8,128)(2,1)S(1)}, bf16[64,512]{1,0:T(8,128)(2,1)S(1)}, u32[]{:S(2)}, u32[]{:S(2)}) %collective-permute-start.6) | collective-permute-done | bytes 65568 | tf_op jit(solution)/shard_map/ppermute | solution.py:100
  60.0 1.9 collective-permute-start.7
  62.2 2.4 collective-permute-start.15
  65.2 2.9 %collective-permute-start.8 = (bf16[128,2048]{1,0:T(8,128)(2,1)S(1)}, bf16[128,2048]{1,0:T(8,128)(2,1)S(1)}, u32[]{:S(2)}, u32[]{:S(2)}) collective-permute-start(bf16[128,2048]{1,0:T(8,128)(2,1)S(1)} %slice.199), channel_id=1, source_target_pairs={{0,64},{32,96},{64,0},{96,32},{128,192},{160,224},{192,128},{224,1... | collective-permute-start | bytes 1572872 | tf_op jit(solution)/shard_map/ppermute | solution.py:121
  68.5 2.9 %collective-permute-start.16 = (bf16[128,1024]{1,0:T(8,128)(2,1)S(1)}, bf16[128,1024]{1,0:T(8,128)(2,1)S(1)}, u32[]{:S(2)}, u32[]{:S(2)}) collective-permute-start(bf16[128,1024]{1,0:T(8,128)(2,1)S(1)} %slice.209), channel_id=1, source_target_pairs={{0,64},{32,96},{64,0},{96,32},{128,192},{160,224},{192,128},{224,1... | collective-permute-start | bytes 786440 | tf_op jit(solution)/shard_map/ppermute | solution.py:121
  71.4 10.4 %collective-permute-done.8 = bf16[128,2048]{1,0:T(8,128)(2,1)S(1)} collective-permute-done((bf16[128,2048]{1,0:T(8,128)(2,1)S(1)}, bf16[128,2048]{1,0:T(8,128)(2,1)S(1)}, u32[]{:S(2)}, u32[]{:S(2)}) %collective-permute-start.8) | collective-permute-done | bytes 524320 | tf_op jit(solution)/shard_map/ppermute | solution.py:121
  82.0 3.4 %collective-permute-start.9 = (bf16[64,2048]{1,0:T(8,128)(2,1)S(1)}, bf16[64,2048]{1,0:T(8,128)(2,1)S(1)}, u32[]{:S(2)}, u32[]{:S(2)}) collective-permute-start(bf16[64,2048]{1,0:T(8,128)(2,1)S(1)} %slice.201), channel_id=1, source_target_pairs={{0,128},{32,160},{64,192},{96,224},{128,0},{160,32},{192,64},{224,... | collective-permute-start | bytes 786440 | tf_op jit(solution)/shard_map/ppermute | solution.py:121
  85.4 2.9 %collective-permute-done.16 = bf16[128,1024]{1,0:T(8,128)(2,1)S(1)} collective-permute-done((bf16[128,1024]{1,0:T(8,128)(2,1)S(1)}, bf16[128,1024]{1,0:T(8,128)(2,1)S(1)}, u32[]{:S(2)}, u32[]{:S(2)}) %collective-permute-start.16) | collective-permute-done | bytes 262176 | tf_op jit(solution)/shard_map/ppermute | solution.py:121
  88.4 2.6 %collective-permute-start.17 = (bf16[64,1024]{1,0:T(8,128)(2,1)S(1)}, bf16[64,1024]{1,0:T(8,128)(2,1)S(1)}, u32[]{:S(2)}, u32[]{:S(2)}) collective-permute-start(bf16[64,1024]{1,0:T(8,128)(2,1)S(1)} %slice.211), channel_id=1, source_target_pairs={{0,128},{32,160},{64,192},{96,224},{128,0},{160,32},{192,64},{224,... | collective-permute-start | bytes 393224 | tf_op jit(solution)/shard_map/ppermute | solution.py:121
  90.9 10.1 %collective-permute-done.9 = bf16[64,2048]{1,0:T(8,128)(2,1)S(1)} collective-permute-done((bf16[64,2048]{1,0:T(8,128)(2,1)S(1)}, bf16[64,2048]{1,0:T(8,128)(2,1)S(1)}, u32[]{:S(2)}, u32[]{:S(2)}) %collective-permute-start.9) | collective-permute-done | bytes 262176 | tf_op jit(solution)/shard_map/ppermute | solution.py:121
  101.2 6.5 %collective-permute-start.10 = (bf16[32,2048]{1,0:T(8,128)(2,1)S(1)}, bf16[32,2048]{1,0:T(8,128)(2,1)S(1)}, u32[]{:S(2)}, u32[]{:S(2)}) collective-permute-start(bf16[32,2048]{1,0:T(8,128)(2,1)S(1)} %slice.203), channel_id=1, source_target_pairs={{0,256},{32,288},{64,320},{96,352},{128,384},{160,416},{192,448},{... | collective-permute-start | bytes 393224 | tf_op jit(solution)/shard_map/ppermute | solution.py:121
  107.7 3.3 %collective-permute-start.18 = (bf16[32,1024]{1,0:T(8,128)(2,1)S(1)}, bf16[32,1024]{1,0:T(8,128)(2,1)S(1)}, u32[]{:S(2)}, u32[]{:S(2)}) collective-permute-start(bf16[32,1024]{1,0:T(8,128)(2,1)S(1)} %slice.213), channel_id=1, source_target_pairs={{0,256},{32,288},{64,320},{96,352},{128,384},{160,416},{192,448},{... | collective-permute-start | bytes 196616 | tf_op jit(solution)/shard_map/ppermute | solution.py:121
  111.0 11.0 %collective-permute-done.10 = bf16[32,2048]{1,0:T(8,128)(2,1)S(1)} collective-permute-done((bf16[32,2048]{1,0:T(8,128)(2,1)S(1)}, bf16[32,2048]{1,0:T(8,128)(2,1)S(1)}, u32[]{:S(2)}, u32[]{:S(2)}) %collective-permute-start.10) | collective-permute-done | bytes 131104 | tf_op jit(solution)/shard_map/ppermute | solution.py:121
  122.9 1.9 collective-permute-start.19
  124.8 11.5 %collective-permute-done.19 = bf16[32,2048]{1,0:T(8,128)(2,1)S(1)} collective-permute-done((bf16[32,2048]{1,0:T(8,128)(2,1)S(1)}, bf16[32,2048]{1,0:T(8,128)(2,1)S(1)}, u32[]{:S(2)}, u32[]{:S(2)}) %collective-permute-start.19) | collective-permute-done | bytes 131104 | tf_op jit(solution)/shard_map/ppermute | solution.py:129
  136.4 1.9 collective-permute-start.20
  138.3 3.9 %collective-permute-start.11 = (bf16[32,1024]{1,0:T(8,128)(2,1)S(1)}, bf16[32,1024]{1,0:T(8,128)(2,1)S(1)}, u32[]{:S(2)}, u32[]{:S(2)}) collective-permute-start(bf16[32,1024]{1,0:T(8,128)(2,1)S(1)} %get-tuple-element.5), channel_id=1, source_target_pairs={{0,256},{32,288},{64,320},{96,352},{128,384},{160,416},{192,448},{... | collective-permute-start | bytes 196616 | tf_op jit(solution)/shard_map/ppermute | solution.py:129
  142.2 6.5 %collective-permute-done.11 = bf16[32,1024]{1,0:T(8,128)(2,1)S(1)} collective-permute-done((bf16[32,1024]{1,0:T(8,128)(2,1)S(1)}, bf16[32,1024]{1,0:T(8,128)(2,1)S(1)}, u32[]{:S(2)}, u32[]{:S(2)}) %collective-permute-start.11) | collective-permute-done | bytes 65568 | tf_op jit(solution)/shard_map/ppermute | solution.py:129
  148.8 7.4 %collective-permute-start.12 = (bf16[64,1024]{1,0:T(8,128)(2,1)S(1)}, bf16[64,1024]{1,0:T(8,128)(2,1)S(1)}, u32[]{:S(2)}, u32[]{:S(2)}) collective-permute-start(bf16[64,1024]{1,0:T(8,128)(2,1)S(1)} %pad_maximum_fusion.9), channel_id=1, source_target_pairs={{0,128},{32,160},{64,192},{96,224},{128,0},{160,32},{192,64},{224,... | collective-permute-start | bytes 393224 | tf_op jit(solution)/shard_map/ppermute | solution.py:129
  156.2 1.9 collective-permute-start.21
  158.2 3.5 %collective-permute-done.12 = bf16[64,1024]{1,0:T(8,128)(2,1)S(1)} collective-permute-done((bf16[64,1024]{1,0:T(8,128)(2,1)S(1)}, bf16[64,1024]{1,0:T(8,128)(2,1)S(1)}, u32[]{:S(2)}, u32[]{:S(2)}) %collective-permute-start.12) | collective-permute-done | bytes 131104 | tf_op jit(solution)/shard_map/ppermute | solution.py:129
  161.6 1.9 collective-permute-start.13
  163.6 9.4 %collective-permute-done.21 = bf16[128,2048]{1,0:T(8,128)(2,1)S(1)} collective-permute-done((bf16[128,2048]{1,0:T(8,128)(2,1)S(1)}, bf16[128,2048]{1,0:T(8,128)(2,1)S(1)}, u32[]{:S(2)}, u32[]{:S(2)}) %collective-permute-start.21) | collective-permute-done | bytes 524320 | tf_op jit(solution)/shard_map/ppermute | solution.py:129
  173.1 1.9 collective-permute-start.22
  175.0 3.2 %collective-permute-done.13 = bf16[128,1024]{1,0:T(8,128)(2,1)S(1)} collective-permute-done((bf16[128,1024]{1,0:T(8,128)(2,1)S(1)}, bf16[128,1024]{1,0:T(8,128)(2,1)S(1)}, u32[]{:S(2)}, u32[]{:S(2)}) %collective-permute-start.13) | collective-permute-done | bytes 262176 | tf_op jit(solution)/shard_map/ppermute | solution.py:129
  178.2 1.9 collective-permute-start.14
  180.2 1.8 collective-permute-done.14
  185.5 1.9 collective-permute-start.23
  187.4 6.0 %collective-permute-start.24 = (bf16[64,512]{1,0:T(8,128)(2,1)S(1)}, bf16[64,512]{1,0:T(8,128)(2,1)S(1)}, u32[]{:S(2)}, u32[]{:S(2)}) collective-permute-start(bf16[64,512]{1,0:T(8,128)(2,1)S(1)} %get-tuple-element.13), channel_id=1, source_target_pairs={{0,16},{1,17},{2,18},{3,19},{4,20},{5,21},{6,22},{7,23},{8,24},{9,... | collective-permute-start | bytes 196616 | tf_op jit(solution)/shard_map/ppermute | solution.py:154
  193.4 1.9 collective-permute-start.25
  198.1 15.8 %all-to-all-start.1 = ((bf16[32,8,512]{2,1,0:T(8,128)(2,1)}), bf16[32,8,512]{2,1,0:T(8,128)(2,1)S(1)}, u32[]{:S(2)}, u32[]{:S(2)}) async-start(bf16[32,8,512]{2,1,0:T(8,128)(2,1)} %bitcast.17), calls=%async_computation.1 | async-start | bytes 524288 | tf_op jit(solution)/shard_map/all_to_all | solution.py:81
  214.0 2.3 collective-permute-start.26
  216.3 4.6 %collective-permute-start.27 = (bf16[16,512]{1,0:T(8,128)(2,1)S(1)}, bf16[16,512]{1,0:T(8,128)(2,1)S(1)}, u32[]{:S(2)}, u32[]{:S(2)}) collective-permute-start(bf16[16,512]{1,0:T(8,128)(2,1)S(1)} %get-tuple-element.18), channel_id=1, source_target_pairs={{0,4},{1,5},{2,6},{3,7},{4,0},{5,1},{6,2},{7,3},{8,12},{9,13},{10,... | collective-permute-start | bytes 49160 | tf_op jit(solution)/shard_map/ppermute | solution.py:154
  220.9 1.9 collective-permute-start.28
  222.8 1.3 fusion.1
  224.1 3.6 %collective-permute-done.28 = bf16[16,512]{1,0:T(8,128)(2,1)S(1)} collective-permute-done((bf16[16,512]{1,0:T(8,128)(2,1)S(1)}, bf16[16,512]{1,0:T(8,128)(2,1)S(1)}, u32[]{:S(2)}, u32[]{:S(2)}) %collective-permute-start.28) | collective-permute-done | bytes 16416 | tf_op jit(solution)/shard_map/ppermute | solution.py:154
  227.7 12.1 %collective-permute-start.29 = (bf16[8,512]{1,0:T(8,128)(2,1)S(1)}, bf16[8,512]{1,0:T(8,128)(2,1)S(1)}, u32[]{:S(2)}, u32[]{:S(2)}) collective-permute-start(bf16[8,512]{1,0:T(8,128)(2,1)S(1)} %slice.225), channel_id=1, source_target_pairs={{0,1},{1,0},{2,3},{3,2},{4,5},{5,4},{6,7},{7,6},{8,9},{9,8},{10,11... | collective-permute-start | bytes 24584 | tf_op jit(solution)/shard_map/ppermute | solution.py:154
  239.8 1.7 fusion
  (112 shorter events, 15.5 us)
Async XLA Ops:
  0.6 58.9 %copy-start = (bf16[1,256,2048]{2,1,0:T(8,128)(2,1)S(1)}, bf16[1,256,2048]{2,1,0:T(8,128)(2,1)}, u32[]{:S(2)}) copy-start(bf16[1,256,2048]{2,1,0:T(8,128)(2,1)} %param.10) | copy-start | bytes 3145732
  5.8 24.1 %collective-permute-start = (bf16[8,512]{1,0:T(8,128)(2,1)S(1)}, bf16[8,512]{1,0:T(8,128)(2,1)S(1)}, u32[]{:S(2)}, u32[]{:S(2)}) collective-permute-start(bf16[8,512]{1,0:T(8,128)(2,1)S(1)} %get-tuple-element.7), channel_id=1, source_target_pairs={{0,1},{1,0},{2,3},{3,2},{4,5},{5,4},{6,7},{7,6},{8,9},{9,8},{10,11... | collective-permute-start | bytes 24584 | tf_op jit(solution)/shard_map/ppermute | solution.py:100
  22.2 36.8 %all-to-all-start = ((bf16[32,8,512]{2,1,0:T(8,128)(2,1)}), bf16[32,8,512]{2,1,0:T(8,128)(2,1)S(1)}, u32[]{:S(2)}, u32[]{:S(2)}) async-start(bf16[32,8,512]{2,1,0:T(8,128)(2,1)} %fusion.21), calls=%async_computation | async-start | bytes 524288 | tf_op jit(solution)/shard_map/all_to_all | solution.py:81
  29.9 8.7 %collective-permute-start.1 = (bf16[16,512]{1,0:T(8,128)(2,1)S(1)}, bf16[16,512]{1,0:T(8,128)(2,1)S(1)}, u32[]{:S(2)}, u32[]{:S(2)}) collective-permute-start(bf16[16,512]{1,0:T(8,128)(2,1)S(1)} %pad_maximum_fusion.11), channel_id=1, source_target_pairs={{0,2},{1,3},{2,4},{3,5},{4,6},{5,7},{6,0},{7,1},{8,10},{9,11},{10,... | collective-permute-start | bytes 49160 | tf_op jit(solution)/shard_map/ppermute | solution.py:100
  32.0 7.1 %collective-permute-start.2 = (bf16[16,512]{1,0:T(8,128)(2,1)S(1)}, bf16[16,512]{1,0:T(8,128)(2,1)S(1)}, u32[]{:S(2)}, u32[]{:S(2)}) collective-permute-start(bf16[16,512]{1,0:T(8,128)(2,1)S(1)} %pad_maximum_fusion.11), channel_id=1, source_target_pairs={{0,4},{1,5},{2,6},{3,7},{4,0},{5,1},{6,2},{7,3},{8,12},{9,13},{10,... | collective-permute-start | bytes 49160 | tf_op jit(solution)/shard_map/ppermute | solution.py:100
  36.7 6.8 %collective-permute-start.3 = (bf16[16,512]{1,0:T(8,128)(2,1)S(1)}, bf16[16,512]{1,0:T(8,128)(2,1)S(1)}, u32[]{:S(2)}, u32[]{:S(2)}) collective-permute-start(bf16[16,512]{1,0:T(8,128)(2,1)S(1)} %pad_maximum_fusion.11), channel_id=1, source_target_pairs={{0,6},{1,7},{2,0},{3,1},{4,2},{5,3},{6,4},{7,5},{8,14},{9,15},{10,... | collective-permute-start | bytes 49160 | tf_op jit(solution)/shard_map/ppermute | solution.py:100
  43.5 12.6 %collective-permute-start.4 = (bf16[64,512]{1,0:T(8,128)(2,1)S(1)}, bf16[64,512]{1,0:T(8,128)(2,1)S(1)}, u32[]{:S(2)}, u32[]{:S(2)}) collective-permute-start(bf16[64,512]{1,0:T(8,128)(2,1)S(1)} %get-tuple-element.20), channel_id=1, source_target_pairs={{0,8},{1,9},{2,10},{3,11},{4,12},{5,13},{6,14},{7,15},{8,16},{9,17... | collective-permute-start | bytes 196616 | tf_op jit(solution)/shard_map/ppermute | solution.py:100
  48.2 8.0 %collective-permute-start.5 = (bf16[64,512]{1,0:T(8,128)(2,1)S(1)}, bf16[64,512]{1,0:T(8,128)(2,1)S(1)}, u32[]{:S(2)}, u32[]{:S(2)}) collective-permute-start(bf16[64,512]{1,0:T(8,128)(2,1)S(1)} %get-tuple-element.20), channel_id=1, source_target_pairs={{0,16},{1,17},{2,18},{3,19},{4,20},{5,21},{6,22},{7,23},{8,24},{9,... | collective-permute-start | bytes 196616 | tf_op jit(solution)/shard_map/ppermute | solution.py:100
  52.8 6.2 %collective-permute-start.6 = (bf16[64,512]{1,0:T(8,128)(2,1)S(1)}, bf16[64,512]{1,0:T(8,128)(2,1)S(1)}, u32[]{:S(2)}, u32[]{:S(2)}) collective-permute-start(bf16[64,512]{1,0:T(8,128)(2,1)S(1)} %get-tuple-element.20), channel_id=1, source_target_pairs={{0,24},{1,25},{2,26},{3,27},{4,28},{5,29},{6,30},{7,31},{8,0},{9,1... | collective-permute-start | bytes 196616 | tf_op jit(solution)/shard_map/ppermute | solution.py:100
  59.3 2.6 %copy-start.1 = (bf16[1,1024,256]{2,1,0:T(8,128)(2,1)S(1)}, bf16[1,1024,256]{2,1,0:T(8,128)(2,1)}, u32[]{:S(2)}) copy-start(bf16[1,1024,256]{2,1,0:T(8,128)(2,1)} %param.11) | copy-start | bytes 1572868
  60.0 4.7 %collective-permute-start.7 = (bf16[256,2048]{1,0:T(8,128)(2,1)S(1)}, bf16[256,2048]{1,0:T(8,128)(2,1)S(1)}, u32[]{:S(2)}, u32[]{:S(2)}) collective-permute-start(bf16[256,2048]{1,0:T(8,128)(2,1)S(1)} %convolution_convert_fusion.1), channel_id=1, source_target_pairs={{0,32},{32,0},{64,96},{96,64},{128,160},{160,128},{192,224},{224,1... | collective-permute-start | bytes 3145736 | tf_op jit(solution)/shard_map/ppermute | solution.py:121
  62.2 5.9 %collective-permute-start.15 = (bf16[256,1024]{1,0:T(8,128)(2,1)S(1)}, bf16[256,1024]{1,0:T(8,128)(2,1)S(1)}, u32[]{:S(2)}, u32[]{:S(2)}) collective-permute-start(bf16[256,1024]{1,0:T(8,128)(2,1)S(1)} %convolution_convert_fusion.3), channel_id=1, source_target_pairs={{0,32},{32,0},{64,96},{96,64},{128,160},{160,128},{192,224},{224,1... | collective-permute-start | bytes 1572872 | tf_op jit(solution)/shard_map/ppermute | solution.py:121
  65.2 16.7 %collective-permute-start.8 = (bf16[128,2048]{1,0:T(8,128)(2,1)S(1)}, bf16[128,2048]{1,0:T(8,128)(2,1)S(1)}, u32[]{:S(2)}, u32[]{:S(2)}) collective-permute-start(bf16[128,2048]{1,0:T(8,128)(2,1)S(1)} %slice.199), channel_id=1, source_target_pairs={{0,64},{32,96},{64,0},{96,32},{128,192},{160,224},{192,128},{224,1... | collective-permute-start | bytes 1572872 | tf_op jit(solution)/shard_map/ppermute | solution.py:121
  68.5 19.8 %collective-permute-start.16 = (bf16[128,1024]{1,0:T(8,128)(2,1)S(1)}, bf16[128,1024]{1,0:T(8,128)(2,1)S(1)}, u32[]{:S(2)}, u32[]{:S(2)}) collective-permute-start(bf16[128,1024]{1,0:T(8,128)(2,1)S(1)} %slice.209), channel_id=1, source_target_pairs={{0,64},{32,96},{64,0},{96,32},{128,192},{160,224},{192,128},{224,1... | collective-permute-start | bytes 786440 | tf_op jit(solution)/shard_map/ppermute | solution.py:121
  82.0 19.1 %collective-permute-start.9 = (bf16[64,2048]{1,0:T(8,128)(2,1)S(1)}, bf16[64,2048]{1,0:T(8,128)(2,1)S(1)}, u32[]{:S(2)}, u32[]{:S(2)}) collective-permute-start(bf16[64,2048]{1,0:T(8,128)(2,1)S(1)} %slice.201), channel_id=1, source_target_pairs={{0,128},{32,160},{64,192},{96,224},{128,0},{160,32},{192,64},{224,... | collective-permute-start | bytes 786440 | tf_op jit(solution)/shard_map/ppermute | solution.py:121
  88.4 19.3 %collective-permute-start.17 = (bf16[64,1024]{1,0:T(8,128)(2,1)S(1)}, bf16[64,1024]{1,0:T(8,128)(2,1)S(1)}, u32[]{:S(2)}, u32[]{:S(2)}) collective-permute-start(bf16[64,1024]{1,0:T(8,128)(2,1)S(1)} %slice.211), channel_id=1, source_target_pairs={{0,128},{32,160},{64,192},{96,224},{128,0},{160,32},{192,64},{224,... | collective-permute-start | bytes 393224 | tf_op jit(solution)/shard_map/ppermute | solution.py:121
  101.2 20.9 %collective-permute-start.10 = (bf16[32,2048]{1,0:T(8,128)(2,1)S(1)}, bf16[32,2048]{1,0:T(8,128)(2,1)S(1)}, u32[]{:S(2)}, u32[]{:S(2)}) collective-permute-start(bf16[32,2048]{1,0:T(8,128)(2,1)S(1)} %slice.203), channel_id=1, source_target_pairs={{0,256},{32,288},{64,320},{96,352},{128,384},{160,416},{192,448},{... | collective-permute-start | bytes 393224 | tf_op jit(solution)/shard_map/ppermute | solution.py:121
  107.7 15.0 %collective-permute-start.18 = (bf16[32,1024]{1,0:T(8,128)(2,1)S(1)}, bf16[32,1024]{1,0:T(8,128)(2,1)S(1)}, u32[]{:S(2)}, u32[]{:S(2)}) collective-permute-start(bf16[32,1024]{1,0:T(8,128)(2,1)S(1)} %slice.213), channel_id=1, source_target_pairs={{0,256},{32,288},{64,320},{96,352},{128,384},{160,416},{192,448},{... | collective-permute-start | bytes 196616 | tf_op jit(solution)/shard_map/ppermute | solution.py:121
  122.9 13.5 %collective-permute-start.19 = (bf16[32,2048]{1,0:T(8,128)(2,1)S(1)}, bf16[32,2048]{1,0:T(8,128)(2,1)S(1)}, u32[]{:S(2)}, u32[]{:S(2)}) collective-permute-start(bf16[32,2048]{1,0:T(8,128)(2,1)S(1)} %get-tuple-element.15), channel_id=1, source_target_pairs={{0,256},{32,288},{64,320},{96,352},{128,384},{160,416},{192,448},{... | collective-permute-start | bytes 393224 | tf_op jit(solution)/shard_map/ppermute | solution.py:129
  136.4 19.8 %collective-permute-start.20 = (bf16[64,2048]{1,0:T(8,128)(2,1)S(1)}, bf16[64,2048]{1,0:T(8,128)(2,1)S(1)}, u32[]{:S(2)}, u32[]{:S(2)}) collective-permute-start(bf16[64,2048]{1,0:T(8,128)(2,1)S(1)} %pad_maximum_fusion.6), channel_id=1, source_target_pairs={{0,128},{32,160},{64,192},{96,224},{128,0},{160,32},{192,64},{224,... | collective-permute-start | bytes 786440 | tf_op jit(solution)/shard_map/ppermute | solution.py:129
  138.3 10.4 %collective-permute-start.11 = (bf16[32,1024]{1,0:T(8,128)(2,1)S(1)}, bf16[32,1024]{1,0:T(8,128)(2,1)S(1)}, u32[]{:S(2)}, u32[]{:S(2)}) collective-permute-start(bf16[32,1024]{1,0:T(8,128)(2,1)S(1)} %get-tuple-element.5), channel_id=1, source_target_pairs={{0,256},{32,288},{64,320},{96,352},{128,384},{160,416},{192,448},{... | collective-permute-start | bytes 196616 | tf_op jit(solution)/shard_map/ppermute | solution.py:129
  148.8 12.8 %collective-permute-start.12 = (bf16[64,1024]{1,0:T(8,128)(2,1)S(1)}, bf16[64,1024]{1,0:T(8,128)(2,1)S(1)}, u32[]{:S(2)}, u32[]{:S(2)}) collective-permute-start(bf16[64,1024]{1,0:T(8,128)(2,1)S(1)} %pad_maximum_fusion.9), channel_id=1, source_target_pairs={{0,128},{32,160},{64,192},{96,224},{128,0},{160,32},{192,64},{224,... | collective-permute-start | bytes 393224 | tf_op jit(solution)/shard_map/ppermute | solution.py:129
  156.2 16.8 %collective-permute-start.21 = (bf16[128,2048]{1,0:T(8,128)(2,1)S(1)}, bf16[128,2048]{1,0:T(8,128)(2,1)S(1)}, u32[]{:S(2)}, u32[]{:S(2)}) collective-permute-start(bf16[128,2048]{1,0:T(8,128)(2,1)S(1)} %pad_maximum_fusion.3), channel_id=1, source_target_pairs={{0,64},{32,96},{64,0},{96,32},{128,192},{160,224},{192,128},{224,1... | collective-permute-start | bytes 1572872 | tf_op jit(solution)/shard_map/ppermute | solution.py:129
  161.6 16.5 %collective-permute-start.13 = (bf16[128,1024]{1,0:T(8,128)(2,1)S(1)}, bf16[128,1024]{1,0:T(8,128)(2,1)S(1)}, u32[]{:S(2)}, u32[]{:S(2)}) collective-permute-start(bf16[128,1024]{1,0:T(8,128)(2,1)S(1)} %pad_maximum_fusion.5), channel_id=1, source_target_pairs={{0,64},{32,96},{64,0},{96,32},{128,192},{160,224},{192,128},{224,1... | collective-permute-start | bytes 786440 | tf_op jit(solution)/shard_map/ppermute | solution.py:129
  173.1 9.5 %collective-permute-start.22 = (bf16[256,2048]{1,0:T(8,128)(2,1)S(1)}, bf16[256,2048]{1,0:T(8,128)(2,1)S(1)}, u32[]{:S(2)}, u32[]{:S(2)}) collective-permute-start(bf16[256,2048]{1,0:T(8,128)(2,1)S(1)} %pad_maximum_fusion), channel_id=1, source_target_pairs={{0,32},{32,0},{64,96},{96,64},{128,160},{160,128},{192,224},{224,1... | collective-permute-start | bytes 3145736 | tf_op jit(solution)/shard_map/ppermute | solution.py:129
  178.2 3.8 %collective-permute-start.14 = (bf16[256,1024]{1,0:T(8,128)(2,1)S(1)}, bf16[256,1024]{1,0:T(8,128)(2,1)S(1)}, u32[]{:S(2)}, u32[]{:S(2)}) collective-permute-start(bf16[256,1024]{1,0:T(8,128)(2,1)S(1)} %pad_maximum_fusion.2), channel_id=1, source_target_pairs={{0,32},{32,0},{64,96},{96,64},{128,160},{160,128},{192,224},{224,1... | collective-permute-start | bytes 1572872 | tf_op jit(solution)/shard_map/ppermute | solution.py:129
  182.0 1.5 copy-start.4
  182.7 1.3 copy-start.2
  184.4 10.9 %copy-start.6 = (f32[128,2]{0,1:T(2,128)S(1)}, f32[128,2]{0,1:T(2,128)}, u32[]{:S(2)}) copy-start(f32[128,2]{0,1:T(2,128)} %param.8) | copy-start | bytes 3076
  184.6 38.2 %copy-start.5 = (bf16[512,1024]{1,0:T(8,128)(2,1)S(1)}, bf16[512,1024]{1,0:T(8,128)(2,1)}, u32[]{:S(2)}) copy-start(bf16[512,1024]{1,0:T(8,128)(2,1)} %copy-done.4) | copy-start | bytes 3145732
  185.5 28.5 %collective-permute-start.23 = (bf16[64,512]{1,0:T(8,128)(2,1)S(1)}, bf16[64,512]{1,0:T(8,128)(2,1)S(1)}, u32[]{:S(2)}, u32[]{:S(2)}) collective-permute-start(bf16[64,512]{1,0:T(8,128)(2,1)S(1)} %get-tuple-element.14), channel_id=1, source_target_pairs={{0,8},{1,9},{2,10},{3,11},{4,12},{5,13},{6,14},{7,15},{8,16},{9,17... | collective-permute-start | bytes 196616 | tf_op jit(solution)/shard_map/ppermute | solution.py:154
  187.4 26.5 %collective-permute-start.24 = (bf16[64,512]{1,0:T(8,128)(2,1)S(1)}, bf16[64,512]{1,0:T(8,128)(2,1)S(1)}, u32[]{:S(2)}, u32[]{:S(2)}) collective-permute-start(bf16[64,512]{1,0:T(8,128)(2,1)S(1)} %get-tuple-element.13), channel_id=1, source_target_pairs={{0,16},{1,17},{2,18},{3,19},{4,20},{5,21},{6,22},{7,23},{8,24},{9,... | collective-permute-start | bytes 196616 | tf_op jit(solution)/shard_map/ppermute | solution.py:154
  193.4 20.6 %collective-permute-start.25 = (bf16[64,512]{1,0:T(8,128)(2,1)S(1)}, bf16[64,512]{1,0:T(8,128)(2,1)S(1)}, u32[]{:S(2)}, u32[]{:S(2)}) collective-permute-start(bf16[64,512]{1,0:T(8,128)(2,1)S(1)} %get-tuple-element.12), channel_id=1, source_target_pairs={{0,24},{1,25},{2,26},{3,27},{4,28},{5,29},{6,30},{7,31},{8,0},{9,1... | collective-permute-start | bytes 196616 | tf_op jit(solution)/shard_map/ppermute | solution.py:154
  198.1 43.9 %all-to-all-start.1 = ((bf16[32,8,512]{2,1,0:T(8,128)(2,1)}), bf16[32,8,512]{2,1,0:T(8,128)(2,1)S(1)}, u32[]{:S(2)}, u32[]{:S(2)}) async-start(bf16[32,8,512]{2,1,0:T(8,128)(2,1)} %bitcast.17), calls=%async_computation.1 | async-start | bytes 524288 | tf_op jit(solution)/shard_map/all_to_all | solution.py:81
  213.9 25.9 %copy-start.3 = (bf16[512,2048]{1,0:T(8,128)(2,1)S(1)}, bf16[512,2048]{1,0:T(8,128)(2,1)}, u32[]{:S(2)}) copy-start(bf16[512,2048]{1,0:T(8,128)(2,1)} %copy-done.2) | copy-start | bytes 6291460
  214.0 10.1 %collective-permute-start.26 = (bf16[16,512]{1,0:T(8,128)(2,1)S(1)}, bf16[16,512]{1,0:T(8,128)(2,1)S(1)}, u32[]{:S(2)}, u32[]{:S(2)}) collective-permute-start(bf16[16,512]{1,0:T(8,128)(2,1)S(1)} %get-tuple-element.19), channel_id=1, source_target_pairs={{0,2},{1,3},{2,4},{3,5},{4,6},{5,7},{6,0},{7,1},{8,10},{9,11},{10,... | collective-permute-start | bytes 49160 | tf_op jit(solution)/shard_map/ppermute | solution.py:154
  216.3 7.8 %collective-permute-start.27 = (bf16[16,512]{1,0:T(8,128)(2,1)S(1)}, bf16[16,512]{1,0:T(8,128)(2,1)S(1)}, u32[]{:S(2)}, u32[]{:S(2)}) collective-permute-start(bf16[16,512]{1,0:T(8,128)(2,1)S(1)} %get-tuple-element.18), channel_id=1, source_target_pairs={{0,4},{1,5},{2,6},{3,7},{4,0},{5,1},{6,2},{7,3},{8,12},{9,13},{10,... | collective-permute-start | bytes 49160 | tf_op jit(solution)/shard_map/ppermute | solution.py:154
  220.9 6.8 %collective-permute-start.28 = (bf16[16,512]{1,0:T(8,128)(2,1)S(1)}, bf16[16,512]{1,0:T(8,128)(2,1)S(1)}, u32[]{:S(2)}, u32[]{:S(2)}) collective-permute-start(bf16[16,512]{1,0:T(8,128)(2,1)S(1)} %get-tuple-element.17), channel_id=1, source_target_pairs={{0,6},{1,7},{2,0},{3,1},{4,2},{5,3},{6,4},{7,5},{8,14},{9,15},{10,... | collective-permute-start | bytes 49160 | tf_op jit(solution)/shard_map/ppermute | solution.py:154
  227.7 14.3 %collective-permute-start.29 = (bf16[8,512]{1,0:T(8,128)(2,1)S(1)}, bf16[8,512]{1,0:T(8,128)(2,1)S(1)}, u32[]{:S(2)}, u32[]{:S(2)}) collective-permute-start(bf16[8,512]{1,0:T(8,128)(2,1)S(1)} %slice.225), channel_id=1, source_target_pairs={{0,1},{1,0},{2,3},{3,2},{4,5},{5,4},{6,7},{7,6},{8,9},{9,8},{10,11... | collective-permute-start | bytes 24584 | tf_op jit(solution)/shard_map/ppermute | solution.py:154

commit v5 on v2

--- a/solution.py
+++ b/solution.py
@@ -98,24 +98,27 @@
             own = jnp.concatenate([own, lax.ppermute(own, "dp", perm)], axis=0)
         return own
 
-    gate_up = reduce_scatter(mm, x_rows, gu)
+    gu_gate, gu_up = gu[:, :width], gu[:, width:]
+    gate = reduce_scatter(mm, x_rows, gu_gate)
+    up = reduce_scatter(mm, x_rows, gu_up)
     hidden_grad = reduce_scatter(mm_nt, g_rows, down)
-    gate = gate_up[:, :width]
-    up = gate_up[:, width:]
     sig = jax.nn.sigmoid(gate)
     silu_vals = gate * sig
     hidden = all_gather((silu_vals * up).astype(BF))
-    dgate = hidden_grad * up * sig * (1.0 + gate * (1.0 - sig))
-    dup = hidden_grad * silu_vals
-    gate_up_grad = all_gather(jnp.concatenate([dgate, dup], axis=1).astype(BF))
+    dup = all_gather((hidden_grad * silu_vals).astype(BF))
+    dgate = all_gather((hidden_grad * up * sig * (1.0 + gate * (1.0 - sig))).astype(BF))
 
     back = jnp.concatenate(
-        [mm(hidden, down).astype(BF), mm_nt(gate_up_grad, gu).astype(BF)], axis=1
+        [
+            mm(hidden, down).astype(BF),
+            (mm_nt(dgate, gu_gate) + mm_nt(dup, gu_up)).astype(BF),
+        ],
+        axis=1,
     )
     back = flip(back).reshape(experts, slots, 2 * feat)
     ret = lax.all_to_all(back, "expert", split_axis=0, concat_axis=0, tiled=True)
     ret = ret.reshape(rows, 2 * feat)
-    grad_gu = mm_tn(x_rows, gate_up_grad).astype(BF)
+    grad_gu = mm_tn(x_rows, jnp.concatenate([dgate, dup], axis=1)).astype(BF)
     grad_dn = mm_tn(hidden, g_rows).astype(BF)
 
     mixed = sum(

time: 232 us -> 230 us (level)
  the two profiles are of different devices: /device:TPU:33 before, /device:TPU:193 now
where the time goes in v5:
time: 230 us; the launch traced here: 229 us
  starting transfers between devices  111 us (48%)
  waiting for transfers between devices  93.3 us (41%)
  matrix products  13.7 us (6%)
  local copies, waits for them, and re-layouts  5.94 us (3%)
  other arithmetic  3.43 us (1%)
    ppermute x12, starting transfers between devices, all_gather(): own = jnp.concatenate([own, lax.ppermute(own, 'dp', perm)], axis=0)  54.9 us
    ppermute x12, starting transfers between devices, reduce_scatter(): keep = lax.ppermute(away, 'dp', perm).astype(F32) + keep.astype(F32)  37.9 us
    all_to_all x1, waiting for transfers between devices, on_device(): lax.all_to_all(send, 'expert', split_axis=0, concat_axis=0, tiled=True)  36.9 us
    all_to_all x1, waiting for transfers between devices, on_device(): lax.all_to_all(back, 'expert', split_axis=0, concat_axis=0, tiled=True)  32.9 us
    all_to_all x1, starting transfers between devices, on_device(): lax.all_to_all(send, 'expert', split_axis=0, concat_axis=0, tiled=True)  13.7 us
    ppermute x12, waiting for transfers between devices, reduce_scatter(): keep = lax.ppermute(away, 'dp', perm).astype(F32) + keep.astype(F32)  12.7 us
    ppermute x12, waiting for transfers between devices, all_gather(): own = jnp.concatenate([own, lax.ppermute(own, 'dp', perm)], axis=0)  10.9 us
    dot_general x5, matrix products, mm_tn(): lax.dot_general(a, b, (((0,), (0,)), ((), ())), preferred_element_type=F32)  7.88 us
  transfers between devices with their start and end apart: 26, of which 11 were waited for; matrix products, arithmetic and copies ran while one was open for 3% of the time, Pallas kernels for 0%

profile of v5, /device:TPU:193, one launch (start us, length us, event | category | flops | bytes accessed | tf_op | source)
XLA Modules:
  0.0 229.1 jit_solution(2686424741266960270)
XLA Ops:
  1.7 0.8 slice_bitcast_fusion.2
  2.6 0.8 fusion.60
  3.4 1.1 convolution_convert_fusion.6
  4.7 1.1 fusion.6
  5.8 1.0 copy.12
  6.9 13.7 %all-to-all-start = ((bf16[32,16,512]{2,1,0:T(8,128)(2,1)}), bf16[32,16,512]{2,1,0:T(8,128)(2,1)S(1)}, u32[]{:S(2)}, u32[]{:S(2)}) async-start(bf16[32,16,512]{2,1,0:T(8,128)(2,1)} %bitcast.10), calls=%async_computation | async-start | bytes 1048576 | tf_op jit(solution)/shard_map/all_to_all | solution.py:70
  20.6 36.9 %all-to-all-done = bf16[32,16,512]{2,1,0:T(8,128)(2,1)S(1)} async-done(((bf16[32,16,512]{2,1,0:T(8,128)(2,1)}), bf16[32,16,512]{2,1,0:T(8,128)(2,1)S(1)}, u32[]{:S(2)}, u32[]{:S(2)}) %all-to-all-start) | async-done | bytes 524320 | tf_op jit(solution)/shard_map/all_to_all | solution.py:70
  58.0 1.0 copy-done.1
  59.3 3.6 %collective-permute-start.4 = (bf16[256,1024]{1,0:T(8,128)(2,1)S(1)}, bf16[256,1024]{1,0:T(8,128)(2,1)S(1)}, u32[]{:S(2)}, u32[]{:S(2)}) collective-permute-start(bf16[256,1024]{1,0:T(8,128)(2,1)S(1)} %convolution_convert_fusion.3), channel_id=1, source_target_pairs={{0,32},{32,0},{64,96},{96,64},{128,160},{160,128},{192,224},{224,1... | collective-permute-start | bytes 1572872 | tf_op jit(solution)/shard_map/ppermute | solution.py:90
  63.3 1.9 collective-permute-start
  65.5 2.4 %collective-permute-start.12 = (bf16[256,1024]{1,0:T(8,128)(2,1)S(1)}, bf16[256,1024]{1,0:T(8,128)(2,1)S(1)}, u32[]{:S(2)}, u32[]{:S(2)}) collective-permute-start(bf16[256,1024]{1,0:T(8,128)(2,1)S(1)} %convolution_convert_fusion.2), channel_id=1, source_target_pairs={{0,32},{32,0},{64,96},{96,64},{128,160},{160,128},{192,224},{224,1... | collective-permute-start | bytes 1572872 | tf_op jit(solution)/shard_map/ppermute | solution.py:90
  68.3 1.9 collective-permute-start.5
  70.6 3.4 %collective-permute-start.1 = (bf16[128,1024]{1,0:T(8,128)(2,1)S(1)}, bf16[128,1024]{1,0:T(8,128)(2,1)S(1)}, u32[]{:S(2)}, u32[]{:S(2)}) collective-permute-start(bf16[128,1024]{1,0:T(8,128)(2,1)S(1)} %slice.166), channel_id=1, source_target_pairs={{0,64},{32,96},{64,0},{96,32},{128,192},{160,224},{192,128},{224,1... | collective-permute-start | bytes 786440 | tf_op jit(solution)/shard_map/ppermute | solution.py:90
  74.3 1.9 collective-permute-start.13
  76.3 1.9 collective-permute-done.5
  78.2 1.9 collective-permute-start.6
  80.2 3.6 %collective-permute-done.1 = bf16[128,1024]{1,0:T(8,128)(2,1)S(1)} collective-permute-done((bf16[128,1024]{1,0:T(8,128)(2,1)S(1)}, bf16[128,1024]{1,0:T(8,128)(2,1)S(1)}, u32[]{:S(2)}, u32[]{:S(2)}) %collective-permute-start.1) | collective-permute-done | bytes 262176 | tf_op jit(solution)/shard_map/ppermute | solution.py:90
  83.8 1.9 collective-permute-start.2
  85.8 5.5 %collective-permute-done.13 = bf16[128,1024]{1,0:T(8,128)(2,1)S(1)} collective-permute-done((bf16[128,1024]{1,0:T(8,128)(2,1)S(1)}, bf16[128,1024]{1,0:T(8,128)(2,1)S(1)}, u32[]{:S(2)}, u32[]{:S(2)}) %collective-permute-start.13) | collective-permute-done | bytes 262176 | tf_op jit(solution)/shard_map/ppermute | solution.py:90
  91.4 1.9 collective-permute-start.14
  93.4 7.8 %collective-permute-start.7 = (bf16[32,1024]{1,0:T(8,128)(2,1)S(1)}, bf16[32,1024]{1,0:T(8,128)(2,1)S(1)}, u32[]{:S(2)}, u32[]{:S(2)}) collective-permute-start(bf16[32,1024]{1,0:T(8,128)(2,1)S(1)} %slice.177), channel_id=1, source_target_pairs={{0,256},{32,288},{64,320},{96,352},{128,384},{160,416},{192,448},{... | collective-permute-start | bytes 196616 | tf_op jit(solution)/shard_map/ppermute | solution.py:90
  101.3 1.9 collective-permute-start.3
  103.3 7.3 %collective-permute-start.15 = (bf16[32,1024]{1,0:T(8,128)(2,1)S(1)}, bf16[32,1024]{1,0:T(8,128)(2,1)S(1)}, u32[]{:S(2)}, u32[]{:S(2)}) collective-permute-start(bf16[32,1024]{1,0:T(8,128)(2,1)S(1)} %slice.185), channel_id=1, source_target_pairs={{0,256},{32,288},{64,320},{96,352},{128,384},{160,416},{192,448},{... | collective-permute-start | bytes 196616 | tf_op jit(solution)/shard_map/ppermute | solution.py:90
  110.6 0.8 collective-permute-done.3
  111.3 0.9 collective-permute-done.15
  112.3 7.3 %collective-permute-start.20 = (bf16[32,1024]{1,0:T(8,128)(2,1)S(1)}, bf16[32,1024]{1,0:T(8,128)(2,1)S(1)}, u32[]{:S(2)}, u32[]{:S(2)}) collective-permute-start(bf16[32,1024]{1,0:T(8,128)(2,1)S(1)} %get-tuple-element.13), channel_id=1, source_target_pairs={{0,256},{32,288},{64,320},{96,352},{128,384},{160,416},{192,448},{... | collective-permute-start | bytes 196616 | tf_op jit(solution)/shard_map/ppermute | solution.py:98
  119.6 1.9 collective-permute-start.16
  121.5 7.3 %collective-permute-start.8 = (bf16[32,1024]{1,0:T(8,128)(2,1)S(1)}, bf16[32,1024]{1,0:T(8,128)(2,1)S(1)}, u32[]{:S(2)}, u32[]{:S(2)}) collective-permute-start(bf16[32,1024]{1,0:T(8,128)(2,1)S(1)} %get-tuple-element.5), channel_id=1, source_target_pairs={{0,256},{32,288},{64,320},{96,352},{128,384},{160,416},{192,448},{... | collective-permute-start | bytes 196616 | tf_op jit(solution)/shard_map/ppermute | solution.py:98
  128.8 8.1 %collective-permute-start.21 = (bf16[64,1024]{1,0:T(8,128)(2,1)S(1)}, bf16[64,1024]{1,0:T(8,128)(2,1)S(1)}, u32[]{:S(2)}, u32[]{:S(2)}) collective-permute-start(bf16[64,1024]{1,0:T(8,128)(2,1)S(1)} %pad_maximum_fusion.10), channel_id=1, source_target_pairs={{0,128},{32,160},{64,192},{96,224},{128,0},{160,32},{192,64},{224,... | collective-permute-start | bytes 393224 | tf_op jit(solution)/shard_map/ppermute | solution.py:98
  136.9 2.9 %collective-permute-start.17 = (bf16[64,1024]{1,0:T(8,128)(2,1)S(1)}, bf16[64,1024]{1,0:T(8,128)(2,1)S(1)}, u32[]{:S(2)}, u32[]{:S(2)}) collective-permute-start(bf16[64,1024]{1,0:T(8,128)(2,1)S(1)} %pad_maximum_fusion.9), channel_id=1, source_target_pairs={{0,128},{32,160},{64,192},{96,224},{128,0},{160,32},{192,64},{224,... | collective-permute-start | bytes 393224 | tf_op jit(solution)/shard_map/ppermute | solution.py:98
  139.9 3.3 %collective-permute-start.9 = (bf16[64,1024]{1,0:T(8,128)(2,1)S(1)}, bf16[64,1024]{1,0:T(8,128)(2,1)S(1)}, u32[]{:S(2)}, u32[]{:S(2)}) collective-permute-start(bf16[64,1024]{1,0:T(8,128)(2,1)S(1)} %pad_maximum_fusion.8), channel_id=1, source_target_pairs={{0,128},{32,160},{64,192},{96,224},{128,0},{160,32},{192,64},{224,... | collective-permute-start | bytes 393224 | tf_op jit(solution)/shard_map/ppermute | solution.py:98
  144.0 11.6 %collective-permute-start.22 = (bf16[128,1024]{1,0:T(8,128)(2,1)S(1)}, bf16[128,1024]{1,0:T(8,128)(2,1)S(1)}, u32[]{:S(2)}, u32[]{:S(2)}) collective-permute-start(bf16[128,1024]{1,0:T(8,128)(2,1)S(1)} %pad_maximum_fusion.7), channel_id=1, source_target_pairs={{0,64},{32,96},{64,0},{96,32},{128,192},{160,224},{192,128},{224,1... | collective-permute-start | bytes 786440 | tf_op jit(solution)/shard_map/ppermute | solution.py:98
  155.6 2.8 %collective-permute-start.18 = (bf16[128,1024]{1,0:T(8,128)(2,1)S(1)}, bf16[128,1024]{1,0:T(8,128)(2,1)S(1)}, u32[]{:S(2)}, u32[]{:S(2)}) collective-permute-start(bf16[128,1024]{1,0:T(8,128)(2,1)S(1)} %pad_maximum_fusion.6), channel_id=1, source_target_pairs={{0,64},{32,96},{64,0},{96,32},{128,192},{160,224},{192,128},{224,1... | collective-permute-start | bytes 786440 | tf_op jit(solution)/shard_map/ppermute | solution.py:98
  158.4 2.8 %collective-permute-start.10 = (bf16[128,1024]{1,0:T(8,128)(2,1)S(1)}, bf16[128,1024]{1,0:T(8,128)(2,1)S(1)}, u32[]{:S(2)}, u32[]{:S(2)}) collective-permute-start(bf16[128,1024]{1,0:T(8,128)(2,1)S(1)} %pad_maximum_fusion.5), channel_id=1, source_target_pairs={{0,64},{32,96},{64,0},{96,32},{128,192},{160,224},{192,128},{224,1... | collective-permute-start | bytes 786440 | tf_op jit(solution)/shard_map/ppermute | solution.py:98
  161.3 1.4 collective-permute-done.22
  162.7 2.8 %collective-permute-start.23 = (bf16[256,1024]{1,0:T(8,128)(2,1)S(1)}, bf16[256,1024]{1,0:T(8,128)(2,1)S(1)}, u32[]{:S(2)}, u32[]{:S(2)}) collective-permute-start(bf16[256,1024]{1,0:T(8,128)(2,1)S(1)} %pad_maximum_fusion.3), channel_id=1, source_target_pairs={{0,32},{32,0},{64,96},{96,64},{128,160},{160,128},{192,224},{224,1... | collective-permute-start | bytes 1572872 | tf_op jit(solution)/shard_map/ppermute | solution.py:98
  165.5 8.4 %collective-permute-done.10 = bf16[128,1024]{1,0:T(8,128)(2,1)S(1)} collective-permute-done((bf16[128,1024]{1,0:T(8,128)(2,1)S(1)}, bf16[128,1024]{1,0:T(8,128)(2,1)S(1)}, u32[]{:S(2)}, u32[]{:S(2)}) %collective-permute-start.10) | collective-permute-done | bytes 262176 | tf_op jit(solution)/shard_map/ppermute | solution.py:98
  174.0 2.4 %collective-permute-start.11 = (bf16[256,1024]{1,0:T(8,128)(2,1)S(1)}, bf16[256,1024]{1,0:T(8,128)(2,1)S(1)}, u32[]{:S(2)}, u32[]{:S(2)}) collective-permute-start(bf16[256,1024]{1,0:T(8,128)(2,1)S(1)} %pad_maximum_fusion.1), channel_id=1, source_target_pairs={{0,32},{32,0},{64,96},{96,64},{128,160},{160,128},{192,224},{224,1... | collective-permute-start | bytes 1572872 | tf_op jit(solution)/shard_map/ppermute | solution.py:98
  176.4 1.9 collective-permute-start.19
  180.3 1.0 copy-done.2
  182.4 0.9 reverse_select_fusion
  183.3 4.6 %all-to-all-start.1 = ((bf16[32,16,512]{2,1,0:T(8,128)(2,1)}), bf16[32,16,512]{2,1,0:T(8,128)(2,1)}, u32[]{:S(2)}, u32[]{:S(2)}) async-start(bf16[32,16,512]{2,1,0:T(8,128)(2,1)} %bitcast.16), calls=%async_computation.1 | async-start | bytes 1048576 | tf_op jit(solution)/shard_map/all_to_all | solution.py:119
  188.0 1.3 fusion.4
  189.7 1.7 fusion
  191.4 32.9 %all-to-all-done.1 = bf16[32,16,512]{2,1,0:T(8,128)(2,1)} async-done(((bf16[32,16,512]{2,1,0:T(8,128)(2,1)}), bf16[32,16,512]{2,1,0:T(8,128)(2,1)}, u32[]{:S(2)}, u32[]{:S(2)}) %all-to-all-start.1) | async-done | bytes 524320 | tf_op jit(solution)/shard_map/all_to_all | solution.py:119
  224.2 1.8 convolution_convert_fusion.7
  226.1 1.2 convolution_multiply_fusion.2
  227.3 1.9 fusion.8
  (92 shorter events, 8.5 us)
Async XLA Ops:
  0.6 64.6 %copy-start = (bf16[1,1024,256]{2,1,0:T(8,128)(2,1)S(1)}, bf16[1,1024,256]{2,1,0:T(8,128)(2,1)}, u32[]{:S(2)}) copy-start(bf16[1,1024,256]{2,1,0:T(8,128)(2,1)} %param.11) | copy-start | bytes 1572868
  6.9 50.7 %all-to-all-start = ((bf16[32,16,512]{2,1,0:T(8,128)(2,1)}), bf16[32,16,512]{2,1,0:T(8,128)(2,1)S(1)}, u32[]{:S(2)}, u32[]{:S(2)}) async-start(bf16[32,16,512]{2,1,0:T(8,128)(2,1)} %bitcast.10), calls=%async_computation | async-start | bytes 1048576 | tf_op jit(solution)/shard_map/all_to_all | solution.py:70
  57.8 1.2 copy-start.1
  59.3 8.7 %collective-permute-start.4 = (bf16[256,1024]{1,0:T(8,128)(2,1)S(1)}, bf16[256,1024]{1,0:T(8,128)(2,1)S(1)}, u32[]{:S(2)}, u32[]{:S(2)}) collective-permute-start(bf16[256,1024]{1,0:T(8,128)(2,1)S(1)} %convolution_convert_fusion.3), channel_id=1, source_target_pairs={{0,32},{32,0},{64,96},{96,64},{128,160},{160,128},{192,224},{224,1... | collective-permute-start | bytes 1572872 | tf_op jit(solution)/shard_map/ppermute | solution.py:90
  63.3 7.0 %collective-permute-start = (bf16[256,1024]{1,0:T(8,128)(2,1)S(1)}, bf16[256,1024]{1,0:T(8,128)(2,1)S(1)}, u32[]{:S(2)}, u32[]{:S(2)}) collective-permute-start(bf16[256,1024]{1,0:T(8,128)(2,1)S(1)} %convolution_convert_fusion.4), channel_id=1, source_target_pairs={{0,32},{32,0},{64,96},{96,64},{128,160},{160,128},{192,224},{224,1... | collective-permute-start | bytes 1572872 | tf_op jit(solution)/shard_map/ppermute | solution.py:90
  65.5 8.4 %collective-permute-start.12 = (bf16[256,1024]{1,0:T(8,128)(2,1)S(1)}, bf16[256,1024]{1,0:T(8,128)(2,1)S(1)}, u32[]{:S(2)}, u32[]{:S(2)}) collective-permute-start(bf16[256,1024]{1,0:T(8,128)(2,1)S(1)} %convolution_convert_fusion.2), channel_id=1, source_target_pairs={{0,32},{32,0},{64,96},{96,64},{128,160},{160,128},{192,224},{224,1... | collective-permute-start | bytes 1572872 | tf_op jit(solution)/shard_map/ppermute | solution.py:90
  68.3 9.8 %collective-permute-start.5 = (bf16[128,1024]{1,0:T(8,128)(2,1)S(1)}, bf16[128,1024]{1,0:T(8,128)(2,1)S(1)}, u32[]{:S(2)}, u32[]{:S(2)}) collective-permute-start(bf16[128,1024]{1,0:T(8,128)(2,1)S(1)} %slice.173), channel_id=1, source_target_pairs={{0,64},{32,96},{64,0},{96,32},{128,192},{160,224},{192,128},{224,1... | collective-permute-start | bytes 786440 | tf_op jit(solution)/shard_map/ppermute | solution.py:90
  70.6 13.2 %collective-permute-start.1 = (bf16[128,1024]{1,0:T(8,128)(2,1)S(1)}, bf16[128,1024]{1,0:T(8,128)(2,1)S(1)}, u32[]{:S(2)}, u32[]{:S(2)}) collective-permute-start(bf16[128,1024]{1,0:T(8,128)(2,1)S(1)} %slice.166), channel_id=1, source_target_pairs={{0,64},{32,96},{64,0},{96,32},{128,192},{160,224},{192,128},{224,1... | collective-permute-start | bytes 786440 | tf_op jit(solution)/shard_map/ppermute | solution.py:90
  74.3 17.0 %collective-permute-start.13 = (bf16[128,1024]{1,0:T(8,128)(2,1)S(1)}, bf16[128,1024]{1,0:T(8,128)(2,1)S(1)}, u32[]{:S(2)}, u32[]{:S(2)}) collective-permute-start(bf16[128,1024]{1,0:T(8,128)(2,1)S(1)} %slice.181), channel_id=1, source_target_pairs={{0,64},{32,96},{64,0},{96,32},{128,192},{160,224},{192,128},{224,1... | collective-permute-start | bytes 786440 | tf_op jit(solution)/shard_map/ppermute | solution.py:90
  78.2 15.1 %collective-permute-start.6 = (bf16[64,1024]{1,0:T(8,128)(2,1)S(1)}, bf16[64,1024]{1,0:T(8,128)(2,1)S(1)}, u32[]{:S(2)}, u32[]{:S(2)}) collective-permute-start(bf16[64,1024]{1,0:T(8,128)(2,1)S(1)} %slice.175), channel_id=1, source_target_pairs={{0,128},{32,160},{64,192},{96,224},{128,0},{160,32},{192,64},{224,... | collective-permute-start | bytes 393224 | tf_op jit(solution)/shard_map/ppermute | solution.py:90
  83.8 17.4 %collective-permute-start.2 = (bf16[64,1024]{1,0:T(8,128)(2,1)S(1)}, bf16[64,1024]{1,0:T(8,128)(2,1)S(1)}, u32[]{:S(2)}, u32[]{:S(2)}) collective-permute-start(bf16[64,1024]{1,0:T(8,128)(2,1)S(1)} %slice.168), channel_id=1, source_target_pairs={{0,128},{32,160},{64,192},{96,224},{128,0},{160,32},{192,64},{224,... | collective-permute-start | bytes 393224 | tf_op jit(solution)/shard_map/ppermute | solution.py:90
  91.4 11.8 %collective-permute-start.14 = (bf16[64,1024]{1,0:T(8,128)(2,1)S(1)}, bf16[64,1024]{1,0:T(8,128)(2,1)S(1)}, u32[]{:S(2)}, u32[]{:S(2)}) collective-permute-start(bf16[64,1024]{1,0:T(8,128)(2,1)S(1)} %slice.183), channel_id=1, source_target_pairs={{0,128},{32,160},{64,192},{96,224},{128,0},{160,32},{192,64},{224,... | collective-permute-start | bytes 393224 | tf_op jit(solution)/shard_map/ppermute | solution.py:90
  93.4 17.2 %collective-permute-start.7 = (bf16[32,1024]{1,0:T(8,128)(2,1)S(1)}, bf16[32,1024]{1,0:T(8,128)(2,1)S(1)}, u32[]{:S(2)}, u32[]{:S(2)}) collective-permute-start(bf16[32,1024]{1,0:T(8,128)(2,1)S(1)} %slice.177), channel_id=1, source_target_pairs={{0,256},{32,288},{64,320},{96,352},{128,384},{160,416},{192,448},{... | collective-permute-start | bytes 196616 | tf_op jit(solution)/shard_map/ppermute | solution.py:90
  101.3 10.1 %collective-permute-start.3 = (bf16[32,1024]{1,0:T(8,128)(2,1)S(1)}, bf16[32,1024]{1,0:T(8,128)(2,1)S(1)}, u32[]{:S(2)}, u32[]{:S(2)}) collective-permute-start(bf16[32,1024]{1,0:T(8,128)(2,1)S(1)} %slice.170), channel_id=1, source_target_pairs={{0,256},{32,288},{64,320},{96,352},{128,384},{160,416},{192,448},{... | collective-permute-start | bytes 196616 | tf_op jit(solution)/shard_map/ppermute | solution.py:90
  103.3 8.9 %collective-permute-start.15 = (bf16[32,1024]{1,0:T(8,128)(2,1)S(1)}, bf16[32,1024]{1,0:T(8,128)(2,1)S(1)}, u32[]{:S(2)}, u32[]{:S(2)}) collective-permute-start(bf16[32,1024]{1,0:T(8,128)(2,1)S(1)} %slice.185), channel_id=1, source_target_pairs={{0,256},{32,288},{64,320},{96,352},{128,384},{160,416},{192,448},{... | collective-permute-start | bytes 196616 | tf_op jit(solution)/shard_map/ppermute | solution.py:90
  112.3 16.5 %collective-permute-start.20 = (bf16[32,1024]{1,0:T(8,128)(2,1)S(1)}, bf16[32,1024]{1,0:T(8,128)(2,1)S(1)}, u32[]{:S(2)}, u32[]{:S(2)}) collective-permute-start(bf16[32,1024]{1,0:T(8,128)(2,1)S(1)} %get-tuple-element.13), channel_id=1, source_target_pairs={{0,256},{32,288},{64,320},{96,352},{128,384},{160,416},{192,448},{... | collective-permute-start | bytes 196616 | tf_op jit(solution)/shard_map/ppermute | solution.py:98
  119.6 17.3 %collective-permute-start.16 = (bf16[32,1024]{1,0:T(8,128)(2,1)S(1)}, bf16[32,1024]{1,0:T(8,128)(2,1)S(1)}, u32[]{:S(2)}, u32[]{:S(2)}) collective-permute-start(bf16[32,1024]{1,0:T(8,128)(2,1)S(1)} %get-tuple-element.11), channel_id=1, source_target_pairs={{0,256},{32,288},{64,320},{96,352},{128,384},{160,416},{192,448},{... | collective-permute-start | bytes 196616 | tf_op jit(solution)/shard_map/ppermute | solution.py:98
  121.5 18.3 %collective-permute-start.8 = (bf16[32,1024]{1,0:T(8,128)(2,1)S(1)}, bf16[32,1024]{1,0:T(8,128)(2,1)S(1)}, u32[]{:S(2)}, u32[]{:S(2)}) collective-permute-start(bf16[32,1024]{1,0:T(8,128)(2,1)S(1)} %get-tuple-element.5), channel_id=1, source_target_pairs={{0,256},{32,288},{64,320},{96,352},{128,384},{160,416},{192,448},{... | collective-permute-start | bytes 196616 | tf_op jit(solution)/shard_map/ppermute | solution.py:98
  128.8 15.1 %collective-permute-start.21 = (bf16[64,1024]{1,0:T(8,128)(2,1)S(1)}, bf16[64,1024]{1,0:T(8,128)(2,1)S(1)}, u32[]{:S(2)}, u32[]{:S(2)}) collective-permute-start(bf16[64,1024]{1,0:T(8,128)(2,1)S(1)} %pad_maximum_fusion.10), channel_id=1, source_target_pairs={{0,128},{32,160},{64,192},{96,224},{128,0},{160,32},{192,64},{224,... | collective-permute-start | bytes 393224 | tf_op jit(solution)/shard_map/ppermute | solution.py:98
  136.9 18.6 %collective-permute-start.17 = (bf16[64,1024]{1,0:T(8,128)(2,1)S(1)}, bf16[64,1024]{1,0:T(8,128)(2,1)S(1)}, u32[]{:S(2)}, u32[]{:S(2)}) collective-permute-start(bf16[64,1024]{1,0:T(8,128)(2,1)S(1)} %pad_maximum_fusion.9), channel_id=1, source_target_pairs={{0,128},{32,160},{64,192},{96,224},{128,0},{160,32},{192,64},{224,... | collective-permute-start | bytes 393224 | tf_op jit(solution)/shard_map/ppermute | solution.py:98
  139.9 18.5 %collective-permute-start.9 = (bf16[64,1024]{1,0:T(8,128)(2,1)S(1)}, bf16[64,1024]{1,0:T(8,128)(2,1)S(1)}, u32[]{:S(2)}, u32[]{:S(2)}) collective-permute-start(bf16[64,1024]{1,0:T(8,128)(2,1)S(1)} %pad_maximum_fusion.8), channel_id=1, source_target_pairs={{0,128},{32,160},{64,192},{96,224},{128,0},{160,32},{192,64},{224,... | collective-permute-start | bytes 393224 | tf_op jit(solution)/shard_map/ppermute | solution.py:98
  144.0 18.7 %collective-permute-start.22 = (bf16[128,1024]{1,0:T(8,128)(2,1)S(1)}, bf16[128,1024]{1,0:T(8,128)(2,1)S(1)}, u32[]{:S(2)}, u32[]{:S(2)}) collective-permute-start(bf16[128,1024]{1,0:T(8,128)(2,1)S(1)} %pad_maximum_fusion.7), channel_id=1, source_target_pairs={{0,64},{32,96},{64,0},{96,32},{128,192},{160,224},{192,128},{224,1... | collective-permute-start | bytes 786440 | tf_op jit(solution)/shard_map/ppermute | solution.py:98
  155.6 20.7 %collective-permute-start.18 = (bf16[128,1024]{1,0:T(8,128)(2,1)S(1)}, bf16[128,1024]{1,0:T(8,128)(2,1)S(1)}, u32[]{:S(2)}, u32[]{:S(2)}) collective-permute-start(bf16[128,1024]{1,0:T(8,128)(2,1)S(1)} %pad_maximum_fusion.6), channel_id=1, source_target_pairs={{0,64},{32,96},{64,0},{96,32},{128,192},{160,224},{192,128},{224,1... | collective-permute-start | bytes 786440 | tf_op jit(solution)/shard_map/ppermute | solution.py:98
  158.4 15.5 %collective-permute-start.10 = (bf16[128,1024]{1,0:T(8,128)(2,1)S(1)}, bf16[128,1024]{1,0:T(8,128)(2,1)S(1)}, u32[]{:S(2)}, u32[]{:S(2)}) collective-permute-start(bf16[128,1024]{1,0:T(8,128)(2,1)S(1)} %pad_maximum_fusion.5), channel_id=1, source_target_pairs={{0,64},{32,96},{64,0},{96,32},{128,192},{160,224},{192,128},{224,1... | collective-permute-start | bytes 786440 | tf_op jit(solution)/shard_map/ppermute | solution.py:98
  162.7 15.7 %collective-permute-start.23 = (bf16[256,1024]{1,0:T(8,128)(2,1)S(1)}, bf16[256,1024]{1,0:T(8,128)(2,1)S(1)}, u32[]{:S(2)}, u32[]{:S(2)}) collective-permute-start(bf16[256,1024]{1,0:T(8,128)(2,1)S(1)} %pad_maximum_fusion.3), channel_id=1, source_target_pairs={{0,32},{32,0},{64,96},{96,64},{128,160},{160,128},{192,224},{224,1... | collective-permute-start | bytes 1572872 | tf_op jit(solution)/shard_map/ppermute | solution.py:98
  174.0 4.5 %collective-permute-start.11 = (bf16[256,1024]{1,0:T(8,128)(2,1)S(1)}, bf16[256,1024]{1,0:T(8,128)(2,1)S(1)}, u32[]{:S(2)}, u32[]{:S(2)}) collective-permute-start(bf16[256,1024]{1,0:T(8,128)(2,1)S(1)} %pad_maximum_fusion.1), channel_id=1, source_target_pairs={{0,32},{32,0},{64,96},{96,64},{128,160},{160,128},{192,224},{224,1... | collective-permute-start | bytes 1572872 | tf_op jit(solution)/shard_map/ppermute | solution.py:98
  176.4 3.8 %collective-permute-start.19 = (bf16[256,1024]{1,0:T(8,128)(2,1)S(1)}, bf16[256,1024]{1,0:T(8,128)(2,1)S(1)}, u32[]{:S(2)}, u32[]{:S(2)}) collective-permute-start(bf16[256,1024]{1,0:T(8,128)(2,1)S(1)} %pad_maximum_fusion.2), channel_id=1, source_target_pairs={{0,32},{32,0},{64,96},{96,64},{128,160},{160,128},{192,224},{224,1... | collective-permute-start | bytes 1572872 | tf_op jit(solution)/shard_map/ppermute | solution.py:98
  178.5 1.0 copy-start.4
  180.3 1.0 copy-start.2
  182.4 5.6 %copy-start.6 = (f32[128,2]{0,1:T(2,128)S(1)}, f32[128,2]{0,1:T(2,128)}, u32[]{:S(2)}) copy-start(f32[128,2]{0,1:T(2,128)} %param.8) | copy-start | bytes 3076
  183.3 41.0 %all-to-all-start.1 = ((bf16[32,16,512]{2,1,0:T(8,128)(2,1)}), bf16[32,16,512]{2,1,0:T(8,128)(2,1)}, u32[]{:S(2)}, u32[]{:S(2)}) async-start(bf16[32,16,512]{2,1,0:T(8,128)(2,1)} %bitcast.16), calls=%async_computation.1 | async-start | bytes 1048576 | tf_op jit(solution)/shard_map/all_to_all | solution.py:119
  187.9 1.3 copy-start.3
  187.9 1.7 copy-start.5

commit v6 on v5

--- a/solution.py
+++ b/solution.py
@@ -64,9 +64,10 @@
         jnp.sum(jnp.where(p, weights[k : k + 1], 0.0), axis=1, keepdims=True)
         for k, p in enumerate(picked)
     )
-    send_x = mm(selector, tokens).astype(BF)
-    send_g = (mm(selector, cotangent) * slot_weight).astype(BF)
-    send = jnp.concatenate([send_x, send_g], axis=1).reshape(experts, slots, 2 * feat)
+    columns = lax.broadcasted_iota(jnp.int32, (rows, 2 * feat), 1)
+    scale = jnp.where(columns < feat, 1.0, slot_weight)
+    send = mm(selector, jnp.concatenate([tokens, cotangent], axis=1)) * scale
+    send = send.astype(BF).reshape(experts, slots, 2 * feat)
     recv = lax.all_to_all(send, "expert", split_axis=0, concat_axis=0, tiled=True)
 
     def flip(rows_):

time: 230 us -> 229 us (level)
  no operation moved by 1% of the time
where the time goes in v6:
time: 229 us; the launch traced here: 228 us
  starting transfers between devices  111 us (48%)
  waiting for transfers between devices  93.3 us (41%)
  matrix products  13.4 us (6%)
  local copies, waits for them, and re-layouts  4.94 us (2%)
  other arithmetic  3.4 us (1%)
    ppermute x12, starting transfers between devices, all_gather(): own = jnp.concatenate([own, lax.ppermute(own, 'dp', perm)], axis=0)  54.9 us
    ppermute x12, starting transfers between devices, reduce_scatter(): keep = lax.ppermute(away, 'dp', perm).astype(F32) + keep.astype(F32)  37.9 us
    all_to_all x1, waiting for transfers between devices, on_device(): lax.all_to_all(send, 'expert', split_axis=0, concat_axis=0, tiled=True)  36.9 us
    all_to_all x1, waiting for transfers between devices, on_device(): lax.all_to_all(back, 'expert', split_axis=0, concat_axis=0, tiled=True)  32.9 us
    all_to_all x1, starting transfers between devices, on_device(): lax.all_to_all(send, 'expert', split_axis=0, concat_axis=0, tiled=True)  13.7 us
    ppermute x12, waiting for transfers between devices, reduce_scatter(): keep = lax.ppermute(away, 'dp', perm).astype(F32) + keep.astype(F32)  12.7 us
    ppermute x12, waiting for transfers between devices, all_gather(): own = jnp.concatenate([own, lax.ppermute(own, 'dp', perm)], axis=0)  10.9 us
    dot_general x5, matrix products, mm_tn(): lax.dot_general(a, b, (((0,), (0,)), ((), ())), preferred_element_type=F32)  7.88 us
  transfers between devices with their start and end apart: 26, of which 11 were waited for; matrix products, arithmetic and copies ran while one was open for 3% of the time, Pallas kernels for 0%

profile of v6, /device:TPU:193, one launch (start us, length us, event | category | flops | bytes accessed | tf_op | source)
XLA Modules:
  0.0 227.8 jit_solution(3780653938578083156)
XLA Ops:
  0.6 0.8 slice_bitcast_fusion.4
  1.7 0.8 slice_bitcast_fusion.2
  2.6 0.8 fusion.60
  3.6 2.0 fusion.4
  5.5 13.7 %all-to-all-start = ((bf16[32,16,512]{2,1,0:T(8,128)(2,1)}), bf16[32,16,512]{2,1,0:T(8,128)(2,1)S(1)}, u32[]{:S(2)}, u32[]{:S(2)}) async-start(bf16[32,16,512]{2,1,0:T(8,128)(2,1)} %bitcast.10), calls=%async_computation | async-start | bytes 1048576 | tf_op jit(solution)/shard_map/all_to_all | solution.py:71
  19.3 36.9 %all-to-all-done = bf16[32,16,512]{2,1,0:T(8,128)(2,1)S(1)} async-done(((bf16[32,16,512]{2,1,0:T(8,128)(2,1)}), bf16[32,16,512]{2,1,0:T(8,128)(2,1)S(1)}, u32[]{:S(2)}, u32[]{:S(2)}) %all-to-all-start) | async-done | bytes 524320 | tf_op jit(solution)/shard_map/all_to_all | solution.py:71
  56.7 1.0 copy-done.1
  58.0 3.6 %collective-permute-start.4 = (bf16[256,1024]{1,0:T(8,128)(2,1)S(1)}, bf16[256,1024]{1,0:T(8,128)(2,1)S(1)}, u32[]{:S(2)}, u32[]{:S(2)}) collective-permute-start(bf16[256,1024]{1,0:T(8,128)(2,1)S(1)} %convolution_convert_fusion.3), channel_id=1, source_target_pairs={{0,32},{32,0},{64,96},{96,64},{128,160},{160,128},{192,224},{224,1... | collective-permute-start | bytes 1572872 | tf_op jit(solution)/shard_map/ppermute | solution.py:91
  62.0 1.9 collective-permute-start
  64.2 2.4 %collective-permute-start.12 = (bf16[256,1024]{1,0:T(8,128)(2,1)S(1)}, bf16[256,1024]{1,0:T(8,128)(2,1)S(1)}, u32[]{:S(2)}, u32[]{:S(2)}) collective-permute-start(bf16[256,1024]{1,0:T(8,128)(2,1)S(1)} %convolution_convert_fusion.2), channel_id=1, source_target_pairs={{0,32},{32,0},{64,96},{96,64},{128,160},{160,128},{192,224},{224,1... | collective-permute-start | bytes 1572872 | tf_op jit(solution)/shard_map/ppermute | solution.py:91
  67.0 1.9 collective-permute-start.5
  69.3 3.4 %collective-permute-start.1 = (bf16[128,1024]{1,0:T(8,128)(2,1)S(1)}, bf16[128,1024]{1,0:T(8,128)(2,1)S(1)}, u32[]{:S(2)}, u32[]{:S(2)}) collective-permute-start(bf16[128,1024]{1,0:T(8,128)(2,1)S(1)} %slice.166), channel_id=1, source_target_pairs={{0,64},{32,96},{64,0},{96,32},{128,192},{160,224},{192,128},{224,1... | collective-permute-start | bytes 786440 | tf_op jit(solution)/shard_map/ppermute | solution.py:91
  73.0 1.9 collective-permute-start.13
  75.0 1.9 collective-permute-done.5
  76.9 1.9 collective-permute-start.6
  78.8 3.6 %collective-permute-done.1 = bf16[128,1024]{1,0:T(8,128)(2,1)S(1)} collective-permute-done((bf16[128,1024]{1,0:T(8,128)(2,1)S(1)}, bf16[128,1024]{1,0:T(8,128)(2,1)S(1)}, u32[]{:S(2)}, u32[]{:S(2)}) %collective-permute-start.1) | collective-permute-done | bytes 262176 | tf_op jit(solution)/shard_map/ppermute | solution.py:91
  82.5 1.9 collective-permute-start.2
  84.5 5.5 %collective-permute-done.13 = bf16[128,1024]{1,0:T(8,128)(2,1)S(1)} collective-permute-done((bf16[128,1024]{1,0:T(8,128)(2,1)S(1)}, bf16[128,1024]{1,0:T(8,128)(2,1)S(1)}, u32[]{:S(2)}, u32[]{:S(2)}) %collective-permute-start.13) | collective-permute-done | bytes 262176 | tf_op jit(solution)/shard_map/ppermute | solution.py:91
  90.1 1.9 collective-permute-start.14
  92.1 7.8 %collective-permute-start.7 = (bf16[32,1024]{1,0:T(8,128)(2,1)S(1)}, bf16[32,1024]{1,0:T(8,128)(2,1)S(1)}, u32[]{:S(2)}, u32[]{:S(2)}) collective-permute-start(bf16[32,1024]{1,0:T(8,128)(2,1)S(1)} %slice.177), channel_id=1, source_target_pairs={{0,256},{32,288},{64,320},{96,352},{128,384},{160,416},{192,448},{... | collective-permute-start | bytes 196616 | tf_op jit(solution)/shard_map/ppermute | solution.py:91
  100.0 1.9 collective-permute-start.3
  102.0 7.3 %collective-permute-start.15 = (bf16[32,1024]{1,0:T(8,128)(2,1)S(1)}, bf16[32,1024]{1,0:T(8,128)(2,1)S(1)}, u32[]{:S(2)}, u32[]{:S(2)}) collective-permute-start(bf16[32,1024]{1,0:T(8,128)(2,1)S(1)} %slice.185), channel_id=1, source_target_pairs={{0,256},{32,288},{64,320},{96,352},{128,384},{160,416},{192,448},{... | collective-permute-start | bytes 196616 | tf_op jit(solution)/shard_map/ppermute | solution.py:91
  109.3 0.8 collective-permute-done.3
  110.0 0.9 collective-permute-done.15
  111.0 7.3 %collective-permute-start.20 = (bf16[32,1024]{1,0:T(8,128)(2,1)S(1)}, bf16[32,1024]{1,0:T(8,128)(2,1)S(1)}, u32[]{:S(2)}, u32[]{:S(2)}) collective-permute-start(bf16[32,1024]{1,0:T(8,128)(2,1)S(1)} %get-tuple-element.13), channel_id=1, source_target_pairs={{0,256},{32,288},{64,320},{96,352},{128,384},{160,416},{192,448},{... | collective-permute-start | bytes 196616 | tf_op jit(solution)/shard_map/ppermute | solution.py:99
  118.3 1.9 collective-permute-start.16
  120.2 7.3 %collective-permute-start.8 = (bf16[32,1024]{1,0:T(8,128)(2,1)S(1)}, bf16[32,1024]{1,0:T(8,128)(2,1)S(1)}, u32[]{:S(2)}, u32[]{:S(2)}) collective-permute-start(bf16[32,1024]{1,0:T(8,128)(2,1)S(1)} %get-tuple-element.5), channel_id=1, source_target_pairs={{0,256},{32,288},{64,320},{96,352},{128,384},{160,416},{192,448},{... | collective-permute-start | bytes 196616 | tf_op jit(solution)/shard_map/ppermute | solution.py:99
  127.5 8.1 %collective-permute-start.21 = (bf16[64,1024]{1,0:T(8,128)(2,1)S(1)}, bf16[64,1024]{1,0:T(8,128)(2,1)S(1)}, u32[]{:S(2)}, u32[]{:S(2)}) collective-permute-start(bf16[64,1024]{1,0:T(8,128)(2,1)S(1)} %pad_maximum_fusion.9), channel_id=1, source_target_pairs={{0,128},{32,160},{64,192},{96,224},{128,0},{160,32},{192,64},{224,... | collective-permute-start | bytes 393224 | tf_op jit(solution)/shard_map/ppermute | solution.py:99
  135.6 2.9 %collective-permute-start.17 = (bf16[64,1024]{1,0:T(8,128)(2,1)S(1)}, bf16[64,1024]{1,0:T(8,128)(2,1)S(1)}, u32[]{:S(2)}, u32[]{:S(2)}) collective-permute-start(bf16[64,1024]{1,0:T(8,128)(2,1)S(1)} %pad_maximum_fusion.8), channel_id=1, source_target_pairs={{0,128},{32,160},{64,192},{96,224},{128,0},{160,32},{192,64},{224,... | collective-permute-start | bytes 393224 | tf_op jit(solution)/shard_map/ppermute | solution.py:99
  138.6 3.3 %collective-permute-start.9 = (bf16[64,1024]{1,0:T(8,128)(2,1)S(1)}, bf16[64,1024]{1,0:T(8,128)(2,1)S(1)}, u32[]{:S(2)}, u32[]{:S(2)}) collective-permute-start(bf16[64,1024]{1,0:T(8,128)(2,1)S(1)} %pad_maximum_fusion.7), channel_id=1, source_target_pairs={{0,128},{32,160},{64,192},{96,224},{128,0},{160,32},{192,64},{224,... | collective-permute-start | bytes 393224 | tf_op jit(solution)/shard_map/ppermute | solution.py:99
  141.9 0.7 collective-permute-done.21
  142.7 11.6 %collective-permute-start.22 = (bf16[128,1024]{1,0:T(8,128)(2,1)S(1)}, bf16[128,1024]{1,0:T(8,128)(2,1)S(1)}, u32[]{:S(2)}, u32[]{:S(2)}) collective-permute-start(bf16[128,1024]{1,0:T(8,128)(2,1)S(1)} %pad_maximum_fusion.6), channel_id=1, source_target_pairs={{0,64},{32,96},{64,0},{96,32},{128,192},{160,224},{192,128},{224,1... | collective-permute-start | bytes 786440 | tf_op jit(solution)/shard_map/ppermute | solution.py:99
  154.3 2.8 %collective-permute-start.18 = (bf16[128,1024]{1,0:T(8,128)(2,1)S(1)}, bf16[128,1024]{1,0:T(8,128)(2,1)S(1)}, u32[]{:S(2)}, u32[]{:S(2)}) collective-permute-start(bf16[128,1024]{1,0:T(8,128)(2,1)S(1)} %pad_maximum_fusion.5), channel_id=1, source_target_pairs={{0,64},{32,96},{64,0},{96,32},{128,192},{160,224},{192,128},{224,1... | collective-permute-start | bytes 786440 | tf_op jit(solution)/shard_map/ppermute | solution.py:99
  157.1 2.8 %collective-permute-start.10 = (bf16[128,1024]{1,0:T(8,128)(2,1)S(1)}, bf16[128,1024]{1,0:T(8,128)(2,1)S(1)}, u32[]{:S(2)}, u32[]{:S(2)}) collective-permute-start(bf16[128,1024]{1,0:T(8,128)(2,1)S(1)} %pad_maximum_fusion.4), channel_id=1, source_target_pairs={{0,64},{32,96},{64,0},{96,32},{128,192},{160,224},{192,128},{224,1... | collective-permute-start | bytes 786440 | tf_op jit(solution)/shard_map/ppermute | solution.py:99
  160.0 1.4 collective-permute-done.22
  161.4 2.8 %collective-permute-start.23 = (bf16[256,1024]{1,0:T(8,128)(2,1)S(1)}, bf16[256,1024]{1,0:T(8,128)(2,1)S(1)}, u32[]{:S(2)}, u32[]{:S(2)}) collective-permute-start(bf16[256,1024]{1,0:T(8,128)(2,1)S(1)} %pad_maximum_fusion.2), channel_id=1, source_target_pairs={{0,32},{32,0},{64,96},{96,64},{128,160},{160,128},{192,224},{224,1... | collective-permute-start | bytes 1572872 | tf_op jit(solution)/shard_map/ppermute | solution.py:99
  164.2 8.4 %collective-permute-done.10 = bf16[128,1024]{1,0:T(8,128)(2,1)S(1)} collective-permute-done((bf16[128,1024]{1,0:T(8,128)(2,1)S(1)}, bf16[128,1024]{1,0:T(8,128)(2,1)S(1)}, u32[]{:S(2)}, u32[]{:S(2)}) %collective-permute-start.10) | collective-permute-done | bytes 262176 | tf_op jit(solution)/shard_map/ppermute | solution.py:99
  172.6 2.4 %collective-permute-start.11 = (bf16[256,1024]{1,0:T(8,128)(2,1)S(1)}, bf16[256,1024]{1,0:T(8,128)(2,1)S(1)}, u32[]{:S(2)}, u32[]{:S(2)}) collective-permute-start(bf16[256,1024]{1,0:T(8,128)(2,1)S(1)} %pad_maximum_fusion), channel_id=1, source_target_pairs={{0,32},{32,0},{64,96},{96,64},{128,160},{160,128},{192,224},{224,1... | collective-permute-start | bytes 1572872 | tf_op jit(solution)/shard_map/ppermute | solution.py:99
  175.1 1.9 collective-permute-start.19
  179.0 1.0 copy-done.2
  181.1 0.9 reverse_select_fusion
  182.0 4.6 %all-to-all-start.1 = ((bf16[32,16,512]{2,1,0:T(8,128)(2,1)}), bf16[32,16,512]{2,1,0:T(8,128)(2,1)}, u32[]{:S(2)}, u32[]{:S(2)}) async-start(bf16[32,16,512]{2,1,0:T(8,128)(2,1)} %bitcast.16), calls=%async_computation.1 | async-start | bytes 1048576 | tf_op jit(solution)/shard_map/all_to_all | solution.py:120
  186.7 1.3 fusion.5
  188.4 1.7 fusion
  190.1 32.9 %all-to-all-done.1 = bf16[32,16,512]{2,1,0:T(8,128)(2,1)} async-done(((bf16[32,16,512]{2,1,0:T(8,128)(2,1)}), bf16[32,16,512]{2,1,0:T(8,128)(2,1)}, u32[]{:S(2)}, u32[]{:S(2)}) %all-to-all-start.1) | async-done | bytes 524320 | tf_op jit(solution)/shard_map/all_to_all | solution.py:120
  222.9 1.8 convolution_convert_fusion.6
  224.8 1.2 convolution_multiply_fusion.2
  226.0 1.8 fusion.8
  (90 shorter events, 7.0 us)
Async XLA Ops:
  0.6 63.3 %copy-start = (bf16[1,1024,256]{2,1,0:T(8,128)(2,1)S(1)}, bf16[1,1024,256]{2,1,0:T(8,128)(2,1)}, u32[]{:S(2)}) copy-start(bf16[1,1024,256]{2,1,0:T(8,128)(2,1)} %param.11) | copy-start | bytes 1572868
  5.5 50.7 %all-to-all-start = ((bf16[32,16,512]{2,1,0:T(8,128)(2,1)}), bf16[32,16,512]{2,1,0:T(8,128)(2,1)S(1)}, u32[]{:S(2)}, u32[]{:S(2)}) async-start(bf16[32,16,512]{2,1,0:T(8,128)(2,1)} %bitcast.10), calls=%async_computation | async-start | bytes 1048576 | tf_op jit(solution)/shard_map/all_to_all | solution.py:71
  56.5 1.2 copy-start.1
  58.0 8.7 %collective-permute-start.4 = (bf16[256,1024]{1,0:T(8,128)(2,1)S(1)}, bf16[256,1024]{1,0:T(8,128)(2,1)S(1)}, u32[]{:S(2)}, u32[]{:S(2)}) collective-permute-start(bf16[256,1024]{1,0:T(8,128)(2,1)S(1)} %convolution_convert_fusion.3), channel_id=1, source_target_pairs={{0,32},{32,0},{64,96},{96,64},{128,160},{160,128},{192,224},{224,1... | collective-permute-start | bytes 1572872 | tf_op jit(solution)/shard_map/ppermute | solution.py:91
  62.0 7.0 %collective-permute-start = (bf16[256,1024]{1,0:T(8,128)(2,1)S(1)}, bf16[256,1024]{1,0:T(8,128)(2,1)S(1)}, u32[]{:S(2)}, u32[]{:S(2)}) collective-permute-start(bf16[256,1024]{1,0:T(8,128)(2,1)S(1)} %convolution_convert_fusion.4), channel_id=1, source_target_pairs={{0,32},{32,0},{64,96},{96,64},{128,160},{160,128},{192,224},{224,1... | collective-permute-start | bytes 1572872 | tf_op jit(solution)/shard_map/ppermute | solution.py:91
  64.2 8.4 %collective-permute-start.12 = (bf16[256,1024]{1,0:T(8,128)(2,1)S(1)}, bf16[256,1024]{1,0:T(8,128)(2,1)S(1)}, u32[]{:S(2)}, u32[]{:S(2)}) collective-permute-start(bf16[256,1024]{1,0:T(8,128)(2,1)S(1)} %convolution_convert_fusion.2), channel_id=1, source_target_pairs={{0,32},{32,0},{64,96},{96,64},{128,160},{160,128},{192,224},{224,1... | collective-permute-start | bytes 1572872 | tf_op jit(solution)/shard_map/ppermute | solution.py:91
  67.0 9.8 %collective-permute-start.5 = (bf16[128,1024]{1,0:T(8,128)(2,1)S(1)}, bf16[128,1024]{1,0:T(8,128)(2,1)S(1)}, u32[]{:S(2)}, u32[]{:S(2)}) collective-permute-start(bf16[128,1024]{1,0:T(8,128)(2,1)S(1)} %slice.173), channel_id=1, source_target_pairs={{0,64},{32,96},{64,0},{96,32},{128,192},{160,224},{192,128},{224,1... | collective-permute-start | bytes 786440 | tf_op jit(solution)/shard_map/ppermute | solution.py:91
  69.3 13.2 %collective-permute-start.1 = (bf16[128,1024]{1,0:T(8,128)(2,1)S(1)}, bf16[128,1024]{1,0:T(8,128)(2,1)S(1)}, u32[]{:S(2)}, u32[]{:S(2)}) collective-permute-start(bf16[128,1024]{1,0:T(8,128)(2,1)S(1)} %slice.166), channel_id=1, source_target_pairs={{0,64},{32,96},{64,0},{96,32},{128,192},{160,224},{192,128},{224,1... | collective-permute-start | bytes 786440 | tf_op jit(solution)/shard_map/ppermute | solution.py:91
  73.0 17.0 %collective-permute-start.13 = (bf16[128,1024]{1,0:T(8,128)(2,1)S(1)}, bf16[128,1024]{1,0:T(8,128)(2,1)S(1)}, u32[]{:S(2)}, u32[]{:S(2)}) collective-permute-start(bf16[128,1024]{1,0:T(8,128)(2,1)S(1)} %slice.181), channel_id=1, source_target_pairs={{0,64},{32,96},{64,0},{96,32},{128,192},{160,224},{192,128},{224,1... | collective-permute-start | bytes 786440 | tf_op jit(solution)/shard_map/ppermute | solution.py:91
  76.9 15.1 %collective-permute-start.6 = (bf16[64,1024]{1,0:T(8,128)(2,1)S(1)}, bf16[64,1024]{1,0:T(8,128)(2,1)S(1)}, u32[]{:S(2)}, u32[]{:S(2)}) collective-permute-start(bf16[64,1024]{1,0:T(8,128)(2,1)S(1)} %slice.175), channel_id=1, source_target_pairs={{0,128},{32,160},{64,192},{96,224},{128,0},{160,32},{192,64},{224,... | collective-permute-start | bytes 393224 | tf_op jit(solution)/shard_map/ppermute | solution.py:91
  82.5 17.4 %collective-permute-start.2 = (bf16[64,1024]{1,0:T(8,128)(2,1)S(1)}, bf16[64,1024]{1,0:T(8,128)(2,1)S(1)}, u32[]{:S(2)}, u32[]{:S(2)}) collective-permute-start(bf16[64,1024]{1,0:T(8,128)(2,1)S(1)} %slice.168), channel_id=1, source_target_pairs={{0,128},{32,160},{64,192},{96,224},{128,0},{160,32},{192,64},{224,... | collective-permute-start | bytes 393224 | tf_op jit(solution)/shard_map/ppermute | solution.py:91
  90.1 11.8 %collective-permute-start.14 = (bf16[64,1024]{1,0:T(8,128)(2,1)S(1)}, bf16[64,1024]{1,0:T(8,128)(2,1)S(1)}, u32[]{:S(2)}, u32[]{:S(2)}) collective-permute-start(bf16[64,1024]{1,0:T(8,128)(2,1)S(1)} %slice.183), channel_id=1, source_target_pairs={{0,128},{32,160},{64,192},{96,224},{128,0},{160,32},{192,64},{224,... | collective-permute-start | bytes 393224 | tf_op jit(solution)/shard_map/ppermute | solution.py:91
  92.1 17.2 %collective-permute-start.7 = (bf16[32,1024]{1,0:T(8,128)(2,1)S(1)}, bf16[32,1024]{1,0:T(8,128)(2,1)S(1)}, u32[]{:S(2)}, u32[]{:S(2)}) collective-permute-start(bf16[32,1024]{1,0:T(8,128)(2,1)S(1)} %slice.177), channel_id=1, source_target_pairs={{0,256},{32,288},{64,320},{96,352},{128,384},{160,416},{192,448},{... | collective-permute-start | bytes 196616 | tf_op jit(solution)/shard_map/ppermute | solution.py:91
  100.0 10.1 %collective-permute-start.3 = (bf16[32,1024]{1,0:T(8,128)(2,1)S(1)}, bf16[32,1024]{1,0:T(8,128)(2,1)S(1)}, u32[]{:S(2)}, u32[]{:S(2)}) collective-permute-start(bf16[32,1024]{1,0:T(8,128)(2,1)S(1)} %slice.170), channel_id=1, source_target_pairs={{0,256},{32,288},{64,320},{96,352},{128,384},{160,416},{192,448},{... | collective-permute-start | bytes 196616 | tf_op jit(solution)/shard_map/ppermute | solution.py:91
  102.0 8.9 %collective-permute-start.15 = (bf16[32,1024]{1,0:T(8,128)(2,1)S(1)}, bf16[32,1024]{1,0:T(8,128)(2,1)S(1)}, u32[]{:S(2)}, u32[]{:S(2)}) collective-permute-start(bf16[32,1024]{1,0:T(8,128)(2,1)S(1)} %slice.185), channel_id=1, source_target_pairs={{0,256},{32,288},{64,320},{96,352},{128,384},{160,416},{192,448},{... | collective-permute-start | bytes 196616 | tf_op jit(solution)/shard_map/ppermute | solution.py:91
  111.0 16.5 %collective-permute-start.20 = (bf16[32,1024]{1,0:T(8,128)(2,1)S(1)}, bf16[32,1024]{1,0:T(8,128)(2,1)S(1)}, u32[]{:S(2)}, u32[]{:S(2)}) collective-permute-start(bf16[32,1024]{1,0:T(8,128)(2,1)S(1)} %get-tuple-element.13), channel_id=1, source_target_pairs={{0,256},{32,288},{64,320},{96,352},{128,384},{160,416},{192,448},{... | collective-permute-start | bytes 196616 | tf_op jit(solution)/shard_map/ppermute | solution.py:99
  118.3 17.3 %collective-permute-start.16 = (bf16[32,1024]{1,0:T(8,128)(2,1)S(1)}, bf16[32,1024]{1,0:T(8,128)(2,1)S(1)}, u32[]{:S(2)}, u32[]{:S(2)}) collective-permute-start(bf16[32,1024]{1,0:T(8,128)(2,1)S(1)} %get-tuple-element.11), channel_id=1, source_target_pairs={{0,256},{32,288},{64,320},{96,352},{128,384},{160,416},{192,448},{... | collective-permute-start | bytes 196616 | tf_op jit(solution)/shard_map/ppermute | solution.py:99
  120.2 18.3 %collective-permute-start.8 = (bf16[32,1024]{1,0:T(8,128)(2,1)S(1)}, bf16[32,1024]{1,0:T(8,128)(2,1)S(1)}, u32[]{:S(2)}, u32[]{:S(2)}) collective-permute-start(bf16[32,1024]{1,0:T(8,128)(2,1)S(1)} %get-tuple-element.5), channel_id=1, source_target_pairs={{0,256},{32,288},{64,320},{96,352},{128,384},{160,416},{192,448},{... | collective-permute-start | bytes 196616 | tf_op jit(solution)/shard_map/ppermute | solution.py:99
  127.5 15.1 %collective-permute-start.21 = (bf16[64,1024]{1,0:T(8,128)(2,1)S(1)}, bf16[64,1024]{1,0:T(8,128)(2,1)S(1)}, u32[]{:S(2)}, u32[]{:S(2)}) collective-permute-start(bf16[64,1024]{1,0:T(8,128)(2,1)S(1)} %pad_maximum_fusion.9), channel_id=1, source_target_pairs={{0,128},{32,160},{64,192},{96,224},{128,0},{160,32},{192,64},{224,... | collective-permute-start | bytes 393224 | tf_op jit(solution)/shard_map/ppermute | solution.py:99
  135.6 18.6 %collective-permute-start.17 = (bf16[64,1024]{1,0:T(8,128)(2,1)S(1)}, bf16[64,1024]{1,0:T(8,128)(2,1)S(1)}, u32[]{:S(2)}, u32[]{:S(2)}) collective-permute-start(bf16[64,1024]{1,0:T(8,128)(2,1)S(1)} %pad_maximum_fusion.8), channel_id=1, source_target_pairs={{0,128},{32,160},{64,192},{96,224},{128,0},{160,32},{192,64},{224,... | collective-permute-start | bytes 393224 | tf_op jit(solution)/shard_map/ppermute | solution.py:99
  138.6 18.5 %collective-permute-start.9 = (bf16[64,1024]{1,0:T(8,128)(2,1)S(1)}, bf16[64,1024]{1,0:T(8,128)(2,1)S(1)}, u32[]{:S(2)}, u32[]{:S(2)}) collective-permute-start(bf16[64,1024]{1,0:T(8,128)(2,1)S(1)} %pad_maximum_fusion.7), channel_id=1, source_target_pairs={{0,128},{32,160},{64,192},{96,224},{128,0},{160,32},{192,64},{224,... | collective-permute-start | bytes 393224 | tf_op jit(solution)/shard_map/ppermute | solution.py:99
  142.7 18.7 %collective-permute-start.22 = (bf16[128,1024]{1,0:T(8,128)(2,1)S(1)}, bf16[128,1024]{1,0:T(8,128)(2,1)S(1)}, u32[]{:S(2)}, u32[]{:S(2)}) collective-permute-start(bf16[128,1024]{1,0:T(8,128)(2,1)S(1)} %pad_maximum_fusion.6), channel_id=1, source_target_pairs={{0,64},{32,96},{64,0},{96,32},{128,192},{160,224},{192,128},{224,1... | collective-permute-start | bytes 786440 | tf_op jit(solution)/shard_map/ppermute | solution.py:99
  154.3 20.7 %collective-permute-start.18 = (bf16[128,1024]{1,0:T(8,128)(2,1)S(1)}, bf16[128,1024]{1,0:T(8,128)(2,1)S(1)}, u32[]{:S(2)}, u32[]{:S(2)}) collective-permute-start(bf16[128,1024]{1,0:T(8,128)(2,1)S(1)} %pad_maximum_fusion.5), channel_id=1, source_target_pairs={{0,64},{32,96},{64,0},{96,32},{128,192},{160,224},{192,128},{224,1... | collective-permute-start | bytes 786440 | tf_op jit(solution)/shard_map/ppermute | solution.py:99
  157.1 15.5 %collective-permute-start.10 = (bf16[128,1024]{1,0:T(8,128)(2,1)S(1)}, bf16[128,1024]{1,0:T(8,128)(2,1)S(1)}, u32[]{:S(2)}, u32[]{:S(2)}) collective-permute-start(bf16[128,1024]{1,0:T(8,128)(2,1)S(1)} %pad_maximum_fusion.4), channel_id=1, source_target_pairs={{0,64},{32,96},{64,0},{96,32},{128,192},{160,224},{192,128},{224,1... | collective-permute-start | bytes 786440 | tf_op jit(solution)/shard_map/ppermute | solution.py:99
  161.4 15.7 %collective-permute-start.23 = (bf16[256,1024]{1,0:T(8,128)(2,1)S(1)}, bf16[256,1024]{1,0:T(8,128)(2,1)S(1)}, u32[]{:S(2)}, u32[]{:S(2)}) collective-permute-start(bf16[256,1024]{1,0:T(8,128)(2,1)S(1)} %pad_maximum_fusion.2), channel_id=1, source_target_pairs={{0,32},{32,0},{64,96},{96,64},{128,160},{160,128},{192,224},{224,1... | collective-permute-start | bytes 1572872 | tf_op jit(solution)/shard_map/ppermute | solution.py:99
  172.6 4.5 %collective-permute-start.11 = (bf16[256,1024]{1,0:T(8,128)(2,1)S(1)}, bf16[256,1024]{1,0:T(8,128)(2,1)S(1)}, u32[]{:S(2)}, u32[]{:S(2)}) collective-permute-start(bf16[256,1024]{1,0:T(8,128)(2,1)S(1)} %pad_maximum_fusion), channel_id=1, source_target_pairs={{0,32},{32,0},{64,96},{96,64},{128,160},{160,128},{192,224},{224,1... | collective-permute-start | bytes 1572872 | tf_op jit(solution)/shard_map/ppermute | solution.py:99
  175.1 3.8 %collective-permute-start.19 = (bf16[256,1024]{1,0:T(8,128)(2,1)S(1)}, bf16[256,1024]{1,0:T(8,128)(2,1)S(1)}, u32[]{:S(2)}, u32[]{:S(2)}) collective-permute-start(bf16[256,1024]{1,0:T(8,128)(2,1)S(1)} %pad_maximum_fusion.1), channel_id=1, source_target_pairs={{0,32},{32,0},{64,96},{96,64},{128,160},{160,128},{192,224},{224,1... | collective-permute-start | bytes 1572872 | tf_op jit(solution)/shard_map/ppermute | solution.py:99
  177.2 1.0 copy-start.4
  179.0 1.0 copy-start.2
  181.0 5.6 %copy-start.6 = (f32[128,2]{0,1:T(2,128)S(1)}, f32[128,2]{0,1:T(2,128)}, u32[]{:S(2)}) copy-start(f32[128,2]{0,1:T(2,128)} %param.8) | copy-start | bytes 3076
  182.0 41.0 %all-to-all-start.1 = ((bf16[32,16,512]{2,1,0:T(8,128)(2,1)}), bf16[32,16,512]{2,1,0:T(8,128)(2,1)}, u32[]{:S(2)}, u32[]{:S(2)}) async-start(bf16[32,16,512]{2,1,0:T(8,128)(2,1)} %bitcast.16), calls=%async_computation.1 | async-start | bytes 1048576 | tf_op jit(solution)/shard_map/all_to_all | solution.py:120
  186.6 1.3 copy-start.3
  186.6 1.7 copy-start.5
